TPU v7x, 128 devices: a whole 4x4x4 slice. The times are simulated.
128 devices in a mesh: tm: 2 (over y_hi), tile: 64 (over z, y_lo, x, core).
Axes of the slice: x: 4, y: 4 (y_hi: 2, y_lo: 2; y = y_hi * 2 + y_lo), z: 4, core: 2. Of those that a mesh axis runs over, the one named last changes fastest.
Arguments:
- latent: bfloat16 [2, 192, 512, 256], P('tm', None, 'tile'), may hold values from -200 to 200, as said below
- coarse_cache: bfloat16 [2, 192, 512, 256], P('tm', None, 'tile'), may hold values from -6 to 6
- fine_cache: bfloat16 [2, 96, 1024, 512], P('tm', None, 'tile'), may hold values from -6 to 6
- gain_coarse: float32 [192], replicated, may hold values from 0.1 to 1.9
- shift_coarse: float32 [192], replicated, may hold values from -3 to 3
- weight_coarse: bfloat16 [3, 3, 3, 192, 192], replicated, may hold values from -0.078125 to 0.078125
- weight_up: bfloat16 [3, 3, 96, 192], replicated, may hold values from -0.15625 to 0.15625
- gain_fine: float32 [96], replicated, may hold values from 0.1 to 1.9
- shift_fine: float32 [96], replicated, may hold values from -3 to 3
- weight_fine: bfloat16 [3, 3, 3, 96, 96], replicated, may hold values from -0.125 to 0.125
- bias_fine: float32 [96], replicated, may hold values from -3 to 3
Outputs:
- decoded: bfloat16 [2, 96, 1024, 512], P('tm', None, 'tile')
Inputs may be any that keep to these rules, and one draw needn't show every extreme that they name: `latent`: the coarse block's input before its norm.
All inputs are finite; a program needn't handle non-finite values.
Results may differ from a plain program's by a relative error of at most 0.0046.
Values may be sent and summed in bfloat16 or wider, within the bound.
No kernel may reach another device: no remote copies, remote signals or barrier semaphores. Data moves between devices by JAX's collectives and lax.ppermute only.
A program may use at most 256 MiB of HBM per device.

v0:
```python
import jax
import jax.numpy as jnp
from jax import lax
from jax.sharding import PartitionSpec as P

GROUPS = 32


EPS = 1e-05


def partner(block, axis, stride):
    count = lax.axis_size(axis)
    route = []
    for low in range(count):
        high = low | 1 << stride
        if high != low and high < count:
            route += [(low, high), (high, low)]
    return lax.ppermute(block, axis, route)


def extended(shard, sides, width):
    for axis, dim in sides:
        devices, length = (lax.axis_size(axis), shard.shape[dim])
        up = [(i, (i + 1) % devices) for i in range(devices - 1)]
        down = [(j, i) for i, j in up]
        last = lax.slice_in_dim(shard, length - width, length, axis=dim)
        first = lax.slice_in_dim(shard, 0, width, axis=dim)
        before = lax.ppermute(last, axis, up)
        after = lax.ppermute(first, axis, down)
        shard = jnp.concatenate([before, shard, after], axis=dim)
    return shard


def statistics(stacked):
    frames = stacked.shape[0]
    grouped = stacked.astype(jnp.float32).reshape(frames, GROUPS, -1)
    entries = grouped.shape[2] * lax.axis_size("tile")
    totals = lax.psum(jnp.sum(grouped, axis=2), "tile")
    centre = totals / entries
    centred = grouped - centre[:, :, None]
    variance = lax.psum(jnp.sum(centred * centred, axis=2), "tile") / entries
    return (centre, lax.rsqrt(variance + EPS))


def activate(frame_data, centre, spread, gain, shift):
    channels = frame_data.shape[0]
    centre_full = jnp.repeat(centre, channels // GROUPS)[:, None, None]
    spread_full = jnp.repeat(spread, channels // GROUPS)[:, None, None]
    value = (frame_data.astype(jnp.float32) - centre_full) * spread_full * gain[
        :, None, None
    ] + shift[:, None, None]
    return jax.nn.silu(value).astype(jnp.bfloat16)


def conv_frames(padded, weight, out_rows, out_cols):
    summed = jnp.zeros((weight.shape[3], out_rows, out_cols), jnp.float32)
    for time_tap in range(3):
        for row_tap in range(3):
            for col_tap in range(3):
                window = padded[
                    time_tap, :, row_tap : row_tap + out_rows, col_tap : col_tap + out_cols
                ]
                summed = summed + jnp.einsum(
                    "oc,crw->orw",
                    weight[time_tap, row_tap, col_tap],
                    window,
                    preferred_element_type=jnp.float32,
                )
    return summed


def upsample_conv(coarse_ext, weight, row_count, col_count):
    upsampled = jnp.repeat(jnp.repeat(coarse_ext, 2, axis=1), 2, axis=2)
    upsampled = upsampled[:, 1 : 2 * row_count + 3, :]
    upsampled = jnp.pad(upsampled, ((0, 0), (0, 0), (1, 1)))
    summed = jnp.zeros((weight.shape[2], 2 * row_count, 2 * col_count), jnp.float32)
    for row_tap in range(3):
        for col_tap in range(3):
            window = upsampled[
                :, row_tap : row_tap + 2 * row_count, col_tap : col_tap + 2 * col_count
            ]
            summed = summed + jnp.einsum(
                "oc,crw->orw", weight[row_tap, col_tap], window, preferred_element_type=jnp.float32
            )
    return summed.astype(jnp.bfloat16)


def per_device(
    latent,
    coarse_cache,
    fine_cache,
    gain_coarse,
    shift_coarse,
    weight_coarse,
    weight_up,
    gain_fine,
    shift_fine,
    weight_fine,
    bias_fine,
):
    frame_index = lax.axis_index("tm")
    row_count = latent.shape[2]
    col_count = latent.shape[3]
    centre, spread = statistics(latent)
    active = activate(latent[0], centre[0], spread[0], gain_coarse, shift_coarse)
    outgoing = jnp.where(frame_index == 0, active, coarse_cache[0])
    received = partner(outgoing, "tm", 0)
    stacked = jnp.stack([coarse_cache[0], received, active])
    rim_width = 1
    framed = extended(stacked, (("tile", 2),), rim_width)
    framed = jnp.pad(framed, ((0, 0), (0, 0), (0, 0), (1, 1)))
    coarse_out = conv_frames(framed, weight_coarse, row_count, col_count).astype(jnp.bfloat16)
    coarse_ext = extended(coarse_out, (("tile", 1),), 1)
    raised = upsample_conv(coarse_ext, weight_up, row_count, col_count)
    centre, spread = statistics(raised[None])
    fine_active = activate(raised, centre[0], spread[0], gain_fine, shift_fine)
    outgoing_fine = jnp.where(frame_index == 0, fine_active, fine_cache[0])
    received_fine = partner(outgoing_fine, "tm", 0)
    stacked_fine = jnp.stack([fine_cache[0], received_fine, fine_active])
    framed_fine = extended(stacked_fine, (("tile", 2),), 1)
    framed_fine = jnp.pad(framed_fine, ((0, 0), (0, 0), (0, 0), (1, 1)))
    result = (
        conv_frames(framed_fine, weight_fine, 2 * row_count, 2 * col_count)
        + bias_fine[:, None, None]
    )
    return result.astype(jnp.bfloat16)[None]


def solution(mesh):
    in_specs = (
        P("tm", None, "tile", None),
        P("tm", None, "tile", None),
        P("tm", None, "tile", None),
        P(),
        P(),
        P(),
        P(),
        P(),
        P(),
        P(),
        P(),
    )
    out_specs = P("tm", None, "tile", None)
    return jax.shard_map(
        per_device, mesh=mesh, in_specs=in_specs, out_specs=out_specs, check_vma=False
    )
```

profile of v0, /device:TPU:16, one launch (start us, length us, event | category | flops | bytes accessed | tf_op | source)
XLA Modules:
  0.0 869.3 jit_solution(14596547999683494573)
XLA Ops:
  1.6 144.8 %psum.28 = f32[1,32]{1,0:T(1,128)S(1)} all-reduce(f32[1,32]{1,0:T(1,128)S(1)} %bitcast.816), channel_id=1, replica_groups=mesh['tm'=2,'tile'=64] {'tile'}, use_global_device_ids=true, to_apply=%region_2.0 | all-reduce | flops 32 | bytes 256 | tf_op jit(solution)/shard_map/psum | solution.py:39
  150.5 138.7 %psum.29 = f32[1,32]{1,0:T(1,128)S(1)} all-reduce(f32[1,32]{1,0:T(1,128)S(1)} %bitcast.817), channel_id=1, replica_groups=mesh['tm'=2,'tile'=64] {'tile'}, use_global_device_ids=true, to_apply=%region_5.6 | all-reduce | flops 32 | bytes 256 | tf_op jit(solution)/shard_map/psum | solution.py:42
  292.7 21.8 %collective-permute-done = bf16[192,8,256]{2,0,1:T(8,128)(2,1)S(1)} collective-permute-done((bf16[192,8,256]{2,0,1:T(8,128)(2,1)S(1)}, bf16[192,8,256]{2,0,1:T(8,128)(2,1)S(1)}, u32[]{:S(2)}, u32[]{:S(2)}) %collective-permute-start) | collective-permute-done | bytes 786464 | tf_op jit(solution)/shard_map/ppermute | solution.py:19
  319.4 4.3 select_maximum_fusion.2
  358.7 13.1 %fusion.115 = bf16[192,8,256]{2,0,1:T(8,128)(2,1)} fusion(f32[8,256,192]{1,2,0:T(8,128)} %fusion.119, f32[8,256,192]{1,2,0:T(8,128)S(1)} %fusion.122, f32[8,256,192]{1,2,0:T(8,128)} %fusion.123, f32[8,256,192]{1,2,0:T(8,128)S(1)} %fusion.171, f32[8,256,192]{1,2,0:T(8,128)} %fusion.124, f32[8,256,192]{1,2,0:T(8,128)} %fusion.125, ...), kind=kOutput, calls=%fused_computation.187 | convolution fusion | flops 161611776 | bytes 42565632 | tf_op jit(solution)/shard_map/oc,crw->orw/dot_general | solution.py:64
  372.7 6.1 collective-permute-start.3
  384.1 4.4 broadcast_in_dim.32
  388.5 10.0 %reshape.68 = bf16[192,20,512]{0,2,1:T(8,128)(2,1)} reshape(bf16[192,20,256,2]{0,3,2,1:T(2,128)(2,1)} %broadcast_in_dim.32) | data formatting | bytes 7864320 | tf_op jit(solution)/shard_map/reshape | solution.py:74
  398.5 5.4 fusion.14
  403.9 4.0 fusion.16
  407.9 4.0 fusion.12
  411.8 2.4 slice.576
  414.3 4.6 copy.31
  422.7 3.5 fusion.34
  426.2 3.7 fusion.35
  429.9 3.6 fusion.31
  433.6 6.3 convert_reduce_fusion
  440.1 141.4 %psum.30 = f32[1,32]{1,0:T(1,128)S(1)} all-reduce(f32[1,32]{1,0:T(1,128)S(1)} %bitcast.818), channel_id=1, replica_groups=mesh['tm'=2,'tile'=64] {'tile'}, use_global_device_ids=true, to_apply=%region_8.9 | all-reduce | flops 32 | bytes 256 | tf_op jit(solution)/shard_map/psum | solution.py:39
  583.6 3.5 sub.64
  587.2 3.8 fusion.21
  591.2 138.7 %psum.31 = f32[1,32]{1,0:T(1,128)S(1)} all-reduce(f32[1,32]{1,0:T(1,128)S(1)} %bitcast.815), channel_id=1, replica_groups=mesh['tm'=2,'tile'=64] {'tile'}, use_global_device_ids=true, to_apply=%region_11.12 | all-reduce | flops 32 | bytes 256 | tf_op jit(solution)/shard_map/psum | solution.py:42
  733.6 3.8 fusion.113
  737.4 2.2 fusion.252
  739.6 33.3 %collective-permute-done.5 = bf16[96,16,512]{2,0,1:T(8,128)(2,1)S(1)} collective-permute-done((bf16[96,16,512]{2,0,1:T(8,128)(2,1)S(1)}, bf16[96,16,512]{2,0,1:T(8,128)(2,1)S(1)}, u32[]{:S(2)}, u32[]{:S(2)}) %collective-permute-start.5) | collective-permute-done | bytes 1572896 | tf_op jit(solution)/shard_map/ppermute | solution.py:19
  775.6 2.3 fusion.262
  777.9 6.8 select_maximum_fusion
  784.7 2.6 fusion.64
  787.4 2.3 fusion.65
  789.7 2.3 fusion.66
  791.9 2.3 fusion.67
  794.2 2.3 fusion.72
  796.6 2.3 fusion.73
  801.0 2.4 fusion.82
  805.6 2.3 fusion.84
  807.9 2.2 fusion.92
  810.1 2.3 fusion.93
  812.4 2.2 fusion.101
  814.6 2.4 fusion.102
  817.0 2.2 fusion.103
  819.2 2.3 fusion.104
  821.5 2.4 fusion.112
  826.0 2.3 fusion.74
  828.3 2.3 fusion.61
  830.6 2.2 fusion.105
  832.8 2.2 fusion.85
  835.1 2.3 fusion.69
  837.9 27.8 %fusion.116 = bf16[1,96,16,512]{3,1,2,0:T(8,128)(2,1)} fusion(f32[96]{0:T(128)S(1)} %copy-done.16, bf16[3,96,18,514]{3,1,2,0:T(8,128)(2,1)} %copy-done, f32[16,512,96]{1,2,0:T(8,128)} %fusion.61, f32[16,512,96]{1,2,0:T(8,128)} %fusion.64, f32[16,512,96]{1,2,0:T(8,128)} %fusion.65, f32[16,512,96]{1,2,0:T(8,128)} %fusion.252, f32[16,512,96]{1,2,0:T(8,128)} %fusion.66, ...), kind=kOutput, calls=%fused_computation.210 | convolution fusion | flops 173015040 | bytes 84959616 | tf_op jit(solution)/shard_map/oc,crw->orw/dot_general | solution.py:64
  865.7 3.4 copy.30
  (114 shorter events, 74.7 us)
Async XLA Ops:
  0.0 148.2 %copy-start.8 = (bf16[1,192,8,256]{3,2,1,0:T(8,128)(2,1)S(1)}, bf16[1,192,8,256]{3,2,1,0:T(8,128)(2,1)}, u32[]{:S(2)}) copy-start(bf16[1,192,8,256]{3,2,1,0:T(8,128)(2,1)} %param.11) | copy-start | bytes 2359300
  146.8 142.6 %copy-start.9 = (bf16[1,192,8,256]{3,2,1,0:T(8,128)(2,1)S(1)}, bf16[1,192,8,256]{3,2,1,0:T(8,128)(2,1)}, u32[]{:S(2)}) copy-start(bf16[1,192,8,256]{3,2,1,0:T(8,128)(2,1)} %param.12) | copy-start | bytes 2359300
  146.8 142.6 %copy-start.12 = (f32[192]{0:T(256)S(1)}, f32[192]{0:T(256)}, u32[]{:S(2)}) copy-start(f32[192]{0:T(256)} %param.15) | copy-start | bytes 2308
  146.8 142.6 %copy-start.13 = (f32[192]{0:T(256)S(1)}, f32[192]{0:T(256)}, u32[]{:S(2)}) copy-start(f32[192]{0:T(256)} %param.14) | copy-start | bytes 2308
  289.4 2.9 copy-start.10
  290.5 24.1 %collective-permute-start = (bf16[192,8,256]{2,0,1:T(8,128)(2,1)S(1)}, bf16[192,8,256]{2,0,1:T(8,128)(2,1)S(1)}, u32[]{:S(2)}, u32[]{:S(2)}) collective-permute-start(bf16[192,8,256]{2,0,1:T(8,128)(2,1)S(1)} %fusion.117), channel_id=1, source_target_pairs={{0,64},{64,0},{1,65},{65,1},{2,66},{66,2},{3,67},{67,3},{4,68},{68... | collective-permute-start | bytes 2359304 | tf_op jit(solution)/shard_map/ppermute | solution.py:19
  314.6 3.9 collective-permute-start.1
  315.9 3.5 collective-permute-start.2
  372.7 7.6 collective-permute-start.3
  378.8 3.2 collective-permute-start.4
  398.5 5.4 copy-start.1
  426.2 7.4 copy-start.7
  429.9 3.7 copy-start.5
  429.9 3.7 copy-start.6
  583.6 3.5 copy-start.2
  587.1 143.0 %copy-start.3 = (bf16[1,96,16,512]{3,2,1,0:T(8,128)(2,1)S(1)}, bf16[1,96,16,512]{3,2,1,0:T(8,128)(2,1)}, u32[]{:S(2)}) copy-start(bf16[1,96,16,512]{3,2,1,0:T(8,128)(2,1)} %param.13) | copy-start | bytes 4718596
  587.2 143.0 %copy-start.14 = (f32[96]{0:T(128)S(1)}, f32[96]{0:T(128)}, u32[]{:S(2)}) copy-start(f32[96]{0:T(128)} %param.19) | copy-start | bytes 1156
  587.2 143.0 %copy-start.15 = (f32[96]{0:T(128)S(1)}, f32[96]{0:T(128)}, u32[]{:S(2)}) copy-start(f32[96]{0:T(128)} %param.18) | copy-start | bytes 1156
  732.0 1.6 copy-start.11
  732.0 40.9 %collective-permute-start.5 = (bf16[96,16,512]{2,0,1:T(8,128)(2,1)S(1)}, bf16[96,16,512]{2,0,1:T(8,128)(2,1)S(1)}, u32[]{:S(2)}, u32[]{:S(2)}) collective-permute-start(bf16[96,16,512]{2,0,1:T(8,128)(2,1)S(1)} %get-tuple-element.5), channel_id=1, source_target_pairs={{0,64},{64,0},{1,65},{65,1},{2,66},{66,2},{3,67},{67,3},{4,68},{68... | collective-permute-start | bytes 4718600 | tf_op jit(solution)/shard_map/ppermute | solution.py:19
  773.0 4.9 collective-permute-start.6
  774.3 3.6 collective-permute-start.7
  784.7 36.8 %copy-start = (bf16[3,96,18,514]{3,1,2,0:T(8,128)(2,1)}, bf16[3,96,18,514]{3,1,2,0:T(8,128)(2,1)S(1)}, u32[]{:S(2)}) copy-start(bf16[3,96,18,514]{3,1,2,0:T(8,128)(2,1)S(1)} %select_maximum_fusion) | copy-start | bytes 15987460
  835.1 2.8 copy-start.4
  835.1 2.8 copy-start.16
where the time goes:
time: 879 us; the launch traced here: 869 us
  blocking collectives  564 us (64%)
  matrix products  172 us (20%)
  waiting for transfers between devices  57.8 us (7%)
  local copies, waits for them, and re-layouts  36.5 us (4%)
  other arithmetic  24 us (3%)
  starting transfers between devices  14.7 us (2%)
    psum x2, blocking collectives, statistics(): totals = lax.psum(jnp.sum(grouped, axis=2), 'tile')  286 us
    psum x2, blocking collectives, statistics(): variance = lax.psum(jnp.sum(centred * centred, axis=2), 'tile') / entries  277 us
    dot_general x54, matrix products, conv_frames(): jnp.einsum('oc,crw->orw', weight[time_tap, row_tap, col_tap], window, pre...  138 us
    ppermute x2, waiting for transfers between devices, partner(): return lax.ppermute(block, axis, route)  55.1 us
    dot_general x9, matrix products, upsample_conv(): jnp.einsum('oc,crw->orw', weight[row_tap, col_tap], window, preferred_ele...  34.3 us
  transfers between devices with their start and end apart: 8, of which 4 were waited for; matrix products, arithmetic and copies ran while one was open for 1% of the time, Pallas kernels for 0%

commit v1 on v0

v1 whole, which is shorter than its diff:
```python
import jax
import jax.numpy as jnp
from jax import lax
from jax.experimental import pallas as pl
from jax.experimental.pallas import tpu as pltpu
from jax.sharding import PartitionSpec as P

GROUPS = 32
EPS = 1e-05
f32 = jnp.float32
bf16 = jnp.bfloat16


def call(kernel, name, outs, scratch=()):
    return pl.pallas_call(
        kernel,
        out_shape=[jax.ShapeDtypeStruct(s, d) for s, d in outs],
        scratch_shapes=list(scratch),
        compiler_params=pltpu.CompilerParams(vmem_limit_bytes=56 * 2**20),
        name=name,
    )


def dot(a, b):
    return jnp.dot(a, b, preferred_element_type=f32)


def moments(rows, count):
    total = rows[0].astype(f32)
    for row in rows[1:]:
        total = total + row.astype(f32)
    mean = jnp.sum(total, axis=1, keepdims=True) / count
    squares = None
    for row in rows:
        centred = row.astype(f32) - mean
        squares = centred * centred if squares is None else squares + centred * centred
    return mean, jnp.sum(squares, axis=1, keepdims=True)


def payload(ref, mean, squares):
    channels = mean.shape[0]
    lane = lax.broadcasted_iota(jnp.int32, (channels, 128), 1)
    turned = jnp.transpose(jnp.where(lane == 0, mean, squares))
    half = ref.shape[1] // 2
    ref[...] = jnp.zeros(ref.shape, f32)
    ref[:, :channels] = jnp.broadcast_to(turned[0:1], (ref.shape[0], channels))
    ref[:, half : half + channels] = jnp.broadcast_to(turned[1:2], (ref.shape[0], channels))


def combine(stats, channels, per_device):
    devices, width = stats.shape
    half = width // 2
    turned = jnp.transpose(stats)
    mean = turned[:channels]
    squares = turned[half : half + channels]
    size = channels // GROUPS
    row = lax.broadcasted_iota(jnp.int32, (channels, channels), 0) // size
    col = lax.broadcasted_iota(jnp.int32, (channels, channels), 1) // size
    same = (row == col).astype(f32)

    def group_sum(column):
        wide = jnp.broadcast_to(column, (channels, 128))
        return jnp.dot(
            same, wide, preferred_element_type=f32, precision=lax.Precision.HIGHEST
        )[:, :1]

    centre = group_sum(jnp.sum(mean, axis=1, keepdims=True)) / (devices * size)
    away = mean - centre
    total = jnp.sum(squares + per_device * (away * away), axis=1, keepdims=True)
    variance = group_sum(total) / (devices * size * per_device)
    return centre, lax.rsqrt(variance + EPS)


def silu_norm(x, centre, scale, shift):
    half = 0.5 * ((x.astype(f32) - centre) * scale + shift)
    return half + half * jnp.tanh(half)


def put(ref, slot, row, x):
    channels, width = x.shape
    lane = lax.broadcasted_iota(jnp.int32, (channels, width), 1)
    wide = x.astype(f32)
    left = jnp.where(lane == 0, 0.0, pltpu.roll(wide, 1, 1))
    right = jnp.where(lane == width - 1, 0.0, pltpu.roll(wide, width - 1, 1))
    base = row * 3 * channels
    ref[slot, base : base + channels] = left.astype(bf16)
    ref[slot, base + channels : base + 2 * channels] = x.astype(bf16)
    ref[slot, base + 2 * channels : base + 3 * channels] = right.astype(bf16)


def weights_kernel(coarse, up, fine, out_coarse, out_up, out_fine):
    c1, c2 = coarse.shape[3], fine.shape[3]
    for t in range(3):
        for a in range(3):
            for b in range(3):
                at = (a * 3 + b) * c1
                out_coarse[t, :, at : at + c1] = coarse[t, a, b]
    for b in range(3):
        first, second, third = (up[a, b].astype(f32) for a in range(3))
        at = b * c1
        for rows, a, value in (
            (0, 0, first + second),
            (0, 1, third),
            (1, 0, first),
            (1, 1, second + third),
        ):
            out_up[rows * c2 : (rows + 1) * c2, a * 3 * c1 + at : a * 3 * c1 + at + c1] = (
                value.astype(bf16)
            )
    out_fine[...] = jnp.zeros(out_fine.shape, bf16)
    for t in range(3):
        for a in range(3):
            for b in range(3):
                block = fine[t, a, b]
                for rho in range(2):
                    at = ((a + rho) * 3 + b) * c2
                    out_fine[t, rho * c2 : (rho + 1) * c2, at : at + c2] = block


def first_kernel(latent, cache, fine, lat_t, cache_t, fine_t, send, up, down, pay):
    frame = lax.axis_index("tm")
    rows = latent.shape[1]
    lat = jnp.swapaxes(latent[...], 0, 1)
    lat_t[...] = lat
    cac = jnp.swapaxes(cache[...], 0, 1)
    cache_t[...] = cac
    fin = jnp.swapaxes(fine[...], 0, 1)
    fine_t[...] = fin

    @pl.when(frame == 0)
    def _():
        send[...] = lat_t[...]

    @pl.when(frame != 0)
    def _():
        send[...] = cache_t[...]

    c2, half = fine.shape[0], latent.shape[2]
    for ref, cut, edge in ((up, slice(rows - 2, rows), 2 * rows - 1), (down, slice(0, 2), 0)):
        ref[0:2] = lat_t[cut]
        ref[2:4] = cache_t[cut]
        ref[4, :c2] = fine_t[edge, :, :half]
        ref[4, c2:] = fine_t[edge, :, half:]
    payload(pay, *moments([lat_t[r] for r in range(rows)], rows * latent.shape[2]))


def conv_coarse_a(lat_t, cache_t, above, below, stats, gain, weights, acc, stack):
    tile = lax.axis_index("tile")
    last = lax.axis_size("tile") - 1
    rows, channels, width = lat_t.shape
    centre, spread = combine(stats[...], channels, rows * width)
    scale, shift = spread * gain[:, 0:1], gain[:, 1:2]
    top = jnp.where(tile == 0, 0.0, 1.0)
    bottom = jnp.where(tile == last, 0.0, 1.0)
    for r in range(2):
        put(stack, 0, r, above[2 + r])
        put(stack, 0, rows + 2 + r, below[2 + r])
        put(stack, 1, r, silu_norm(above[r], centre, scale, shift) * top)
        put(stack, 1, rows + 2 + r, silu_norm(below[r], centre, scale, shift) * bottom)
    for r in range(rows):
        put(stack, 0, 2 + r, cache_t[r])
        put(stack, 1, 2 + r, silu_norm(lat_t[r], centre, scale, shift))
    step = 3 * channels
    for r in range(rows + 2):
        acc[r] = dot(weights[0], stack[0, r * step : (r + 3) * step]) + dot(
            weights[2], stack[1, r * step : (r + 3) * step]
        )


def conv_coarse_b(other, above, below, stats, gain, weights, acc, out, stack):
    frame = lax.axis_index("tm")
    tile = lax.axis_index("tile")
    last = lax.axis_size("tile") - 1
    rows, channels, width = other.shape

    @pl.when(frame == 0)
    def _():
        for r in range(2):
            put(stack, 0, r, above[r])
            put(stack, 0, rows + 2 + r, below[r])
        for r in range(rows):
            put(stack, 0, 2 + r, other[r])

    @pl.when(frame != 0)
    def _():
        centre, spread = combine(stats[...], channels, rows * width)
        scale, shift = spread * gain[:, 0:1], gain[:, 1:2]
        top = jnp.where(tile == 0, 0.0, 1.0)
        bottom = jnp.where(tile == last, 0.0, 1.0)
        for r in range(2):
            put(stack, 0, r, silu_norm(above[r], centre, scale, shift) * top)
            put(stack, 0, rows + 2 + r, silu_norm(below[r], centre, scale, shift) * bottom)
        for r in range(rows):
            put(stack, 0, 2 + r, silu_norm(other[r], centre, scale, shift))

    step = 3 * channels
    for r in range(rows + 2):
        value = acc[r] + dot(weights[1], stack[0, r * step : (r + 3) * step])
        if r == 0:
            value = value * jnp.where(tile == 0, 0.0, 1.0)
        if r == rows + 1:
            value = value * jnp.where(tile == last, 0.0, 1.0)
        out[r] = value.astype(bf16)


def raise_rows(coarse, weights, raised, stack):
    rows, channels, width = coarse.shape
    row = lax.broadcasted_iota(jnp.int32, (width, 2 * width), 0)
    col = lax.broadcasted_iota(jnp.int32, (width, 2 * width), 1) // 2
    spread_out = (row == col).astype(f32).astype(bf16)
    for r in range(rows):
        put(stack, 0, r, dot(coarse[r], spread_out))
    step = 3 * channels
    c2 = weights.shape[0] // 2
    for m in range(rows - 1):
        both = dot(weights[...], stack[0, m * step : (m + 2) * step]).astype(bf16)
        raised[2 * m] = both[:c2]
        raised[2 * m + 1] = both[c2:]


def up_kernel(coarse, weights, raised, pay, stack):
    raise_rows(coarse, weights, raised, stack)
    count = raised.shape[0] - 2
    payload(pay, *moments([raised[r + 1] for r in range(count)], count * raised.shape[2]))


def put_active(stack, slot, raised, stats, gain):
    tile = lax.axis_index("tile")
    last = lax.axis_size("tile") - 1
    rows, channels, width = raised.shape
    centre, spread = combine(stats[...], channels, (rows - 2) * width)
    scale, shift = spread * gain[:, 0:1], gain[:, 1:2]
    for r in range(rows):
        value = silu_norm(raised[r], centre, scale, shift)
        if r == 0:
            value = value * jnp.where(tile == 0, 0.0, 1.0)
        if r == rows - 1:
            value = value * jnp.where(tile == last, 0.0, 1.0)
        put(stack, slot, r, value)


def put_cache(stack, slot, fine_t, above, below):
    rows, channels, width = fine_t.shape
    for r, ref in ((0, above), (rows + 1, below)):
        put(stack, slot, r, jnp.concatenate([ref[:channels], ref[channels:]], axis=1))
    for r in range(rows):
        put(stack, slot, r + 1, fine_t[r])


def conv_fine_a(raised, fine_t, above, below, stats, gain, weights, acc, stack):
    put_cache(stack, 0, fine_t, above[4], below[4])
    put_active(stack, 1, raised, stats, gain)
    step = 3 * fine_t.shape[1]
    for m in range(acc.shape[0]):
        window = slice(2 * m * step, (2 * m + 4) * step)
        acc[m] = dot(weights[0], stack[0, window]) + dot(weights[2], stack[1, window])


def conv_fine_b(
    fine_r, edges, coarse_r, stats, gain, weights_up, weights, acc, out, raised, stack_up, stack, rows_out
):
    frame = lax.axis_index("tm")

    @pl.when(frame == 0)
    def _():
        put_cache(stack, 0, fine_r, edges[0], edges[1])

    @pl.when(frame != 0)
    def _():
        raise_rows(coarse_r, weights_up, raised, stack_up)
        put_active(stack, 0, raised, stats, gain)

    c2 = fine_r.shape[1]
    step = 3 * c2
    bias = gain[:, 2:3]
    for m in range(acc.shape[0]):
        window = slice(2 * m * step, (2 * m + 4) * step)
        both = acc[m] + dot(weights[1], stack[0, window])
        rows_out[2 * m] = (both[:c2] + bias).astype(bf16)
        rows_out[2 * m + 1] = (both[c2:] + bias).astype(bf16)
    out[...] = jnp.swapaxes(rows_out[...], 0, 1)


def per_device(
    latent,
    coarse_cache,
    fine_cache,
    gain_coarse,
    shift_coarse,
    weight_coarse,
    weight_up,
    gain_fine,
    shift_fine,
    weight_fine,
    bias_fine,
):
    _, c1, rows, cols = latent.shape
    c2 = fine_cache.shape[1]
    tiles = lax.axis_size("tile")
    fine_rows, fine_cols = 2 * rows, 2 * cols
    forward = [(i, i + 1) for i in range(tiles - 1)]
    backward = [(i + 1, i) for i in range(tiles - 1)]
    later, earlier = [(0, 1)], [(1, 0)]

    def shared(stats):
        return lax.all_to_all(stats, "tile", 0, 0)

    lat_t, cache_t, fine_t, send, pack_up, pack_down, pay = call(
        first_kernel,
        "first",
        [
            ((rows, c1, cols), bf16),
            ((rows, c1, cols), bf16),
            ((fine_rows, c2, fine_cols), bf16),
            ((rows, c1, cols), bf16),
            ((5, c1, cols), bf16),
            ((5, c1, cols), bf16),
            ((tiles, 512), f32),
        ],
    )(latent[0], coarse_cache[0], fine_cache[0])
    above = lax.ppermute(pack_up, "tile", forward)
    below = lax.ppermute(pack_down, "tile", backward)
    other = lax.ppermute(send, "tm", [(0, 1), (1, 0)])
    fine_r = lax.ppermute(fine_t, "tm", earlier)
    w_coarse, w_up, w_fine = call(
        weights_kernel,
        "weights",
        [((3, c1, 9 * c1), bf16), ((2 * c2, 6 * c1), bf16), ((3, 2 * c2, 12 * c2), bf16)],
    )(weight_coarse, weight_up, weight_fine)
    par_coarse = jnp.stack([gain_coarse, shift_coarse], axis=1)
    par_fine = jnp.stack([gain_fine, shift_fine, bias_fine], axis=1)
    edges = lax.ppermute(jnp.stack([above[4], below[4]]), "tm", earlier)

    stats = shared(pay)
    stats_r = lax.ppermute(stats, "tm", later)
    other_above = lax.ppermute(other[rows - 2 :], "tile", forward)
    other_below = lax.ppermute(other[:2], "tile", backward)
    (acc,) = call(
        conv_coarse_a,
        "coarse_a",
        [((rows + 2, c1, cols), f32)],
        [pltpu.VMEM((2, (rows + 4) * 3 * c1, cols), bf16)],
    )(lat_t, cache_t, above, below, stats, par_coarse, w_coarse)
    (coarse,) = call(
        conv_coarse_b,
        "coarse_b",
        [((rows + 2, c1, cols), bf16)],
        [pltpu.VMEM((1, (rows + 4) * 3 * c1, cols), bf16)],
    )(other, other_above, other_below, stats_r, par_coarse, w_coarse, acc)
    coarse_r = lax.ppermute(coarse, "tm", later)
    up_stack = pltpu.VMEM((1, (rows + 2) * 3 * c1, fine_cols), bf16)
    raised, pay = call(
        up_kernel,
        "up",
        [((fine_rows + 2, c2, fine_cols), bf16), ((tiles, 256), f32)],
        [up_stack],
    )(coarse, w_up)
    stats = shared(pay)
    stats_r = lax.ppermute(stats, "tm", later)
    (acc,) = call(
        conv_fine_a,
        "fine_a",
        [((rows, 2 * c2, fine_cols), f32)],
        [pltpu.VMEM((2, (fine_rows + 2) * 3 * c2, fine_cols), bf16)],
    )(raised, fine_t, above, below, stats, par_fine, w_fine)
    (out,) = call(
        conv_fine_b,
        "fine_b",
        [((c2, fine_rows, fine_cols), bf16)],
        [
            pltpu.VMEM((fine_rows + 2, c2, fine_cols), bf16),
            up_stack,
            pltpu.VMEM((1, (fine_rows + 2) * 3 * c2, fine_cols), bf16),
            pltpu.VMEM((fine_rows, c2, fine_cols), bf16),
        ],
    )(fine_r, edges, coarse_r, stats_r, par_fine, w_up, w_fine, acc)
    return out[None]


def solution(mesh):
    split = P("tm", None, "tile", None)
    return jax.shard_map(
        per_device,
        mesh=mesh,
        in_specs=(split,) * 3 + (P(),) * 8,
        out_specs=split,
        check_vma=False,
    )
```

time: 879 us -> 153 us (0.17); the launches traced: 869 us -> 152 us
  blocking collectives: 564 us -> 14.1 us
  matrix products: 172 us -> 0 us
  Pallas kernels: 0 us -> 55.4 us
  local copies, waits for them, and re-layouts: 36.5 us -> 9.18 us
  other arithmetic: 24 us -> 0.04 us
  starting transfers between devices: 14.7 us -> 34.3 us
  waiting for transfers between devices: 57.8 us -> 39.2 us
    psum x4 -> x0, blocking collectives: 564 us -> none  [the longest x2 286 us: statistics(): totals = lax.psum(jnp.sum(grouped, axis=2), 'tile')]
    dot_general x63 -> x0, matrix products: 172 us -> none  [the longest x54 138 us: conv_frames(): jnp.einsum('oc,crw->orw', weight[time_tap, row_tap, col_tap], window, pre...]
    pallas_call x0 -> x7, Pallas kernels: none -> 55.4 us  [the longest x1 12.3 us: per_device(): call(conv_fine_b, 'fine_b', [((c2, fine_rows, fine_cols), bf16)], [pltpu....]
    ppermute x8 -> x10, waiting for transfers between devices: 57.8 us -> 5.06 us  [the longest x1 5.04 us: per_device(): other = lax.ppermute(send, 'tm', [(0, 1), (1, 0)])]
    all_to_all x0 -> x1, waiting for transfers between devices: none -> 34.1 us  [shared(): return lax.all_to_all(stats, 'tile', 0, 0)]
    all_to_all x0 -> x1, blocking collectives: none -> 14.1 us  [shared(): return lax.all_to_all(stats, 'tile', 0, 0)]
    all_to_all x0 -> x1, starting transfers between devices: none -> 12.4 us  [shared(): return lax.all_to_all(stats, 'tile', 0, 0)]
    concatenate x3 -> x0, other arithmetic: 12.3 us -> none  [extended(): shard = jnp.concatenate([before, shard, after], axis=dim)]
  transfers between devices with their start and end apart: 8 -> 11, of which waited for: 4 -> 2; matrix products, arithmetic and copies ran while one was open for 1% -> 4% of each run, Pallas kernels for 0% -> 25%
where the time goes in v1:
time: 153 us; the launch traced here: 152 us
  Pallas kernels  55.4 us (36%)
  waiting for transfers between devices  39.2 us (26%)
  starting transfers between devices  34.3 us (22%)
  blocking collectives  14.1 us (9%)
  local copies, waits for them, and re-layouts  9.18 us (6%)
    all_to_all x1, waiting for transfers between devices, shared(): return lax.all_to_all(stats, 'tile', 0, 0)  34.1 us
    all_to_all x1, blocking collectives, shared(): return lax.all_to_all(stats, 'tile', 0, 0)  14.1 us
    all_to_all x1, starting transfers between devices, shared(): return lax.all_to_all(stats, 'tile', 0, 0)  12.4 us
    pallas_call x1, Pallas kernels, per_device(): call(conv_fine_b, 'fine_b', [((c2, fine_rows, fine_cols), bf16)], [pltpu....  12.3 us
    pallas_call x1, Pallas kernels, per_device(): call(conv_fine_a, 'fine_a', [((rows, 2 * c2, fine_cols), f32)], [pltpu.VM...  10.4 us
    pallas_call x1, Pallas kernels, per_device(): call(conv_coarse_a, 'coarse_a', [((rows + 2, c1, cols), f32)], [pltpu.VME...  9.19 us
    pallas_call x1, Pallas kernels, per_device(): call(conv_coarse_b, 'coarse_b', [((rows + 2, c1, cols), bf16)], [pltpu.VM...  7.88 us
    ppermute x1, starting transfers between devices, per_device(): edges = lax.ppermute(jnp.stack([above[4], below[4]]), 'tm', earlier)  6.12 us
  transfers between devices with their start and end apart: 11, of which 2 were waited for; matrix products, arithmetic and copies ran while one was open for 4% of the time, Pallas kernels for 25%

profile of v1, /device:TPU:16, one launch (start us, length us, event | category | flops | bytes accessed | tf_op | source)
XLA Modules:
  0.0 152.4 jit_solution(7198266776426143881)
XLA Ops:
  0.0 5.1 %first.1 = (bf16[8,192,256]{2,1,0:T(8,128)(2,1)}, bf16[8,192,256]{2,1,0:T(8,128)(2,1)}, bf16[16,96,512]{2,1,0:T(8,128)(2,1)}, bf16[8,192,256]{2,1,0:T(8,128)(2,1...) custom-call(bf16[192,8,256]{2,1,0:T(8,128)(2,1)} %bitcast.18, ...), custom_call_target="tpu_custom_call" | custom-call | tf_op jit(solution)/shard_map/first/pallas_call | solution.py:308
  5.1 0.2 collective-permute-start.4
  5.3 1.5 collective-permute-start.1
  6.8 5.2 %collective-permute-start = (bf16[16,96,512]{2,1,0:T(8,128)(2,1)}, bf16[16,96,512]{2,1,0:T(8,128)(2,1)S(1)}, u32[]{:S(2)}, u32[]{:S(2)}) collective-permute-start(bf16[16,96,512]{2,1,0:T(8,128)(2,1)} %get-tuple-element.17.fine_t), channel_id=1, source_target_pairs={{64,0},{65,1},{66,2},{67,3},{68,4},{69,5},{70,6},{71,7},{72,8},{73... | collective-permute-start | bytes 4718600 | tf_op jit(solution)/shard_map/ppermute | solution.py:324
  12.1 1.3 collective-permute-start.2
  13.4 1.7 %copy.20 = f32[64,1,512]{2,1,0:T(1,128)} copy(f32[64,1,512]{2,0,1:T(8,128)} %bitcast.22) | data formatting | bytes 262144 | tf_op jit(solution)/shard_map/all_to_all | solution.py:306
  15.1 12.4 %all-to-all-start = ((f32[64,1,512]{2,1,0:T(1,128)}), f32[64,1,512]{2,1,0:T(1,128)S(1)}, u32[]{:S(2)}, u32[]{:S(2)}) async-start(f32[64,1,512]{2,1,0:T(1,128)} %copy.20), calls=%async_computation | async-start | bytes 262144 | tf_op jit(solution)/shard_map/all_to_all | solution.py:306
  27.5 5.0 %collective-permute-done.4.other = bf16[8,192,256]{2,1,0:T(8,128)(2,1)S(1)} collective-permute-done((bf16[8,192,256]{2,1,0:T(8,128)(2,1)}, bf16[8,192,256]{2,1,0:T(8,128)(2,1)S(1)}, u32[]{:S(2)}, u32[]{:S(2)}) %collective-permute-start.4) | collective-permute-done | bytes 786464 | tf_op jit(solution)/shard_map/ppermute | solution.py:323
  32.6 0.8 fusion
  33.4 2.0 %collective-permute-start.5 = (bf16[2,192,256]{2,1,0:T(8,128)(2,1)}, bf16[2,192,256]{2,1,0:T(8,128)(2,1)}, u32[]{:S(2)}, u32[]{:S(2)}) collective-permute-start(bf16[2,192,256]{2,1,0:T(8,128)(2,1)} %get-tuple-element.30), channel_id=1, source_target_pairs={{0,1},{1,2},{2,3},{3,4},{4,5},{5,6},{6,7},{7,8},{8,9},{9,10},{10,1... | collective-permute-start | bytes 589832 | tf_op jit(solution)/shard_map/ppermute | solution.py:336
  35.4 1.3 collective-permute-start.6
  36.6 34.1 %all-to-all-done = f32[64,1,512]{2,1,0:T(1,128)S(1)} async-done(((f32[64,1,512]{2,1,0:T(1,128)}), f32[64,1,512]{2,1,0:T(1,128)S(1)}, u32[]{:S(2)}, u32[]{:S(2)}) %all-to-all-start) | async-done | bytes 131104 | tf_op jit(solution)/shard_map/all_to_all | solution.py:306
  70.7 0.7 copy.30
  71.4 0.0 collective-permute-done.1.above
  71.4 1.3 collective-permute-start.7
  72.7 0.0 copy-done.9
  72.7 0.0 copy-done.10
  72.7 0.8 copy.22.gain
  73.5 4.7 %weights.1 = (bf16[3,192,1728]{2,1,0:T(8,128)(2,1)}, bf16[192,1152]{1,0:T(8,128)(2,1)}, bf16[3,192,1152]{2,1,0:T(8,128)(2,1)}) custom-call(bf16[3,3,3,192,192]{4,3,2,1,0:T(8,128)(2,1)} %coarse.1, bf16[3,3,96,192]{3,2,1,0:T(8,128)(2,1)} %up.2, bf16[3,3,3,96,96]{4,3,2,1,0:T(8,128)(2,1)} %fine.1), custom_call_target="tpu_custom_call" | custom-call | tf_op jit(solution)/shard_map/weights/pallas_call | solution.py:325
  78.2 0.0 copy-done.2
  78.2 0.0 copy-done
  78.2 0.0 collective-permute-done.2.below
  78.2 0.8 copy-done.1
  79.1 9.2 %coarse_a.1.acc = f32[10,192,256]{2,1,0:T(8,128)} custom-call(bf16[8,192,256]{2,1,0:T(8,128)(2,1)} %get-tuple-element.23.lat_t, bf16[8,192,256]{2,1,0:T(8,128)(2,1)} %get-tuple-element.24.cache_t, bf16[5,192,256]{2,1,0:T(8,128)(2,1)} %copy-done, bf16[5,192,256]{2,1,0:T(8,128)(2,1)} %copy-done.1, f32[64,512]{1,0:T(8,128)} %bitcast.15.stats, ...), custom_call_target="tpu_custom_call" | custom-call | tf_op jit(solution)/shard_map/coarse_a/pallas_call | solution.py:338
  88.3 0.0 collective-permute-done.7.stats
  88.3 0.0 collective-permute-done.5.above
  88.3 0.0 collective-permute-done.6.below
  88.3 0.6 copy-done.7
  88.9 7.9 %coarse_b.1.coarse = bf16[10,192,256]{2,1,0:T(8,128)(2,1)} custom-call(bf16[8,192,256]{2,1,0:T(8,128)(2,1)} %copy-done.2, bf16[2,192,256]{2,1,0:T(8,128)(2,1)} %collective-permute-done.5.above, bf16[2,192,256]{2,1,0:T(8,128)(2,1)} %collective-permute-done.6.below, f32[64,512]{1,0:T(8,128)} %copy-done.7, f32[192,2]{1,0:T(8,128)} %copy.22.gain, ...), custom_call_target="tpu_custom_call" | custom-call | tf_op jit(solution)/shard_map/coarse_b/pallas_call | solution.py:344
  96.8 1.4 collective-permute-start.8
  98.3 6.1 %collective-permute-start.3 = (bf16[2,192,256]{2,1,0:T(8,128)(2,1)S(1)}, bf16[2,192,256]{2,1,0:T(8,128)(2,1)S(1)}, u32[]{:S(2)}, u32[]{:S(2)}) collective-permute-start(bf16[2,192,256]{2,1,0:T(8,128)(2,1)S(1)} %pad_maximum_fusion), channel_id=1, source_target_pairs={{64,0},{65,1},{66,2},{67,3},{68,4},{69,5},{70,6},{71,7},{72,8},{73... | collective-permute-start | bytes 589832 | tf_op jit(solution)/shard_map/ppermute | solution.py:332
  104.4 5.8 %up.3 = (bf16[18,96,512]{2,1,0:T(8,128)(2,1)}, f32[64,256]{1,0:T(8,128)}) custom-call(bf16[10,192,256]{2,1,0:T(8,128)(2,1)} %coarse_b.1.coarse, bf16[192,1152]{1,0:T(8,128)(2,1)} %get-tuple-element.25.weights.weights_up), custom_call_target="tpu_custom_call" | custom-call | tf_op jit(solution)/shard_map/up/pallas_call | solution.py:352
  110.2 0.9 copy.23
  111.1 14.1 %all_to_all.22 = f32[64,1,256]{2,1,0:T(1,128)S(1)} all-to-all(f32[64,1,256]{2,1,0:T(1,128)S(1)} %copy.23), channel_id=1, replica_groups=mesh['tm'=2,'tile'=64] {'tile'}, dimensions={0} | all-to-all | bytes 131072 | tf_op jit(solution)/shard_map/all_to_all | solution.py:306
  125.2 1.5 collective-permute-start.9
  126.8 0.7 copy.25.gain
  127.5 0.0 copy-done.5
  127.5 10.4 %fine_a.1.acc = f32[8,192,512]{2,1,0:T(8,128)} custom-call(bf16[18,96,512]{2,1,0:T(8,128)(2,1)} %get-tuple-element.28.raised, bf16[16,96,512]{2,1,0:T(8,128)(2,1)} %get-tuple-element.17.fine_t, bf16[5,192,256]{2,1,0:T(8,128)(2,1)} %copy-done, bf16[5,192,256]{2,1,0:T(8,128)(2,1)} %copy-done.1, f32[64,256]{1,0:T(8,128)} %bitcast.21, f32[96,3]{1,0:T(8,128)} %copy.25.gain, ...), custom_call_target="tpu_custom_call" | custom-call | tf_op jit(solution)/shard_map/fine_a/pallas_call | solution.py:360
  137.9 0.0 collective-permute-done.3.edges
  137.9 0.0 collective-permute-done.9.stats
  137.9 0.0 collective-permute-done.fine_r
  137.9 0.0 copy-start.3
  137.9 0.0 collective-permute-done.8.coarse_r
  138.0 0.6 copy-done.6
  138.6 0.0 copy-done.8
  138.6 0.6 copy-done.3
  139.2 0.9 copy-done.4
  140.1 12.3 %fine_b.1 = bf16[96,16,512]{2,1,0:T(8,128)(2,1)} custom-call(bf16[16,96,512]{2,1,0:T(8,128)(2,1)} %copy-done.3, bf16[2,192,256]{2,1,0:T(8,128)(2,1)} %copy-done.6, bf16[10,192,256]{2,1,0:T(8,128)(2,1)} %copy-done.4, f32[64,256]{1,0:T(8,128)} %copy-done.8, f32[96,3]{1,0:T(8,128)} %copy.25.gain, bf16[192,1152]{1,0:T(8,128)(2,1)} %get-tuple-element.25.weights.weights_up, ...), custom_call_target="tpu_custom_call" | custom-call | tf_op jit(solution)/shard_map/fine_b/pallas_call | solution.py:366
  (24 shorter events, 0.1 us)
Async XLA Ops:
  0.0 72.7 %copy-start.9 = (f32[192]{0:T(256)S(1)}, f32[192]{0:T(256)}, u32[]{:S(2)}) copy-start(f32[192]{0:T(256)} %param.15) | copy-start | bytes 2308
  0.0 72.7 %copy-start.10 = (f32[192]{0:T(256)S(1)}, f32[192]{0:T(256)}, u32[]{:S(2)}) copy-start(f32[192]{0:T(256)} %param.14) | copy-start | bytes 2308
  5.1 27.5 %collective-permute-start.4 = (bf16[8,192,256]{2,1,0:T(8,128)(2,1)}, bf16[8,192,256]{2,1,0:T(8,128)(2,1)S(1)}, u32[]{:S(2)}, u32[]{:S(2)}) collective-permute-start(bf16[8,192,256]{2,1,0:T(8,128)(2,1)} %get-tuple-element.20), channel_id=1, source_target_pairs={{0,64},{64,0},{1,65},{65,1},{2,66},{66,2},{3,67},{67,3},{4,68},{68... | collective-permute-start | bytes 2359304 | tf_op jit(solution)/shard_map/ppermute | solution.py:323
  5.3 66.1 %collective-permute-start.1 = (bf16[5,192,256]{2,1,0:T(8,128)(2,1)}, bf16[5,192,256]{2,1,0:T(8,128)(2,1)S(1)}, u32[]{:S(2)}, u32[]{:S(2)}) collective-permute-start(bf16[5,192,256]{2,1,0:T(8,128)(2,1)} %get-tuple-element.18), channel_id=1, source_target_pairs={{0,1},{1,2},{2,3},{3,4},{4,5},{5,6},{6,7},{7,8},{8,9},{9,10},{10,1... | collective-permute-start | bytes 1474568 | tf_op jit(solution)/shard_map/ppermute | solution.py:321
  6.8 131.1 %collective-permute-start = (bf16[16,96,512]{2,1,0:T(8,128)(2,1)}, bf16[16,96,512]{2,1,0:T(8,128)(2,1)S(1)}, u32[]{:S(2)}, u32[]{:S(2)}) collective-permute-start(bf16[16,96,512]{2,1,0:T(8,128)(2,1)} %get-tuple-element.17.fine_t), channel_id=1, source_target_pairs={{64,0},{65,1},{66,2},{67,3},{68,4},{69,5},{70,6},{71,7},{72,8},{73... | collective-permute-start | bytes 4718600 | tf_op jit(solution)/shard_map/ppermute | solution.py:324
  12.1 66.1 %collective-permute-start.2 = (bf16[5,192,256]{2,1,0:T(8,128)(2,1)}, bf16[5,192,256]{2,1,0:T(8,128)(2,1)S(1)}, u32[]{:S(2)}, u32[]{:S(2)}) collective-permute-start(bf16[5,192,256]{2,1,0:T(8,128)(2,1)} %get-tuple-element.19), channel_id=1, source_target_pairs={{1,0},{2,1},{3,2},{4,3},{5,4},{6,5},{7,6},{8,7},{9,8},{10,9},{11,1... | collective-permute-start | bytes 1474568 | tf_op jit(solution)/shard_map/ppermute | solution.py:322
  15.1 55.7 %all-to-all-start = ((f32[64,1,512]{2,1,0:T(1,128)}), f32[64,1,512]{2,1,0:T(1,128)S(1)}, u32[]{:S(2)}, u32[]{:S(2)}) async-start(f32[64,1,512]{2,1,0:T(1,128)} %copy.20), calls=%async_computation | async-start | bytes 262144 | tf_op jit(solution)/shard_map/all_to_all | solution.py:306
  32.6 45.7 %copy-start.2 = (bf16[8,192,256]{2,1,0:T(8,128)(2,1)}, bf16[8,192,256]{2,1,0:T(8,128)(2,1)S(1)}, u32[]{:S(2)}) copy-start(bf16[8,192,256]{2,1,0:T(8,128)(2,1)S(1)} %collective-permute-done.4.other) | copy-start | bytes 2359300
  33.4 54.9 %collective-permute-start.5 = (bf16[2,192,256]{2,1,0:T(8,128)(2,1)}, bf16[2,192,256]{2,1,0:T(8,128)(2,1)}, u32[]{:S(2)}, u32[]{:S(2)}) collective-permute-start(bf16[2,192,256]{2,1,0:T(8,128)(2,1)} %get-tuple-element.30), channel_id=1, source_target_pairs={{0,1},{1,2},{2,3},{3,4},{4,5},{5,6},{6,7},{7,8},{8,9},{9,10},{10,1... | collective-permute-start | bytes 589832 | tf_op jit(solution)/shard_map/ppermute | solution.py:336
  35.4 52.9 %collective-permute-start.6 = (bf16[2,192,256]{2,1,0:T(8,128)(2,1)}, bf16[2,192,256]{2,1,0:T(8,128)(2,1)}, u32[]{:S(2)}, u32[]{:S(2)}) collective-permute-start(bf16[2,192,256]{2,1,0:T(8,128)(2,1)} %get-tuple-element.29), channel_id=1, source_target_pairs={{1,0},{2,1},{3,2},{4,3},{5,4},{6,5},{7,6},{8,7},{9,8},{10,9},{11,1... | collective-permute-start | bytes 589832 | tf_op jit(solution)/shard_map/ppermute | solution.py:337
  71.4 6.8 %copy-start = (bf16[5,192,256]{2,1,0:T(8,128)(2,1)}, bf16[5,192,256]{2,1,0:T(8,128)(2,1)S(1)}, u32[]{:S(2)}) copy-start(bf16[5,192,256]{2,1,0:T(8,128)(2,1)S(1)} %collective-permute-done.1.above) | copy-start | bytes 1474564
  71.4 16.9 %collective-permute-start.7 = (f32[64,512]{1,0:T(8,128)}, f32[64,512]{1,0:T(8,128)S(1)}, u32[]{:S(2)}, u32[]{:S(2)}) collective-permute-start(f32[64,512]{1,0:T(8,128)} %bitcast.15.stats), channel_id=1, source_target_pairs={{0,64},{1,65},{2,66},{3,67},{4,68},{5,69},{6,70},{7,71},{8,72},{9,... | collective-permute-start | bytes 393224 | tf_op jit(solution)/shard_map/ppermute | solution.py:335
  78.2 0.8 copy-start.1
  88.3 10.0 %slice-start = ((bf16[5,192,256]{2,1,0:T(8,128)(2,1)}), bf16[1,192,256]{2,1,0:T(8,128)(2,1)S(1)}, s32[]{:S(2)}) async-start(bf16[5,192,256]{2,1,0:T(8,128)(2,1)} %copy-done), calls=%async_computation.2 | async-start | bytes 196608 | tf_op jit(solution)/shard_map/slice | solution.py:332
  88.3 10.0 %slice-start.1 = ((bf16[5,192,256]{2,1,0:T(8,128)(2,1)}), bf16[1,192,256]{2,1,0:T(8,128)(2,1)S(1)}, s32[]{:S(2)}) async-start(bf16[5,192,256]{2,1,0:T(8,128)(2,1)} %copy-done.1), calls=%async_computation.3 | async-start | bytes 196608 | tf_op jit(solution)/shard_map/slice | solution.py:332
  88.3 0.6 copy-start.7
  96.8 29.9 %copy-start.11 = (f32[96]{0:T(128)S(1)}, f32[96]{0:T(128)}, u32[]{:S(2)}) copy-start(f32[96]{0:T(128)} %param.21) | copy-start | bytes 1156
  96.8 29.9 %copy-start.12 = (f32[96]{0:T(128)S(1)}, f32[96]{0:T(128)}, u32[]{:S(2)}) copy-start(f32[96]{0:T(128)} %param.19) | copy-start | bytes 1156
  96.8 30.0 %copy-start.13 = (f32[96]{0:T(128)S(1)}, f32[96]{0:T(128)}, u32[]{:S(2)}) copy-start(f32[96]{0:T(128)} %param.18) | copy-start | bytes 1156
  96.8 41.1 %collective-permute-start.8 = (bf16[10,192,256]{2,1,0:T(8,128)(2,1)}, bf16[10,192,256]{2,1,0:T(8,128)(2,1)S(1)}, u32[]{:S(2)}, u32[]{:S(2)}) collective-permute-start(bf16[10,192,256]{2,1,0:T(8,128)(2,1)} %coarse_b.1.coarse), channel_id=1, source_target_pairs={{0,64},{1,65},{2,66},{3,67},{4,68},{5,69},{6,70},{7,71},{8,72},{9,... | collective-permute-start | bytes 2949128 | tf_op jit(solution)/shard_map/ppermute | solution.py:350
  98.3 39.6 %collective-permute-start.3 = (bf16[2,192,256]{2,1,0:T(8,128)(2,1)S(1)}, bf16[2,192,256]{2,1,0:T(8,128)(2,1)S(1)}, u32[]{:S(2)}, u32[]{:S(2)}) collective-permute-start(bf16[2,192,256]{2,1,0:T(8,128)(2,1)S(1)} %pad_maximum_fusion), channel_id=1, source_target_pairs={{64,0},{65,1},{66,2},{67,3},{68,4},{69,5},{70,6},{71,7},{72,8},{73... | collective-permute-start | bytes 589832 | tf_op jit(solution)/shard_map/ppermute | solution.py:332
  125.2 2.3 %copy-start.5 = (f32[64,1,256]{2,0,1:T(8,128)}, f32[64,1,256]{2,0,1:T(8,128)S(1)}, u32[]{:S(2)}) copy-start(f32[64,1,256]{2,0,1:T(8,128)S(1)} %copy.31) | copy-start | bytes 196612
  125.2 12.7 %collective-permute-start.9 = (f32[64,256]{1,0:T(8,128)S(1)}, f32[64,256]{1,0:T(8,128)S(1)}, u32[]{:S(2)}, u32[]{:S(2)}) collective-permute-start(f32[64,256]{1,0:T(8,128)S(1)} %bitcast.20), channel_id=1, source_target_pairs={{0,64},{1,65},{2,66},{3,67},{4,68},{5,69},{6,70},{7,71},{8,72},{9,... | collective-permute-start | bytes 196616 | tf_op jit(solution)/shard_map/ppermute | solution.py:359
  137.9 0.7 copy-start.6
  137.9 0.7 copy-start.8
  137.9 1.2 copy-start.3
  139.2 0.9 copy-start.4

commit v2 on v1

v2 whole, which is shorter than its diff:
```python
import jax
import jax.numpy as jnp
from jax import lax
from jax.experimental import pallas as pl
from jax.experimental.pallas import tpu as pltpu
from jax.sharding import PartitionSpec as P

GROUPS = 32
EPS = 1e-05
f32 = jnp.float32
bf16 = jnp.bfloat16


def call(kernel, name, outs, scratch=(), local=True, limit=12):
    run = pl.pallas_call(
        kernel,
        out_shape=[pltpu.VMEM(s, d) if local else jax.ShapeDtypeStruct(s, d) for s, d in outs],
        scratch_shapes=list(scratch),
        compiler_params=pltpu.CompilerParams(vmem_limit_bytes=limit * 2**20),
        name=name,
    )

    def with_arrays(*arrays):
        return run(*[pltpu.with_memory_space_constraint(a, pltpu.VMEM) for a in arrays])

    return with_arrays


def dot(a, b):
    return jnp.dot(a, b, preferred_element_type=f32)


def exact(a, b):
    return jnp.dot(a, b, preferred_element_type=f32, precision=lax.Precision.HIGHEST)


def members(channels, transposed=False):
    shape, dim = ((channels, GROUPS), 1) if transposed else ((GROUPS, channels), 0)
    group = lax.broadcasted_iota(jnp.int32, shape, dim)
    channel = lax.broadcasted_iota(jnp.int32, shape, 1 - dim)
    return (group == channel // (channels // GROUPS)).astype(f32)


def moments(rows, count):
    channels = rows[0].shape[0]
    total = rows[0].astype(f32)
    for row in rows[1:]:
        total = total + row.astype(f32)
    total = jnp.broadcast_to(jnp.sum(total, axis=1, keepdims=True), (channels, 128))
    mean = exact(members(channels), total) / (count * (channels // GROUPS))
    centre = exact(members(channels, True), mean)[:, :1]
    squares = None
    for row in rows:
        centred = row.astype(f32) - centre
        squares = centred * centred if squares is None else squares + centred * centred
    squares = jnp.broadcast_to(jnp.sum(squares, axis=1, keepdims=True), (channels, 128))
    return mean, exact(members(channels), squares)


def payload(ref, mean, squares):
    both = jnp.concatenate([mean, squares, mean, squares], axis=0)
    ref[...] = jnp.broadcast_to(jnp.transpose(both)[0:1][None], ref.shape)


def column(ref):
    return jnp.transpose(jnp.broadcast_to(ref[...], (128, ref.shape[1])))[:, :1]


def combine(stats, frame, channels, per_device):
    devices = lax.axis_size("tile")
    turned = jnp.transpose(stats[pl.ds(frame * devices, devices)].reshape(devices, 4 * GROUPS))
    mean, squares = turned[:GROUPS], turned[GROUPS : 2 * GROUPS]
    size = per_device * (channels // GROUPS)
    centre = jnp.sum(mean, axis=1, keepdims=True) / devices
    away = mean - centre
    total = jnp.sum(squares + size * (away * away), axis=1, keepdims=True)
    spread = lax.rsqrt(total / (devices * size) + EPS)
    lane = lax.broadcasted_iota(jnp.int32, (GROUPS, 128), 1)
    wide = exact(members(channels, True), jnp.where(lane == 0, centre, spread))
    return wide[:, 0:1], wide[:, 1:2]


def silu_norm(x, centre, scale, shift):
    half = 0.5 * ((x[...].astype(f32) - centre) * scale + shift)
    return half + half * jnp.tanh(half)


def put(ref, slot, row, x):
    channels, width = x.shape
    lane = lax.broadcasted_iota(jnp.int32, (channels, width), 1)
    wide = x.astype(f32)
    left = jnp.where(lane == 0, 0.0, pltpu.roll(wide, 1, 1))
    right = jnp.where(lane == width - 1, 0.0, pltpu.roll(wide, width - 1, 1))
    base = row * 3 * channels
    ref[slot, base : base + channels] = left.astype(bf16)
    ref[slot, base + channels : base + 2 * channels] = x.astype(bf16)
    ref[slot, base + 2 * channels : base + 3 * channels] = right.astype(bf16)


def weights_kernel(coarse, up, fine, out_coarse, out_up, out_fine):
    c1, c2 = coarse.shape[3], fine.shape[3]
    for t in range(3):
        for a in range(3):
            for b in range(3):
                at = (a * 3 + b) * c1
                out_coarse[t, :, at : at + c1] = coarse[t, a, b]
    for b in range(3):
        first, second, third = (up[a, b].astype(f32) for a in range(3))
        at = b * c1
        for rows, a, value in (
            (0, 0, first + second),
            (0, 1, third),
            (1, 0, first),
            (1, 1, second + third),
        ):
            out_up[rows * c2 : (rows + 1) * c2, a * 3 * c1 + at : a * 3 * c1 + at + c1] = (
                value.astype(bf16)
            )
    out_fine[...] = jnp.zeros(out_fine.shape, bf16)
    for t in range(3):
        for a in range(3):
            for b in range(3):
                block = fine[t, a, b]
                for rho in range(2):
                    at = ((a + rho) * 3 + b) * c2
                    out_fine[t, rho * c2 : (rho + 1) * c2, at : at + c2] = block


def turn_kernel(latent, cache, fine, lat_t, cache_t, send, up, down):
    rows, width = latent.shape[1:]
    c2 = fine.shape[0]
    lat_t[...] = jnp.swapaxes(latent[...], 0, 1)
    cache_t[...] = jnp.swapaxes(cache[...], 0, 1)
    for ref, cut, line in (
        (up, slice(rows - 2, rows), fine[:, 2 * rows - 1, :]),
        (down, slice(0, 2), fine[:, 0, :]),
    ):
        ref[0:2] = lat_t[cut]
        ref[2:4] = cache_t[cut]
        ref[4, :c2] = line[:, :width]
        ref[4, c2:] = line[:, width:]

    @pl.when(lax.axis_index("tm") == 0)
    def _():
        send[...] = lat_t[...]

    @pl.when(lax.axis_index("tm") != 0)
    def _():
        send[...] = cache_t[...]


def moments_kernel(lat_t, fine, pay, fine_t):
    rows, _, width = lat_t.shape
    fine_t[...] = jnp.swapaxes(fine[...], 0, 1)
    payload(pay, *moments([lat_t[r] for r in range(rows)], rows * width))


def coarse_first(cache_t, above, below, fine_t, weights, acc, fine_pad, stack):
    rows, channels, width = cache_t.shape
    fine_rows, c2, _ = fine_t.shape
    fine_pad[1 : fine_rows + 1] = fine_t[...]
    for r, ref in ((0, above), (fine_rows + 1, below)):
        fine_pad[r, :, :width] = ref[4, :c2]
        fine_pad[r, :, width:] = ref[4, c2:]
    for r in range(2):
        put(stack, 0, r, above[2 + r])
        put(stack, 0, rows + 2 + r, below[2 + r])
    for r in range(rows):
        put(stack, 0, 2 + r, cache_t[r])
    step = 3 * channels
    for r in range(rows + 2):
        acc[r] = dot(weights[0], stack[0, r * step : (r + 3) * step])


def put_normed(stack, middle, above, below, stats, frame, gain, shift):
    tile = lax.axis_index("tile")
    last = lax.axis_size("tile") - 1
    rows, (channels, width) = len(middle), middle[0].shape
    centre, spread = combine(stats, frame, channels, rows * width)
    scale, offset = spread * column(gain), column(shift)
    top = jnp.where(tile == 0, 0.0, 1.0)
    bottom = jnp.where(tile == last, 0.0, 1.0)
    for r in range(2):
        put(stack, 0, r, silu_norm(above[r], centre, scale, offset) * top)
        put(stack, 0, rows + 2 + r, silu_norm(below[r], centre, scale, offset) * bottom)
    for r in range(rows):
        put(stack, 0, 2 + r, silu_norm(middle[r], centre, scale, offset))


def rows_of(*refs):
    return [ref.at[r] for ref in refs for r in range(ref.shape[0])]


def coarse_third(lat_t, above, below, stats, gain, shift, weights, acc, out, stack):
    frame = lax.axis_index("tm")
    put_normed(
        stack, rows_of(lat_t), rows_of(above), rows_of(below), stats, frame, gain, shift
    )
    rows, channels, _ = lat_t.shape
    step = 3 * channels
    for r in range(rows + 2):
        out[r] = acc[r] + dot(weights[2], stack[0, r * step : (r + 3) * step])


def coarse_second(
    other, above, below, stats, gain, shift, weights, acc, out, stack
):
    frame = lax.axis_index("tm")
    tile = lax.axis_index("tile")
    last = lax.axis_size("tile") - 1
    rows, channels, _ = other.shape
    other, above, below = rows_of(other), rows_of(above), rows_of(below)

    @pl.when(frame == 0)
    def _():
        for r, ref in enumerate(above + other + below):
            put(stack, 0, r, ref[...])

    @pl.when(frame != 0)
    def _():
        put_normed(stack, other, above, below, stats, 0, gain, shift)

    step = 3 * channels
    for r in range(rows + 2):
        value = acc[r] + dot(weights[1], stack[0, r * step : (r + 3) * step])
        if r == 0:
            value = value * jnp.where(tile == 0, 0.0, 1.0)
        if r == rows + 1:
            value = value * jnp.where(tile == last, 0.0, 1.0)
        out[r] = value.astype(bf16)


def raise_rows(coarse, weights, raised, stack):
    rows, (channels, width) = len(coarse), coarse[0].shape
    row = lax.broadcasted_iota(jnp.int32, (width, 2 * width), 0)
    col = lax.broadcasted_iota(jnp.int32, (width, 2 * width), 1) // 2
    spread_out = (row == col).astype(f32).astype(bf16)
    for r in range(rows):
        put(stack, 0, r, dot(coarse[r][...], spread_out))
    step = 3 * channels
    c2 = weights.shape[0] // 2
    for m in range(rows - 1):
        both = dot(weights[...], stack[0, m * step : (m + 2) * step]).astype(bf16)
        raised[2 * m] = both[:c2]
        raised[2 * m + 1] = both[c2:]


def up_kernel(coarse, weights, raised, pay, stack):
    raise_rows(rows_of(coarse), weights, raised, stack)
    count = raised.shape[0] - 2
    payload(pay, *moments([raised[r + 1] for r in range(count)], count * raised.shape[2]))


def put_active(stack, raised, stats, frame, gain, shift):
    tile = lax.axis_index("tile")
    last = lax.axis_size("tile") - 1
    rows, channels, width = raised.shape
    centre, spread = combine(stats, frame, channels, (rows - 2) * width)
    scale, offset = spread * column(gain), column(shift)
    for r in range(rows):
        value = silu_norm(raised[r], centre, scale, offset)
        if r == 0:
            value = value * jnp.where(tile == 0, 0.0, 1.0)
        if r == rows - 1:
            value = value * jnp.where(tile == last, 0.0, 1.0)
        put(stack, 0, r, value)


def put_cache(stack, fine):
    for r in range(fine.shape[0]):
        put(stack, 0, r, fine[r])


def fine_window(stack, m, step):
    return stack[0, 2 * m * step : (2 * m + 4) * step]


def fine_first(fine, weights, acc, stack):
    put_cache(stack, fine)
    for m in range(acc.shape[0]):
        acc[m] = dot(weights[0], fine_window(stack, m, 3 * fine.shape[1]))


def fine_third(raised, stats, gain, shift, weights, acc, out, stack):
    put_active(stack, raised, stats, lax.axis_index("tm"), gain, shift)
    for m in range(acc.shape[0]):
        out[m] = acc[m] + dot(weights[2], fine_window(stack, m, 3 * raised.shape[1]))


def fine_second(
    fine, coarse, stats, gain, shift, bias, weights_up, weights, acc, out,
    raised, stack_up, stack, turned,
):
    frame = lax.axis_index("tm")

    @pl.when(frame == 0)
    def _():
        put_cache(stack, fine)

    @pl.when(frame != 0)
    def _():
        raise_rows(rows_of(coarse), weights_up, raised, stack_up)
        put_active(stack, raised, stats, 0, gain, shift)

    c2 = fine.shape[1]
    offset = column(bias)
    for m in range(acc.shape[0]):
        both = acc[m] + dot(weights[1], fine_window(stack, m, 3 * c2))
        turned[2 * m] = (both[:c2] + offset).astype(bf16)
        turned[2 * m + 1] = (both[c2:] + offset).astype(bf16)
    out[...] = jnp.swapaxes(turned[...], 0, 1)


def per_device(
    latent,
    coarse_cache,
    fine_cache,
    gain_coarse,
    shift_coarse,
    weight_coarse,
    weight_up,
    gain_fine,
    shift_fine,
    weight_fine,
    bias_fine,
):
    _, c1, rows, cols = latent.shape
    c2 = fine_cache.shape[1]
    tiles = lax.axis_size("tile")
    fine_rows, fine_cols = 2 * rows, 2 * cols
    forward = [(i, i + 1) for i in range(tiles - 1)]
    backward = [(i + 1, i) for i in range(tiles - 1)]
    later, earlier = [(0, 1)], [(1, 0)]
    gain_coarse, shift_coarse = gain_coarse[None], shift_coarse[None]
    gain_fine, shift_fine, bias_fine = gain_fine[None], shift_fine[None], bias_fine[None]

    def shared(stats):
        return lax.all_to_all(stats, ("tm", "tile"), 0, 0)

    def after(value, *others):
        return lax.optimization_barrier((value, *others))[0]

    devices = lax.axis_size("tm") * tiles
    coarse_shape, coarse_acc = (rows, c1, cols), ((rows + 2, c1, cols), f32)
    fine_acc = ((rows, 2 * c2, fine_cols), f32)
    coarse_stack = pltpu.VMEM((1, (rows + 4) * 3 * c1, cols), bf16)
    fine_stack = pltpu.VMEM((1, (fine_rows + 2) * 3 * c2, fine_cols), bf16)
    up_stack = pltpu.VMEM((1, (rows + 2) * 3 * c1, fine_cols), bf16)
    raised_shape = ((fine_rows + 2, c2, fine_cols), bf16)

    rim = ((5, c1, cols), bf16)
    lat_t, cache_t, send, rim_up, rim_down = call(
        turn_kernel, "turn", [(coarse_shape, bf16)] * 3 + [rim] * 2
    )(latent[0], coarse_cache[0], fine_cache[0])
    above = lax.ppermute(rim_up, "tile", forward)
    below = lax.ppermute(rim_down, "tile", backward)
    other = lax.ppermute(send, "tm", [(0, 1), (1, 0)])
    pay, fine_t = call(
        moments_kernel, "moments", [((devices, 1, 4 * GROUPS), f32), ((fine_rows, c2, fine_cols), bf16)]
    )(lat_t, fine_cache[0])
    w_coarse, w_up, w_fine = call(
        weights_kernel,
        "weights",
        [((3, c1, 9 * c1), bf16), ((2 * c2, 6 * c1), bf16), ((3, 2 * c2, 12 * c2), bf16)],
    )(weight_coarse, weight_up, weight_fine)
    stats = shared(after(pay, w_coarse, above, below))
    acc, fine_pad = call(
        coarse_first, "coarse_first", [coarse_acc, raised_shape], [coarse_stack]
    )(after(cache_t, stats), above, below, fine_t, w_coarse)
    other = after(other, stats)
    other_above = lax.ppermute(other[rows - 2 :], "tile", forward)
    other_below = lax.ppermute(other[:2], "tile", backward)
    (acc,) = call(coarse_third, "coarse_third", [coarse_acc], [coarse_stack])(
        lat_t,
        above,
        below,
        stats,
        gain_coarse,
        shift_coarse,
        w_coarse,
        after(acc, other_above, other_below),
    )
    fine_r = lax.ppermute(after(fine_pad, other_above, other_below), "tm", earlier)
    (coarse,) = call(
        coarse_second, "coarse_second", [((rows + 2, c1, cols), bf16)], [coarse_stack]
    )(other, other_above, other_below, stats, gain_coarse, shift_coarse, w_coarse, acc)
    coarse_r = lax.ppermute(coarse, "tm", later)
    raised, pay = call(up_kernel, "up", [raised_shape, ((devices, 1, 4 * GROUPS), f32)], [up_stack])(
        coarse, w_up
    )
    (acc,) = call(fine_first, "fine_first", [fine_acc], [fine_stack])(fine_pad, w_fine)

    stats = shared(after(pay, acc))
    (acc,) = call(fine_third, "fine_third", [fine_acc], [fine_stack])(
        raised, stats, gain_fine, shift_fine, w_fine, acc
    )
    (out,) = call(
        fine_second,
        "fine_second",
        [((c2, fine_rows, fine_cols), bf16)],
        [
            pltpu.VMEM(*raised_shape),
            up_stack,
            fine_stack,
            pltpu.VMEM((fine_rows, c2, fine_cols), bf16),
        ],
        local=False,
        limit=20,
    )(
        fine_r, coarse_r, stats, gain_fine, shift_fine, bias_fine, w_up, w_fine, acc
    )
    return out[None]


def solution(mesh):
    split = P("tm", None, "tile", None)
    return jax.shard_map(
        per_device,
        mesh=mesh,
        in_specs=(split,) * 3 + (P(),) * 8,
        out_specs=split,
        check_vma=False,
    )
```

time: 153 us -> 107 us (0.70)
  blocking collectives: 14.1 us -> 54.7 us
  waiting for transfers between devices: 39.2 us -> 1.26 us
  Pallas kernels: 55.4 us -> 32.8 us
  starting transfers between devices: 34.3 us -> 13.5 us
  local copies, waits for them, and re-layouts: 9.18 us -> 3.75 us
    all_to_all x1 -> x2, blocking collectives: 14.1 us -> 54.7 us  [shared(): return lax.all_to_all(stats, ('tm', 'tile'), 0, 0)]
    all_to_all x1 -> x0, waiting for transfers between devices: 34.1 us -> none  [shared(): return lax.all_to_all(stats, 'tile', 0, 0)]
    pallas_call x7 -> x10, Pallas kernels: 55.4 us -> 32.8 us  [with_arrays(): run(*[pltpu.with_memory_space_constraint(a, pltpu.VMEM) for a in arrays])]
    all_to_all x1 -> x0, starting transfers between devices: 12.4 us -> none  [shared(): return lax.all_to_all(stats, 'tile', 0, 0)]
    ppermute x6 -> x3, starting transfers between devices: 17 us -> 7.57 us  [the longest x1 4.62 us: per_device(): lax.ppermute(after(fine_pad, other_above, other_below), 'tm', earlier)]
    ppermute x1, waiting for transfers between devices: 5.04 us -> 0.01 us  [per_device(): other = lax.ppermute(send, 'tm', [(0, 1), (1, 0)])]
    all_to_all x2 -> x0, local copies, waits for them, and re-layouts: 2.59 us -> none  [shared(): return lax.all_to_all(stats, 'tile', 0, 0)]
    unnamed x30 -> x24, local copies, waits for them, and re-layouts: 4.31 us -> 3.72 us
  transfers between devices with their start and end apart: 11 -> 7, of which waited for: 2 -> 1; matrix products, arithmetic and copies ran while one was open for 4% -> 0% of each run, Pallas kernels for 25% -> 22%
where the time goes in v2:
time: 107 us; the launch traced here: 106 us
  blocking collectives  54.7 us (51%)
  Pallas kernels  32.8 us (31%)
  starting transfers between devices  13.5 us (13%)
  local copies, waits for them, and re-layouts  3.75 us (4%)
  waiting for transfers between devices  1.26 us (1%)
    all_to_all x2, blocking collectives, shared(): return lax.all_to_all(stats, ('tm', 'tile'), 0, 0)  54.7 us
    pallas_call x10, Pallas kernels, with_arrays(): run(*[pltpu.with_memory_space_constraint(a, pltpu.VMEM) for a in arrays])  32.8 us
    ppermute x1, starting transfers between devices, per_device(): lax.ppermute(after(fine_pad, other_above, other_below), 'tm', earlier)  4.62 us
    unnamed x24, local copies, waits for them, and re-layouts  3.72 us
    ppermute x1, starting transfers between devices, per_device(): other_above = lax.ppermute(other[rows - 2:], 'tile', forward)  3.04 us
  transfers between devices with their start and end apart: 7, of which 1 were waited for; matrix products, arithmetic and copies ran while one was open for 0% of the time, Pallas kernels for 22%

profile of v2, /device:TPU:16, one launch (start us, length us, event | category | flops | bytes accessed | tf_op | source)
XLA Modules:
  0.0 106.4 jit_solution(12883945108858881266)
XLA Ops:
  0.0 0.0 copy-start
  0.0 1.4 %copy-done = bf16[1,96,16,512]{3,2,1,0:T(8,128)(2,1)S(1)} copy-done((bf16[1,96,16,512]{3,2,1,0:T(8,128)(2,1)S(1)}, bf16[1,96,16,512]{3,2,1,0:T(8,128)(2,1)}, u32[]{:S(2)}) %copy-start) | copy-done | bytes 1572888
  1.4 0.0 copy-start.3
  1.4 1.1 %copy-done.3 = bf16[1,192,8,256]{3,2,1,0:T(8,128)(2,1)S(1)} copy-done((bf16[1,192,8,256]{3,2,1,0:T(8,128)(2,1)S(1)}, bf16[1,192,8,256]{3,2,1,0:T(8,128)(2,1)}, u32[]{:S(2)}) %copy-start.3) | copy-done | bytes 786456
  2.5 0.0 copy-start.4
  2.5 1.1 %copy-done.4 = bf16[1,192,8,256]{3,2,1,0:T(8,128)(2,1)S(1)} copy-done((bf16[1,192,8,256]{3,2,1,0:T(8,128)(2,1)S(1)}, bf16[1,192,8,256]{3,2,1,0:T(8,128)(2,1)}, u32[]{:S(2)}) %copy-start.4) | copy-done | bytes 786456
  3.7 0.0 copy-start.1
  3.7 0.9 turn.1
  4.6 0.0 copy-start.5
  4.6 0.0 copy-start.6
  4.6 0.3 collective-permute-start.2
  4.9 1.7 %collective-permute-start = (bf16[5,192,256]{2,1,0:T(8,128)(2,1)S(1)}, bf16[5,192,256]{2,1,0:T(8,128)(2,1)S(1)}, u32[]{:S(2)}, u32[]{:S(2)}) collective-permute-start(bf16[5,192,256]{2,1,0:T(8,128)(2,1)S(1)} %get-tuple-element.29), channel_id=1, source_target_pairs={{0,1},{1,2},{2,3},{3,4},{4,5},{5,6},{6,7},{7,8},{8,9},{9,10},{10,1... | collective-permute-start | bytes 1474568 | tf_op jit(solution)/shard_map/ppermute | solution.py:355
  6.6 1.3 %collective-permute-start.1 = (bf16[5,192,256]{2,1,0:T(8,128)(2,1)S(1)}, bf16[5,192,256]{2,1,0:T(8,128)(2,1)S(1)}, u32[]{:S(2)}, u32[]{:S(2)}) collective-permute-start(bf16[5,192,256]{2,1,0:T(8,128)(2,1)S(1)} %get-tuple-element.30), channel_id=1, source_target_pairs={{1,0},{2,1},{3,2},{4,3},{5,4},{6,5},{7,6},{8,7},{9,8},{10,9},{11,1... | collective-permute-start | bytes 1474568 | tf_op jit(solution)/shard_map/ppermute | solution.py:356
  7.9 0.0 copy-done.1
  7.9 1.7 %moments.1 = (f32[128,1,128]{2,1,0:T(1,128)S(1)}, bf16[16,96,512]{2,1,0:T(8,128)(2,1)S(1)}) custom-call(bf16[8,192,256]{2,1,0:T(8,128)(2,1)S(1)} %get-tuple-element.26.lat_t, bf16[96,16,512]{2,1,0:T(8,128)(2,1)S(1)} %bitcast.10), custom_call_target="tpu_custom_call" | custom-call | tf_op jit(solution)/shard_map/moments/pallas_call | solution.py:24
  9.6 0.0 copy-done.2
  9.6 0.0 copy-done.5
  9.6 0.0 copy-done.6
  9.6 1.0 weights.1
  10.7 0.0 collective-permute-done.above
  10.7 1.2 %collective-permute-done.1.below = bf16[5,192,256]{2,1,0:T(8,128)(2,1)S(1)} collective-permute-done((bf16[5,192,256]{2,1,0:T(8,128)(2,1)S(1)}, bf16[5,192,256]{2,1,0:T(8,128)(2,1)S(1)}, u32[]{:S(2)}, u32[]{:S(2)}) %collective-permute-start.1) | collective-permute-done | bytes 491552 | tf_op jit(solution)/shard_map/ppermute | solution.py:356
  11.9 28.2 %all_to_all.10.stats = f32[128,1,128]{2,1,0:T(1,128)S(1)} all-to-all(f32[128,1,128]{2,1,0:T(1,128)S(1)} %get-tuple-element.31), channel_id=1, replica_groups=mesh['tm'=2,'tile'=64] {'tm','tile'}, dimensions={0} | all-to-all | bytes 131072 | tf_op jit(solution)/shard_map/all_to_all | solution.py:338
  40.2 0.0 collective-permute-done.2.other
  40.2 1.3 %collective-permute-start.4 = (bf16[2,192,256]{2,1,0:T(8,128)(2,1)S(1)}, bf16[2,192,256]{2,1,0:T(8,128)(2,1)S(1)}, u32[]{:S(2)}, u32[]{:S(2)}) collective-permute-start(bf16[2,192,256]{2,1,0:T(8,128)(2,1)S(1)} %get-tuple-element.45), channel_id=1, source_target_pairs={{1,0},{2,1},{3,2},{4,3},{5,4},{6,5},{7,6},{8,7},{9,8},{10,9},{11,1... | collective-permute-start | bytes 589832 | tf_op jit(solution)/shard_map/ppermute | solution.py:372
  41.5 3.0 %collective-permute-start.3 = (bf16[2,192,256]{2,1,0:T(8,128)(2,1)S(1)}, bf16[2,192,256]{2,1,0:T(8,128)(2,1)S(1)}, u32[]{:S(2)}, u32[]{:S(2)}) collective-permute-start(bf16[2,192,256]{2,1,0:T(8,128)(2,1)S(1)} %get-tuple-element.46), channel_id=1, source_target_pairs={{0,1},{1,2},{2,3},{3,4},{4,5},{5,6},{6,7},{7,8},{8,9},{9,10},{10,1... | collective-permute-start | bytes 589832 | tf_op jit(solution)/shard_map/ppermute | solution.py:371
  44.6 0.0 copy-start.7
  44.6 0.0 copy-start.8
  44.6 2.1 %coarse_first.1 = (f32[10,192,256]{2,1,0:T(8,128)S(1)}, bf16[18,96,512]{2,1,0:T(8,128)(2,1)S(1)}) custom-call(bf16[8,192,256]{2,1,0:T(8,128)(2,1)S(1)} %get-tuple-element.32.cache_t, bf16[5,192,256]{2,1,0:T(8,128)(2,1)S(1)} %collective-permute-done.above, bf16[5,192,256]{2,1,0:T(8,128)(2,1)S(1)} %collective-permute-done.1.below, ...), custom_call_target="tpu_custom_call" | custom-call | tf_op jit(solution)/shard_map/coarse_first/pallas_call | solution.py:24
  46.7 0.0 collective-permute-done.4.below
  46.7 0.0 collective-permute-done.3.above
  46.7 4.6 %collective-permute-start.5 = (bf16[18,96,512]{2,1,0:T(8,128)(2,1)S(1)}, bf16[18,96,512]{2,1,0:T(8,128)(2,1)S(1)}, u32[]{:S(2)}, u32[]{:S(2)}) collective-permute-start(bf16[18,96,512]{2,1,0:T(8,128)(2,1)S(1)} %get-tuple-element.37.fine), channel_id=1, source_target_pairs={{64,0},{65,1},{66,2},{67,3},{68,4},{69,5},{70,6},{71,7},{72,8},{73... | collective-permute-start | bytes 5308424 | tf_op jit(solution)/shard_map/ppermute | solution.py:383
  51.3 0.0 copy-done.7
  51.3 0.0 copy-done.8
  51.3 3.2 %coarse_third.1.acc = f32[10,192,256]{2,1,0:T(8,128)S(1)} custom-call(bf16[8,192,256]{2,1,0:T(8,128)(2,1)S(1)} %get-tuple-element.26.lat_t, bf16[5,192,256]{2,1,0:T(8,128)(2,1)S(1)} %collective-permute-done.above, bf16[5,192,256]{2,1,0:T(8,128)(2,1)S(1)} %collective-permute-done.1.below, f32[128,1,128]{2,1,0:T(1,128)S(1)} %all_to_all.10.stats, ...), custom_call_target="tpu_custom_call" | custom-call | tf_op jit(solution)/shard_map/coarse_third/pallas_call | solution.py:24
  54.5 4.1 %coarse_second.1.coarse = bf16[10,192,256]{2,1,0:T(8,128)(2,1)S(1)} custom-call(bf16[8,192,256]{2,1,0:T(8,128)(2,1)S(1)} %collective-permute-done.2.other, bf16[2,192,256]{2,1,0:T(8,128)(2,1)S(1)} %collective-permute-done.3.above, bf16[2,192,256]{2,1,0:T(8,128)(2,1)S(1)} %collective-permute-done.4.below, f32[128,1,128]{2,1,0:T(1,128)S(1)} %all_to_all.10.stats, ...), custom_call_target="tpu_custom_call" | custom-call | tf_op jit(solution)/shard_map/coarse_second/pallas_call | solution.py:24
  58.6 1.3 %collective-permute-start.6 = (bf16[10,192,256]{2,1,0:T(8,128)(2,1)S(1)}, bf16[10,192,256]{2,1,0:T(8,128)(2,1)S(1)}, u32[]{:S(2)}, u32[]{:S(2)}) collective-permute-start(bf16[10,192,256]{2,1,0:T(8,128)(2,1)S(1)} %coarse_second.1.coarse), channel_id=1, source_target_pairs={{0,64},{1,65},{2,66},{3,67},{4,68},{5,69},{6,70},{7,71},{8,72},{9,... | collective-permute-start | bytes 2949128 | tf_op jit(solution)/shard_map/ppermute | solution.py:387
  59.9 0.0 copy-start.9
  60.0 0.0 copy-start.10
  60.0 2.3 %fine_first.1.acc = f32[8,192,512]{2,1,0:T(8,128)S(1)} custom-call(bf16[18,96,512]{2,1,0:T(8,128)(2,1)S(1)} %get-tuple-element.37.fine, bf16[3,192,1152]{2,1,0:T(8,128)(2,1)S(1)} %get-tuple-element.42.weights), custom_call_target="tpu_custom_call" | custom-call | tf_op jit(solution)/shard_map/fine_first/pallas_call | solution.py:24
  62.3 4.7 %up.3 = (bf16[18,96,512]{2,1,0:T(8,128)(2,1)S(1)}, f32[128,1,128]{2,1,0:T(1,128)S(1)}) custom-call(bf16[10,192,256]{2,1,0:T(8,128)(2,1)S(1)} %coarse_second.1.coarse, bf16[192,1152]{1,0:T(8,128)(2,1)S(1)} %get-tuple-element.40.weights.weights_up), custom_call_target="tpu_custom_call" | custom-call | tf_op jit(solution)/shard_map/up/pallas_call | solution.py:24
  67.0 26.5 %all_to_all.11.stats = f32[128,1,128]{2,1,0:T(1,128)S(1)} all-to-all(f32[128,1,128]{2,1,0:T(1,128)S(1)} %get-tuple-element.43), channel_id=1, replica_groups=mesh['tm'=2,'tile'=64] {'tm','tile'}, dimensions={0} | all-to-all | bytes 131072 | tf_op jit(solution)/shard_map/all_to_all | solution.py:338
  93.4 0.0 copy-done.9
  93.4 0.0 copy-done.10
  93.5 3.9 %fine_third.1.acc = f32[8,192,512]{2,1,0:T(8,128)S(1)} custom-call(bf16[18,96,512]{2,1,0:T(8,128)(2,1)S(1)} %get-tuple-element.44.raised, f32[128,1,128]{2,1,0:T(1,128)S(1)} %all_to_all.11.stats, f32[1,96]{1,0:T(1,128)S(1)} %bitcast.17, f32[1,96]{1,0:T(1,128)S(1)} %bitcast.19, bf16[3,192,1152]{2,1,0:T(8,128)(2,1)S(1)} %get-tuple-element.42.weights, ...), custom_call_target="tpu_custom_call" | custom-call | tf_op jit(solution)/shard_map/fine_third/pallas_call | solution.py:24
  97.3 0.0 collective-permute-done.6.coarse
  97.3 0.0 collective-permute-done.5.fine
  97.3 0.0 copy-done.11
  97.4 9.0 %fine_second.1 = bf16[96,16,512]{2,1,0:T(8,128)(2,1)} custom-call(bf16[18,96,512]{2,1,0:T(8,128)(2,1)S(1)} %collective-permute-done.5.fine, bf16[10,192,256]{2,1,0:T(8,128)(2,1)S(1)} %collective-permute-done.6.coarse, f32[128,1,128]{2,1,0:T(1,128)S(1)} %all_to_all.11.stats, f32[1,96]{1,0:T(1,128)S(1)} %bitcast.18, f32[1,96]{1,0:T(1,128)S(1)} %bitcast.20, ...), custom_call_target="tpu_custom_call" | custom-call | tf_op jit(solution)/shard_map/fine_second/pallas_call | solution.py:24
  (3 shorter events, 0.0 us)
Async XLA Ops:
  0.0 1.4 %copy-start = (bf16[1,96,16,512]{3,2,1,0:T(8,128)(2,1)S(1)}, bf16[1,96,16,512]{3,2,1,0:T(8,128)(2,1)}, u32[]{:S(2)}) copy-start(bf16[1,96,16,512]{3,2,1,0:T(8,128)(2,1)} %param.13) | copy-start | bytes 4718596
  1.4 1.1 %copy-start.3 = (bf16[1,192,8,256]{3,2,1,0:T(8,128)(2,1)S(1)}, bf16[1,192,8,256]{3,2,1,0:T(8,128)(2,1)}, u32[]{:S(2)}) copy-start(bf16[1,192,8,256]{3,2,1,0:T(8,128)(2,1)} %param.11) | copy-start | bytes 2359300
  2.5 1.1 %copy-start.4 = (bf16[1,192,8,256]{3,2,1,0:T(8,128)(2,1)S(1)}, bf16[1,192,8,256]{3,2,1,0:T(8,128)(2,1)}, u32[]{:S(2)}) copy-start(bf16[1,192,8,256]{3,2,1,0:T(8,128)(2,1)} %param.12) | copy-start | bytes 2359300
  3.7 4.2 %copy-start.1 = (bf16[1,96,16,512]{3,2,1,0:T(8,128)(2,1)S(1)}, bf16[1,96,16,512]{3,2,1,0:T(8,128)(2,1)}, u32[]{:S(2)}) copy-start(bf16[1,96,16,512]{3,2,1,0:T(8,128)(2,1)} %param.13) | copy-start | bytes 4718596
  3.7 5.9 %copy-start.2 = (bf16[3,3,3,192,192]{4,3,2,1,0:T(8,128)(2,1)S(1)}, bf16[3,3,3,192,192]{4,3,2,1,0:T(8,128)(2,1)}, u32[]{:S(2)}) copy-start(bf16[3,3,3,192,192]{4,3,2,1,0:T(8,128)(2,1)} %coarse.1) | copy-start | bytes 5971972
  4.6 5.0 %copy-start.5 = (bf16[3,3,3,96,96]{4,3,2,1,0:T(8,128)(2,1)S(1)}, bf16[3,3,3,96,96]{4,3,2,1,0:T(8,128)(2,1)}, u32[]{:S(2)}) copy-start(bf16[3,3,3,96,96]{4,3,2,1,0:T(8,128)(2,1)} %fine.1) | copy-start | bytes 1492996
  4.6 5.0 %copy-start.6 = (bf16[3,3,96,192]{3,2,1,0:T(8,128)(2,1)S(1)}, bf16[3,3,96,192]{3,2,1,0:T(8,128)(2,1)}, u32[]{:S(2)}) copy-start(bf16[3,3,96,192]{3,2,1,0:T(8,128)(2,1)} %up.2) | copy-start | bytes 995332
  4.6 35.6 %collective-permute-start.2 = (bf16[8,192,256]{2,1,0:T(8,128)(2,1)S(1)}, bf16[8,192,256]{2,1,0:T(8,128)(2,1)S(1)}, u32[]{:S(2)}, u32[]{:S(2)}) collective-permute-start(bf16[8,192,256]{2,1,0:T(8,128)(2,1)S(1)} %get-tuple-element.35), channel_id=1, source_target_pairs={{0,64},{64,0},{1,65},{65,1},{2,66},{66,2},{3,67},{67,3},{4,68},{68... | collective-permute-start | bytes 2359304 | tf_op jit(solution)/shard_map/ppermute | solution.py:357
  4.9 5.7 %collective-permute-start = (bf16[5,192,256]{2,1,0:T(8,128)(2,1)S(1)}, bf16[5,192,256]{2,1,0:T(8,128)(2,1)S(1)}, u32[]{:S(2)}, u32[]{:S(2)}) collective-permute-start(bf16[5,192,256]{2,1,0:T(8,128)(2,1)S(1)} %get-tuple-element.29), channel_id=1, source_target_pairs={{0,1},{1,2},{2,3},{3,4},{4,5},{5,6},{6,7},{7,8},{8,9},{9,10},{10,1... | collective-permute-start | bytes 1474568 | tf_op jit(solution)/shard_map/ppermute | solution.py:355
  6.6 5.3 %collective-permute-start.1 = (bf16[5,192,256]{2,1,0:T(8,128)(2,1)S(1)}, bf16[5,192,256]{2,1,0:T(8,128)(2,1)S(1)}, u32[]{:S(2)}, u32[]{:S(2)}) collective-permute-start(bf16[5,192,256]{2,1,0:T(8,128)(2,1)S(1)} %get-tuple-element.30), channel_id=1, source_target_pairs={{1,0},{2,1},{3,2},{4,3},{5,4},{6,5},{7,6},{8,7},{9,8},{10,9},{11,1... | collective-permute-start | bytes 1474568 | tf_op jit(solution)/shard_map/ppermute | solution.py:356
  40.2 6.5 %collective-permute-start.4 = (bf16[2,192,256]{2,1,0:T(8,128)(2,1)S(1)}, bf16[2,192,256]{2,1,0:T(8,128)(2,1)S(1)}, u32[]{:S(2)}, u32[]{:S(2)}) collective-permute-start(bf16[2,192,256]{2,1,0:T(8,128)(2,1)S(1)} %get-tuple-element.45), channel_id=1, source_target_pairs={{1,0},{2,1},{3,2},{4,3},{5,4},{6,5},{7,6},{8,7},{9,8},{10,9},{11,1... | collective-permute-start | bytes 589832 | tf_op jit(solution)/shard_map/ppermute | solution.py:372
  41.5 5.2 %collective-permute-start.3 = (bf16[2,192,256]{2,1,0:T(8,128)(2,1)S(1)}, bf16[2,192,256]{2,1,0:T(8,128)(2,1)S(1)}, u32[]{:S(2)}, u32[]{:S(2)}) collective-permute-start(bf16[2,192,256]{2,1,0:T(8,128)(2,1)S(1)} %get-tuple-element.46), channel_id=1, source_target_pairs={{0,1},{1,2},{2,3},{3,4},{4,5},{5,6},{6,7},{7,8},{8,9},{9,10},{10,1... | collective-permute-start | bytes 589832 | tf_op jit(solution)/shard_map/ppermute | solution.py:371
  44.6 6.8 %copy-start.7 = (f32[192]{0:T(256)S(1)}, f32[192]{0:T(256)}, u32[]{:S(2)}) copy-start(f32[192]{0:T(256)} %param.14) | copy-start | bytes 2308
  44.6 6.8 %copy-start.8 = (f32[192]{0:T(256)S(1)}, f32[192]{0:T(256)}, u32[]{:S(2)}) copy-start(f32[192]{0:T(256)} %param.15) | copy-start | bytes 2308
  46.7 50.7 %collective-permute-start.5 = (bf16[18,96,512]{2,1,0:T(8,128)(2,1)S(1)}, bf16[18,96,512]{2,1,0:T(8,128)(2,1)S(1)}, u32[]{:S(2)}, u32[]{:S(2)}) collective-permute-start(bf16[18,96,512]{2,1,0:T(8,128)(2,1)S(1)} %get-tuple-element.37.fine), channel_id=1, source_target_pairs={{64,0},{65,1},{66,2},{67,3},{68,4},{69,5},{70,6},{71,7},{72,8},{73... | collective-permute-start | bytes 5308424 | tf_op jit(solution)/shard_map/ppermute | solution.py:383
  58.6 38.7 %collective-permute-start.6 = (bf16[10,192,256]{2,1,0:T(8,128)(2,1)S(1)}, bf16[10,192,256]{2,1,0:T(8,128)(2,1)S(1)}, u32[]{:S(2)}, u32[]{:S(2)}) collective-permute-start(bf16[10,192,256]{2,1,0:T(8,128)(2,1)S(1)} %coarse_second.1.coarse), channel_id=1, source_target_pairs={{0,64},{1,65},{2,66},{3,67},{4,68},{5,69},{6,70},{7,71},{8,72},{9,... | collective-permute-start | bytes 2949128 | tf_op jit(solution)/shard_map/ppermute | solution.py:387
  59.9 33.5 %copy-start.9 = (f32[96]{0:T(128)S(1)}, f32[96]{0:T(128)}, u32[]{:S(2)}) copy-start(f32[96]{0:T(128)} %param.18) | copy-start | bytes 1156
  60.0 33.5 %copy-start.10 = (f32[96]{0:T(128)S(1)}, f32[96]{0:T(128)}, u32[]{:S(2)}) copy-start(f32[96]{0:T(128)} %param.19) | copy-start | bytes 1156
  93.5 3.9 %copy-start.11 = (f32[96]{0:T(128)S(1)}, f32[96]{0:T(128)}, u32[]{:S(2)}) copy-start(f32[96]{0:T(128)} %param.21) | copy-start | bytes 1156

commit v3 on v2

--- a/solution.py
+++ b/solution.py
@@ -11,17 +11,20 @@
 bf16 = jnp.bfloat16
 
 
-def call(kernel, name, outs, scratch=(), local=True, limit=12):
-    run = pl.pallas_call(
-        kernel,
-        out_shape=[pltpu.VMEM(s, d) if local else jax.ShapeDtypeStruct(s, d) for s, d in outs],
-        scratch_shapes=list(scratch),
-        compiler_params=pltpu.CompilerParams(vmem_limit_bytes=limit * 2**20),
-        name=name,
-    )
-
+def call(kernel, name, outs, scratch=(), local=True, limit=12, far=0, aliases=None):
     def with_arrays(*arrays):
-        return run(*[pltpu.with_memory_space_constraint(a, pltpu.VMEM) for a in arrays])
+        near = [pltpu.with_memory_space_constraint(a, pltpu.VMEM) for a in arrays[far:]]
+        away = [pltpu.with_memory_space_constraint(a, pltpu.HBM) for a in arrays[:far]]
+        return pl.pallas_call(
+            kernel,
+            in_specs=[pl.BlockSpec(memory_space=pltpu.HBM)] * far
+            + [pl.BlockSpec(memory_space=pltpu.VMEM)] * len(near),
+            out_shape=[pltpu.VMEM(s, d) if local else jax.ShapeDtypeStruct(s, d) for s, d in outs],
+            scratch_shapes=list(scratch),
+            input_output_aliases=aliases or {},
+            compiler_params=pltpu.CompilerParams(vmem_limit_bytes=limit * 2**20),
+            name=name,
+        )(*away, *near)
 
     return with_arrays
 
@@ -88,13 +91,14 @@
 def put(ref, slot, row, x):
     channels, width = x.shape
     lane = lax.broadcasted_iota(jnp.int32, (channels, width), 1)
-    wide = x.astype(f32)
-    left = jnp.where(lane == 0, 0.0, pltpu.roll(wide, 1, 1))
-    right = jnp.where(lane == width - 1, 0.0, pltpu.roll(wide, width - 1, 1))
+    x = x.astype(bf16)
+    none = jnp.zeros((), bf16)
+    left = jnp.where(lane == 0, none, pltpu.roll(x, 1, 1))
+    right = jnp.where(lane == width - 1, none, pltpu.roll(x, width - 1, 1))
     base = row * 3 * channels
-    ref[slot, base : base + channels] = left.astype(bf16)
-    ref[slot, base + channels : base + 2 * channels] = x.astype(bf16)
-    ref[slot, base + 2 * channels : base + 3 * channels] = right.astype(bf16)
+    ref[slot, base : base + channels] = left
+    ref[slot, base + channels : base + 2 * channels] = x
+    ref[slot, base + 2 * channels : base + 3 * channels] = right
 
 
 def weights_kernel(coarse, up, fine, out_coarse, out_up, out_fine):
@@ -126,42 +130,69 @@
                     out_fine[t, rho * c2 : (rho + 1) * c2, at : at + c2] = block
 
 
-def turn_kernel(latent, cache, fine, lat_t, cache_t, send, up, down):
-    rows, width = latent.shape[1:]
+CHUNKS = 4
+
+
+def fetches(source, target, arrived):
+    part = source.shape[0] // CHUNKS
+    cuts = [pl.ds(k * part, part) for k in range(CHUNKS)]
+    return [
+        pltpu.make_async_copy(source.at[cut], target.at[cut], arrived.at[k])
+        for k, cut in enumerate(cuts)
+    ]
+
+
+def turn_kernel(
+    latent, cache, fine, lat_t, cache_t, send, fine_v, lat_v, cache_v, lat_in, cache_in, fine_in
+):
+    lat_copies = fetches(latent, lat_v, lat_in)
+    cache_copies = fetches(cache, cache_v, cache_in)
+    fine_copies = fetches(fine, fine_v, fine_in)
+    for copy in lat_copies + cache_copies + fine_copies:
+        copy.start()
+    for copy in lat_copies:
+        copy.wait()
+    lat_t[...] = jnp.swapaxes(lat_v[...], 0, 1)
+    for copy in cache_copies:
+        copy.wait()
+    cache_t[...] = jnp.swapaxes(cache_v[...], 0, 1)
+
+    @pl.when(lax.axis_index("tm") == 0)
+    def _():
+        send[...] = lat_t[...]
+
+    @pl.when(lax.axis_index("tm") != 0)
+    def _():
+        send[...] = cache_t[...]
+
+    for copy in fine_copies:
+        copy.wait()
+
+
+def moments_kernel(lat_t, cache_t, fine, pay, fine_t, up, down):
+    rows, _, width = lat_t.shape
     c2 = fine.shape[0]
-    lat_t[...] = jnp.swapaxes(latent[...], 0, 1)
-    cache_t[...] = jnp.swapaxes(cache[...], 0, 1)
+    fine_t[...] = jnp.swapaxes(fine[...], 0, 1)
     for ref, cut, line in (
-        (up, slice(rows - 2, rows), fine[:, 2 * rows - 1, :]),
-        (down, slice(0, 2), fine[:, 0, :]),
+        (up, slice(rows - 2, rows), fine_t[2 * rows - 1]),
+        (down, slice(0, 2), fine_t[0]),
     ):
         ref[0:2] = lat_t[cut]
         ref[2:4] = cache_t[cut]
         ref[4, :c2] = line[:, :width]
         ref[4, c2:] = line[:, width:]
-
-    @pl.when(lax.axis_index("tm") == 0)
-    def _():
-        send[...] = lat_t[...]
-
-    @pl.when(lax.axis_index("tm") != 0)
-    def _():
-        send[...] = cache_t[...]
-
-
-def moments_kernel(lat_t, fine, pay, fine_t):
-    rows, _, width = lat_t.shape
-    fine_t[...] = jnp.swapaxes(fine[...], 0, 1)
     payload(pay, *moments([lat_t[r] for r in range(rows)], rows * width))
 
 
-def coarse_first(cache_t, above, below, fine_t, weights, acc, fine_pad, stack):
+def coarse_first(cache_t, above, below, fine_t, weights, acc, fine_a, fine_b, stack):
     rows, channels, width = cache_t.shape
-    fine_rows, c2, _ = fine_t.shape
-    fine_pad[1 : fine_rows + 1] = fine_t[...]
-    for r, ref in ((0, above), (fine_rows + 1, below)):
-        fine_pad[r, :, :width] = ref[4, :c2]
-        fine_pad[r, :, width:] = ref[4, c2:]
+    c2 = fine_t.shape[1]
+    early, late = fine_a.shape[0], fine_b.shape[0]
+    fine_a[1:] = fine_t[: early - 1]
+    fine_b[: late - 1] = fine_t[early - 1 :]
+    for rim, ref in ((fine_a.at[0], above), (fine_b.at[late - 1], below)):
+        rim[:, :width] = ref[4, :c2]
+        rim[:, width:] = ref[4, c2:]
     for r in range(2):
         put(stack, 0, r, above[2 + r])
         put(stack, 0, rows + 2 + r, below[2 + r])
@@ -266,19 +297,20 @@
         put(stack, 0, r, value)
 
 
-def put_cache(stack, fine):
+def put_cache(stack, start, fine):
     for r in range(fine.shape[0]):
-        put(stack, 0, r, fine[r])
+        put(stack, 0, start + r, fine[r])
 
 
 def fine_window(stack, m, step):
     return stack[0, 2 * m * step : (2 * m + 4) * step]
 
 
-def fine_first(fine, weights, acc, stack):
-    put_cache(stack, fine)
+def fine_first(fine_a, fine_b, weights, acc, stack):
+    put_cache(stack, 0, fine_a)
+    put_cache(stack, fine_a.shape[0], fine_b)
     for m in range(acc.shape[0]):
-        acc[m] = dot(weights[0], fine_window(stack, m, 3 * fine.shape[1]))
+        acc[m] = dot(weights[0], fine_window(stack, m, 3 * fine_a.shape[1]))
 
 
 def fine_third(raised, stats, gain, shift, weights, acc, out, stack):
@@ -287,25 +319,47 @@
         out[m] = acc[m] + dot(weights[2], fine_window(stack, m, 3 * raised.shape[1]))
 
 
-def fine_second(
-    fine, coarse, stats, gain, shift, bias, weights_up, weights, acc, out,
-    raised, stack_up, stack, turned,
-):
+def raise_other(coarse, weights, raised, stack):
+    @pl.when(lax.axis_index("tm") != 0)
+    def _():
+        raise_rows(rows_of(coarse), weights, raised, stack)
+
+
+def fine_stack(fine_a, raised, stats, gain, shift, stack):
     frame = lax.axis_index("tm")
 
     @pl.when(frame == 0)
     def _():
-        put_cache(stack, fine)
+        put_cache(stack, 0, fine_a)
 
     @pl.when(frame != 0)
     def _():
-        raise_rows(rows_of(coarse), weights_up, raised, stack_up)
         put_active(stack, raised, stats, 0, gain, shift)
 
-    c2 = fine.shape[1]
+
+def fine_second(partial, fine_b, bias, weights, acc, out, stack, turned):
+    late, c2, _ = fine_b.shape
+    start = 2 * acc.shape[0] + 2 - late
+    cut = start * 3 * c2
+
+    @pl.when(lax.axis_index("tm") == 0)
+    def _():
+        put_cache(stack, start, fine_b)
+
+    @pl.when(lax.axis_index("tm") != 0)
+    def _():
+        stack[0, cut:] = partial[0, cut:]
+
     offset = column(bias)
+    whole = cut // (6 * c2) - 1
     for m in range(acc.shape[0]):
-        both = acc[m] + dot(weights[1], fine_window(stack, m, 3 * c2))
+        if m < whole:
+            window = fine_window(partial, m, 3 * c2)
+        else:
+            if m == whole:
+                stack[0, 2 * m * 3 * c2 : cut] = partial[0, 2 * m * 3 * c2 : cut]
+            window = fine_window(stack, m, 3 * c2)
+        both = acc[m] + dot(weights[1], window)
         turned[2 * m] = (both[:c2] + offset).astype(bf16)
         turned[2 * m + 1] = (both[c2:] + offset).astype(bf16)
     out[...] = jnp.swapaxes(turned[...], 0, 1)
@@ -344,30 +398,46 @@
     coarse_shape, coarse_acc = (rows, c1, cols), ((rows + 2, c1, cols), f32)
     fine_acc = ((rows, 2 * c2, fine_cols), f32)
     coarse_stack = pltpu.VMEM((1, (rows + 4) * 3 * c1, cols), bf16)
-    fine_stack = pltpu.VMEM((1, (fine_rows + 2) * 3 * c2, fine_cols), bf16)
+    stack_shape = ((1, (fine_rows + 2) * 3 * c2, fine_cols), bf16)
+    fine_scratch = pltpu.VMEM(*stack_shape)
     up_stack = pltpu.VMEM((1, (rows + 2) * 3 * c1, fine_cols), bf16)
     raised_shape = ((fine_rows + 2, c2, fine_cols), bf16)
 
     rim = ((5, c1, cols), bf16)
-    lat_t, cache_t, send, rim_up, rim_down = call(
-        turn_kernel, "turn", [(coarse_shape, bf16)] * 3 + [rim] * 2
+    early = fine_rows + 2 - 2
+    fine_raw = ((c2, fine_rows, fine_cols), bf16)
+    lat_t, cache_t, send, fine_v = call(
+        turn_kernel,
+        "turn",
+        [(coarse_shape, bf16)] * 3 + [fine_raw],
+        [pltpu.VMEM((c1, rows, cols), bf16)] * 2 + [pltpu.SemaphoreType.DMA((CHUNKS,))] * 3,
+        far=3,
     )(latent[0], coarse_cache[0], fine_cache[0])
+    other = lax.ppermute(send, "tm", [(0, 1), (1, 0)])
+    pay, fine_t, rim_up, rim_down = call(
+        moments_kernel,
+        "moments",
+        [((devices, 1, 4 * GROUPS), f32), ((fine_rows, c2, fine_cols), bf16)] + [rim] * 2,
+    )(lat_t, cache_t, fine_v)
     above = lax.ppermute(rim_up, "tile", forward)
     below = lax.ppermute(rim_down, "tile", backward)
-    other = lax.ppermute(send, "tm", [(0, 1), (1, 0)])
-    pay, fine_t = call(
-        moments_kernel, "moments", [((devices, 1, 4 * GROUPS), f32), ((fine_rows, c2, fine_cols), bf16)]
-    )(lat_t, fine_cache[0])
     w_coarse, w_up, w_fine = call(
         weights_kernel,
         "weights",
         [((3, c1, 9 * c1), bf16), ((2 * c2, 6 * c1), bf16), ((3, 2 * c2, 12 * c2), bf16)],
     )(weight_coarse, weight_up, weight_fine)
-    stats = shared(after(pay, w_coarse, above, below))
-    acc, fine_pad = call(
-        coarse_first, "coarse_first", [coarse_acc, raised_shape], [coarse_stack]
-    )(after(cache_t, stats), above, below, fine_t, w_coarse)
-    other = after(other, stats)
+    stats = shared(after(pay, w_coarse))
+    stats, other, above, below = lax.optimization_barrier((stats, other, above, below))
+    acc, fine_a, fine_b = call(
+        coarse_first,
+        "coarse_first",
+        [
+            coarse_acc,
+            ((early, c2, fine_cols), bf16),
+            ((fine_rows + 2 - early, c2, fine_cols), bf16),
+        ],
+        [coarse_stack],
+    )(cache_t, above, below, fine_t, w_coarse)
     other_above = lax.ppermute(other[rows - 2 :], "tile", forward)
     other_below = lax.ppermute(other[:2], "tile", backward)
     (acc,) = call(coarse_third, "coarse_third", [coarse_acc], [coarse_stack])(
@@ -380,7 +450,7 @@
         w_coarse,
         after(acc, other_above, other_below),
     )
-    fine_r = lax.ppermute(after(fine_pad, other_above, other_below), "tm", earlier)
+    fine_ra = lax.ppermute(after(fine_a, other_above, other_below), "tm", earlier)
     (coarse,) = call(
         coarse_second, "coarse_second", [((rows + 2, c1, cols), bf16)], [coarse_stack]
     )(other, other_above, other_below, stats, gain_coarse, shift_coarse, w_coarse, acc)
@@ -388,27 +458,25 @@
     raised, pay = call(up_kernel, "up", [raised_shape, ((devices, 1, 4 * GROUPS), f32)], [up_stack])(
         coarse, w_up
     )
-    (acc,) = call(fine_first, "fine_first", [fine_acc], [fine_stack])(fine_pad, w_fine)
+    (acc,) = call(fine_first, "fine_first", [fine_acc], [fine_scratch])(fine_a, fine_b, w_fine)
 
     stats = shared(after(pay, acc))
-    (acc,) = call(fine_third, "fine_third", [fine_acc], [fine_stack])(
+    stats, fine_ra, coarse_r = lax.optimization_barrier((stats, fine_ra, coarse_r))
+    (raised_r,) = call(raise_other, "raise_other", [raised_shape], [up_stack])(coarse_r, w_up)
+    fine_rb = lax.ppermute(after(fine_b, raised_r), "tm", earlier)
+    (acc,) = call(fine_third, "fine_third", [fine_acc], [fine_scratch])(
         raised, stats, gain_fine, shift_fine, w_fine, acc
+    )
+    (partial,) = call(fine_stack, "fine_stack", [stack_shape])(
+        fine_ra, raised_r, stats, gain_fine, shift_fine
     )
     (out,) = call(
         fine_second,
         "fine_second",
-        [((c2, fine_rows, fine_cols), bf16)],
-        [
-            pltpu.VMEM(*raised_shape),
-            up_stack,
-            fine_stack,
-            pltpu.VMEM((fine_rows, c2, fine_cols), bf16),
-        ],
+        [fine_raw],
+        [fine_scratch, pltpu.VMEM((fine_rows, c2, fine_cols), bf16)],
         local=False,
-        limit=20,
-    )(
-        fine_r, coarse_r, stats, gain_fine, shift_fine, bias_fine, w_up, w_fine, acc
-    )
+    )(partial, fine_rb, bias_fine, w_fine, acc)
     return out[None]
 
 

time: 107 us -> 99.8 us (0.933)
  the two profiles are of different devices: /device:TPU:16 before, /device:TPU:1 now
where the time goes in v3:
time: 99.8 us; the launch traced here: 99.4 us
  blocking collectives  40.9 us (41%)
  Pallas kernels  28 us (28%)
  starting transfers between devices  24.7 us (25%)
  waiting for transfers between devices  5.45 us (5%)
    all_to_all x2, blocking collectives, shared(): return lax.all_to_all(stats, ('tm', 'tile'), 0, 0)  40.9 us
    pallas_call x12, Pallas kernels, with_arrays(): pl.pallas_call(kernel, in_specs=[pl.BlockSpec(memory_space=pltpu.HBM)] *...  28 us
    ppermute x1, starting transfers between devices, per_device(): coarse_r = lax.ppermute(coarse, 'tm', later)  6.64 us
    ppermute x1, waiting for transfers between devices, per_device(): fine_rb = lax.ppermute(after(fine_b, raised_r), 'tm', earlier)  4.99 us
    ppermute x1, starting transfers between devices, per_device(): above = lax.ppermute(rim_up, 'tile', forward)  3.96 us
    ppermute x1, starting transfers between devices, per_device(): other = lax.ppermute(send, 'tm', [(0, 1), (1, 0)])  3.83 us
    ppermute x1, starting transfers between devices, per_device(): other_above = lax.ppermute(other[rows - 2:], 'tile', forward)  2.97 us
    ppermute x1, starting transfers between devices, per_device(): other_below = lax.ppermute(other[:2], 'tile', backward)  2.59 us
  transfers between devices with their start and end apart: 8, of which 2 were waited for; matrix products, arithmetic and copies ran while one was open for 0% of the time, Pallas kernels for 22%

profile of v3, /device:TPU:1, one launch (start us, length us, event | category | flops | bytes accessed | tf_op | source)
XLA Modules:
  0.0 99.4 jit_solution(2001143623029205425)
XLA Ops:
  0.0 0.0 copy-start.1
  0.0 2.4 %turn.1 = (bf16[8,192,256]{2,1,0:T(8,128)(2,1)S(1)}, bf16[8,192,256]{2,1,0:T(8,128)(2,1)S(1)}, bf16[8,192,256]{2,1,0:T(8,128)(2,1)S(1)}, bf16[96,16,512]{2,1,0:T(8,128)(2,1)S(1)}) custom-call(bf16[192,8,256]{2,1,0:T(8,128)(2,1)} %bitcast.19, bf16[192,8,256]{2,1,0:T(8,128)(2,1)} %bitcast.20, bf16[96,16,512]{2,1,0:T(8,128)(2,1)} %bitcast.18), custom_call_target="tpu_custom_call" | custom-call | tf_op jit(solution)/shard_map/turn/pallas_call | solution.py:18
  2.4 0.0 copy-start
  2.4 0.0 copy-start.2
  2.4 3.8 %collective-permute-start = (bf16[8,192,256]{2,1,0:T(8,128)(2,1)S(1)}, bf16[8,192,256]{2,1,0:T(8,128)(2,1)S(1)}, u32[]{:S(2)}, u32[]{:S(2)}) collective-permute-start(bf16[8,192,256]{2,1,0:T(8,128)(2,1)S(1)} %get-tuple-element.39), channel_id=1, source_target_pairs={{0,64},{64,0},{1,65},{65,1},{2,66},{66,2},{3,67},{67,3},{4,68},{68... | collective-permute-start | bytes 2359304 | tf_op jit(solution)/shard_map/ppermute | solution.py:416
  6.2 1.7 %moments.1 = (f32[128,1,128]{2,1,0:T(1,128)S(1)}, bf16[16,96,512]{2,1,0:T(8,128)(2,1)S(1)}, bf16[5,192,256]{2,1,0:T(8,128)(2,1)S(1)}, bf16[5,192,256]{2,1,0:T(8,128)(2,1)S(1)}) custom-call(bf16[8,192,256]{2,1,0:T(8,128)(2,1)S(1)} %get-tuple-element.33.lat_t, bf16[8,192,256]{2,1,0:T(8,128)(2,1)S(1)} %get-tuple-element.34.cache_t, ...), custom_call_target="tpu_custom_call" | custom-call | tf_op jit(solution)/shard_map/moments/pallas_call | solution.py:18
  8.0 4.0 %collective-permute-start.1 = (bf16[5,192,256]{2,1,0:T(8,128)(2,1)S(1)}, bf16[5,192,256]{2,1,0:T(8,128)(2,1)S(1)}, u32[]{:S(2)}, u32[]{:S(2)}) collective-permute-start(bf16[5,192,256]{2,1,0:T(8,128)(2,1)S(1)} %get-tuple-element.40), channel_id=1, source_target_pairs={{0,1},{1,2},{2,3},{3,4},{4,5},{5,6},{6,7},{7,8},{8,9},{9,10},{10,1... | collective-permute-start | bytes 1474568 | tf_op jit(solution)/shard_map/ppermute | solution.py:422
  11.9 1.9 %collective-permute-start.2 = (bf16[5,192,256]{2,1,0:T(8,128)(2,1)S(1)}, bf16[5,192,256]{2,1,0:T(8,128)(2,1)S(1)}, u32[]{:S(2)}, u32[]{:S(2)}) collective-permute-start(bf16[5,192,256]{2,1,0:T(8,128)(2,1)S(1)} %get-tuple-element.41), channel_id=1, source_target_pairs={{1,0},{2,1},{3,2},{4,3},{5,4},{6,5},{7,6},{8,7},{9,8},{10,9},{11,1... | collective-permute-start | bytes 1474568 | tf_op jit(solution)/shard_map/ppermute | solution.py:423
  13.9 0.0 copy-done.1
  13.9 0.0 copy-done
  13.9 0.0 copy-done.2
  13.9 1.0 %weights.1 = (bf16[3,192,1728]{2,1,0:T(8,128)(2,1)S(1)}, bf16[192,1152]{1,0:T(8,128)(2,1)S(1)}, bf16[3,192,1152]{2,1,0:T(8,128)(2,1)S(1)}) custom-call(bf16[3,3,3,192,192]{4,3,2,1,0:T(8,128)(2,1)S(1)} %copy-done, bf16[3,3,96,192]{3,2,1,0:T(8,128)(2,1)S(1)} %copy-done.2, bf16[3,3,3,96,96]{4,3,2,1,0:T(8,128)(2,1)S(1)} %copy-done.1), custom_call_target="tpu_custom_call" | custom-call | tf_op jit(solution)/shard_map/weights/pallas_call | solution.py:18
  14.9 18.8 %all_to_all.10.stats = f32[128,1,128]{2,1,0:T(1,128)S(1)} all-to-all(f32[128,1,128]{2,1,0:T(1,128)S(1)} %get-tuple-element.38), channel_id=1, replica_groups=mesh['tm'=2,'tile'=64] {'tm','tile'}, dimensions={0} | all-to-all | bytes 131072 | tf_op jit(solution)/shard_map/all_to_all | solution.py:392
  33.7 0.0 collective-permute-done.1.above
  33.7 0.0 collective-permute-done.2.below
  33.7 0.0 collective-permute-done.other
  33.7 2.6 %collective-permute-start.4 = (bf16[2,192,256]{2,1,0:T(8,128)(2,1)S(1)}, bf16[2,192,256]{2,1,0:T(8,128)(2,1)S(1)}, u32[]{:S(2)}, u32[]{:S(2)}) collective-permute-start(bf16[2,192,256]{2,1,0:T(8,128)(2,1)S(1)} %get-tuple-element.61), channel_id=1, source_target_pairs={{1,0},{2,1},{3,2},{4,3},{5,4},{6,5},{7,6},{8,7},{9,8},{10,9},{11,1... | collective-permute-start | bytes 589832 | tf_op jit(solution)/shard_map/ppermute | solution.py:442
  36.3 3.0 %collective-permute-start.3 = (bf16[2,192,256]{2,1,0:T(8,128)(2,1)S(1)}, bf16[2,192,256]{2,1,0:T(8,128)(2,1)S(1)}, u32[]{:S(2)}, u32[]{:S(2)}) collective-permute-start(bf16[2,192,256]{2,1,0:T(8,128)(2,1)S(1)} %get-tuple-element.62), channel_id=1, source_target_pairs={{0,1},{1,2},{2,3},{3,4},{4,5},{5,6},{6,7},{7,8},{8,9},{9,10},{10,1... | collective-permute-start | bytes 589832 | tf_op jit(solution)/shard_map/ppermute | solution.py:441
  39.3 0.0 copy-start.3
  39.3 0.0 copy-start.4
  39.3 2.1 %coarse_first.1 = (f32[10,192,256]{2,1,0:T(8,128)S(1)}, bf16[16,96,512]{2,1,0:T(8,128)(2,1)S(1)}, bf16[2,96,512]{2,1,0:T(8,128)(2,1)S(1)}) custom-call(bf16[8,192,256]{2,1,0:T(8,128)(2,1)S(1)} %get-tuple-element.34.cache_t, bf16[5,192,256]{2,1,0:T(8,128)(2,1)S(1)} %collective-permute-done.1.above, bf16[5,192,256]{2,1,0:T(8,128)(2,1)S(1)} %collective-permute-done.2.below, ...), custom_call_target="tpu_custom_call" | custom-call | tf_op jit(solution)/shard_map/coarse_first/pallas_call | solution.py:18
  41.4 0.0 collective-permute-done.4.below
  41.5 0.4 collective-permute-done.3.above
  41.9 1.3 %collective-permute-start.5 = (bf16[16,96,512]{2,1,0:T(8,128)(2,1)S(1)}, bf16[16,96,512]{2,1,0:T(8,128)(2,1)S(1)}, u32[]{:S(2)}, u32[]{:S(2)}) collective-permute-start(bf16[16,96,512]{2,1,0:T(8,128)(2,1)S(1)} %get-tuple-element.55.fine_a), channel_id=1, source_target_pairs={{64,0},{65,1},{66,2},{67,3},{68,4},{69,5},{70,6},{71,7},{72,8},{73... | collective-permute-start | bytes 4718600 | tf_op jit(solution)/shard_map/ppermute | solution.py:453
  43.2 0.0 copy-done.3
  43.2 0.0 copy-done.4
  43.2 2.9 %coarse_third.1.acc = f32[10,192,256]{2,1,0:T(8,128)S(1)} custom-call(bf16[8,192,256]{2,1,0:T(8,128)(2,1)S(1)} %get-tuple-element.33.lat_t, bf16[5,192,256]{2,1,0:T(8,128)(2,1)S(1)} %collective-permute-done.1.above, bf16[5,192,256]{2,1,0:T(8,128)(2,1)S(1)} %collective-permute-done.2.below, f32[128,1,128]{2,1,0:T(1,128)S(1)} %all_to_all.10.stats, ...), custom_call_target="tpu_custom_call" | custom-call | tf_op jit(solution)/shard_map/coarse_third/pallas_call | solution.py:18
  46.1 2.9 %coarse_second.1.coarse = bf16[10,192,256]{2,1,0:T(8,128)(2,1)S(1)} custom-call(bf16[8,192,256]{2,1,0:T(8,128)(2,1)S(1)} %collective-permute-done.other, bf16[2,192,256]{2,1,0:T(8,128)(2,1)S(1)} %collective-permute-done.3.above, bf16[2,192,256]{2,1,0:T(8,128)(2,1)S(1)} %collective-permute-done.4.below, f32[128,1,128]{2,1,0:T(1,128)S(1)} %all_to_all.10.stats, ...), custom_call_target="tpu_custom_call" | custom-call | tf_op jit(solution)/shard_map/coarse_second/pallas_call | solution.py:18
  49.0 6.6 %collective-permute-start.6 = (bf16[10,192,256]{2,1,0:T(8,128)(2,1)S(1)}, bf16[10,192,256]{2,1,0:T(8,128)(2,1)S(1)}, u32[]{:S(2)}, u32[]{:S(2)}) collective-permute-start(bf16[10,192,256]{2,1,0:T(8,128)(2,1)S(1)} %coarse_second.1.coarse), channel_id=1, source_target_pairs={{0,64},{1,65},{2,66},{3,67},{4,68},{5,69},{6,70},{7,71},{8,72},{9,... | collective-permute-start | bytes 2949128 | tf_op jit(solution)/shard_map/ppermute | solution.py:457
  55.7 2.3 %fine_first.1.acc = f32[8,192,512]{2,1,0:T(8,128)S(1)} custom-call(bf16[16,96,512]{2,1,0:T(8,128)(2,1)S(1)} %get-tuple-element.55.fine_a, bf16[2,96,512]{2,1,0:T(8,128)(2,1)S(1)} %get-tuple-element.59.fine_b, bf16[3,192,1152]{2,1,0:T(8,128)(2,1)S(1)} %get-tuple-element.53.weights), custom_call_target="tpu_custom_call" | custom-call | tf_op jit(solution)/shard_map/fine_first/pallas_call | solution.py:18
  58.0 4.4 %up.3 = (bf16[18,96,512]{2,1,0:T(8,128)(2,1)S(1)}, f32[128,1,128]{2,1,0:T(1,128)S(1)}) custom-call(bf16[10,192,256]{2,1,0:T(8,128)(2,1)S(1)} %coarse_second.1.coarse, bf16[192,1152]{1,0:T(8,128)(2,1)S(1)} %get-tuple-element.49.weights), custom_call_target="tpu_custom_call" | custom-call | tf_op jit(solution)/shard_map/up/pallas_call | solution.py:18
  62.4 0.0 copy-start.5
  62.4 0.0 copy-start.6
  62.4 22.2 %all_to_all.11.stats = f32[128,1,128]{2,1,0:T(1,128)S(1)} all-to-all(f32[128,1,128]{2,1,0:T(1,128)S(1)} %get-tuple-element.54), channel_id=1, replica_groups=mesh['tm'=2,'tile'=64] {'tm','tile'}, dimensions={0} | all-to-all | bytes 131072 | tf_op jit(solution)/shard_map/all_to_all | solution.py:392
  84.6 0.0 collective-permute-done.6.coarse
  84.6 0.0 collective-permute-done.5.fine_a
  84.6 1.5 %collective-permute-start.7 = (bf16[2,96,512]{2,1,0:T(8,128)(2,1)S(1)}, bf16[2,96,512]{2,1,0:T(8,128)(2,1)S(1)}, u32[]{:S(2)}, u32[]{:S(2)}) collective-permute-start(bf16[2,96,512]{2,1,0:T(8,128)(2,1)S(1)} %get-tuple-element.59.fine_b), channel_id=1, source_target_pairs={{64,0},{65,1},{66,2},{67,3},{68,4},{69,5},{70,6},{71,7},{72,8},{73... | collective-permute-start | bytes 589832 | tf_op jit(solution)/shard_map/ppermute | solution.py:466
  86.1 0.0 copy-done.5
  86.1 0.0 copy-done.6
  86.1 3.4 %fine_third.1.acc = f32[8,192,512]{2,1,0:T(8,128)S(1)} custom-call(bf16[18,96,512]{2,1,0:T(8,128)(2,1)S(1)} %get-tuple-element.60.raised, f32[128,1,128]{2,1,0:T(1,128)S(1)} %all_to_all.11.stats, f32[1,96]{1,0:T(1,128)S(1)} %bitcast.13, f32[1,96]{1,0:T(1,128)S(1)} %bitcast.15, bf16[3,192,1152]{2,1,0:T(8,128)(2,1)S(1)} %get-tuple-element.53.weights, ...), custom_call_target="tpu_custom_call" | custom-call | tf_op jit(solution)/shard_map/fine_third/pallas_call | solution.py:18
  89.5 0.0 copy-start.7
  89.5 0.9 fine_stack.1.partial
  90.5 5.0 %collective-permute-done.7.fine_b = bf16[2,96,512]{2,1,0:T(8,128)(2,1)S(1)} collective-permute-done((bf16[2,96,512]{2,1,0:T(8,128)(2,1)S(1)}, bf16[2,96,512]{2,1,0:T(8,128)(2,1)S(1)}, u32[]{:S(2)}, u32[]{:S(2)}) %collective-permute-start.7) | collective-permute-done | bytes 196640 | tf_op jit(solution)/shard_map/ppermute | solution.py:466
  95.4 0.0 copy-done.7
  95.5 4.0 %fine_second.1 = bf16[96,16,512]{2,1,0:T(8,128)(2,1)} custom-call(bf16[1,5184,512]{2,1,0:T(8,128)(2,1)S(1)} %fine_stack.1.partial, bf16[2,96,512]{2,1,0:T(8,128)(2,1)S(1)} %collective-permute-done.7.fine_b, f32[1,96]{1,0:T(1,128)S(1)} %bitcast.17, bf16[3,192,1152]{2,1,0:T(8,128)(2,1)S(1)} %get-tuple-element.53.weights, f32[8,192,512]{2,1,0:T(8,128)S(1)} %fine_third.1.acc), custom_call_target="tpu_custom_call" | custom-call | tf_op jit(solution)/shard_map/fine_second/pallas_call | solution.py:18
  (2 shorter events, 0.0 us)
Async XLA Ops:
  0.0 13.9 %copy-start.1 = (bf16[3,3,3,96,96]{4,3,2,1,0:T(8,128)(2,1)S(1)}, bf16[3,3,3,96,96]{4,3,2,1,0:T(8,128)(2,1)}, u32[]{:S(2)}) copy-start(bf16[3,3,3,96,96]{4,3,2,1,0:T(8,128)(2,1)} %fine.1) | copy-start | bytes 1492996
  2.4 11.5 %copy-start = (bf16[3,3,3,192,192]{4,3,2,1,0:T(8,128)(2,1)S(1)}, bf16[3,3,3,192,192]{4,3,2,1,0:T(8,128)(2,1)}, u32[]{:S(2)}) copy-start(bf16[3,3,3,192,192]{4,3,2,1,0:T(8,128)(2,1)} %coarse.1) | copy-start | bytes 5971972
  2.4 11.5 %copy-start.2 = (bf16[3,3,96,192]{3,2,1,0:T(8,128)(2,1)S(1)}, bf16[3,3,96,192]{3,2,1,0:T(8,128)(2,1)}, u32[]{:S(2)}) copy-start(bf16[3,3,96,192]{3,2,1,0:T(8,128)(2,1)} %up.2) | copy-start | bytes 995332
  2.4 31.3 %collective-permute-start = (bf16[8,192,256]{2,1,0:T(8,128)(2,1)S(1)}, bf16[8,192,256]{2,1,0:T(8,128)(2,1)S(1)}, u32[]{:S(2)}, u32[]{:S(2)}) collective-permute-start(bf16[8,192,256]{2,1,0:T(8,128)(2,1)S(1)} %get-tuple-element.39), channel_id=1, source_target_pairs={{0,64},{64,0},{1,65},{65,1},{2,66},{66,2},{3,67},{67,3},{4,68},{68... | collective-permute-start | bytes 2359304 | tf_op jit(solution)/shard_map/ppermute | solution.py:416
  8.0 25.7 %collective-permute-start.1 = (bf16[5,192,256]{2,1,0:T(8,128)(2,1)S(1)}, bf16[5,192,256]{2,1,0:T(8,128)(2,1)S(1)}, u32[]{:S(2)}, u32[]{:S(2)}) collective-permute-start(bf16[5,192,256]{2,1,0:T(8,128)(2,1)S(1)} %get-tuple-element.40), channel_id=1, source_target_pairs={{0,1},{1,2},{2,3},{3,4},{4,5},{5,6},{6,7},{7,8},{8,9},{9,10},{10,1... | collective-permute-start | bytes 1474568 | tf_op jit(solution)/shard_map/ppermute | solution.py:422
  11.9 21.8 %collective-permute-start.2 = (bf16[5,192,256]{2,1,0:T(8,128)(2,1)S(1)}, bf16[5,192,256]{2,1,0:T(8,128)(2,1)S(1)}, u32[]{:S(2)}, u32[]{:S(2)}) collective-permute-start(bf16[5,192,256]{2,1,0:T(8,128)(2,1)S(1)} %get-tuple-element.41), channel_id=1, source_target_pairs={{1,0},{2,1},{3,2},{4,3},{5,4},{6,5},{7,6},{8,7},{9,8},{10,9},{11,1... | collective-permute-start | bytes 1474568 | tf_op jit(solution)/shard_map/ppermute | solution.py:423
  33.7 7.7 %collective-permute-start.4 = (bf16[2,192,256]{2,1,0:T(8,128)(2,1)S(1)}, bf16[2,192,256]{2,1,0:T(8,128)(2,1)S(1)}, u32[]{:S(2)}, u32[]{:S(2)}) collective-permute-start(bf16[2,192,256]{2,1,0:T(8,128)(2,1)S(1)} %get-tuple-element.61), channel_id=1, source_target_pairs={{1,0},{2,1},{3,2},{4,3},{5,4},{6,5},{7,6},{8,7},{9,8},{10,9},{11,1... | collective-permute-start | bytes 589832 | tf_op jit(solution)/shard_map/ppermute | solution.py:442
  36.3 5.6 %collective-permute-start.3 = (bf16[2,192,256]{2,1,0:T(8,128)(2,1)S(1)}, bf16[2,192,256]{2,1,0:T(8,128)(2,1)S(1)}, u32[]{:S(2)}, u32[]{:S(2)}) collective-permute-start(bf16[2,192,256]{2,1,0:T(8,128)(2,1)S(1)} %get-tuple-element.62), channel_id=1, source_target_pairs={{0,1},{1,2},{2,3},{3,4},{4,5},{5,6},{6,7},{7,8},{8,9},{9,10},{10,1... | collective-permute-start | bytes 589832 | tf_op jit(solution)/shard_map/ppermute | solution.py:441
  39.3 3.9 %copy-start.3 = (f32[192]{0:T(256)S(1)}, f32[192]{0:T(256)}, u32[]{:S(2)}) copy-start(f32[192]{0:T(256)} %param.14) | copy-start | bytes 2308
  39.3 3.9 %copy-start.4 = (f32[192]{0:T(256)S(1)}, f32[192]{0:T(256)}, u32[]{:S(2)}) copy-start(f32[192]{0:T(256)} %param.15) | copy-start | bytes 2308
  41.9 42.7 %collective-permute-start.5 = (bf16[16,96,512]{2,1,0:T(8,128)(2,1)S(1)}, bf16[16,96,512]{2,1,0:T(8,128)(2,1)S(1)}, u32[]{:S(2)}, u32[]{:S(2)}) collective-permute-start(bf16[16,96,512]{2,1,0:T(8,128)(2,1)S(1)} %get-tuple-element.55.fine_a), channel_id=1, source_target_pairs={{64,0},{65,1},{66,2},{67,3},{68,4},{69,5},{70,6},{71,7},{72,8},{73... | collective-permute-start | bytes 4718600 | tf_op jit(solution)/shard_map/ppermute | solution.py:453
  49.0 35.6 %collective-permute-start.6 = (bf16[10,192,256]{2,1,0:T(8,128)(2,1)S(1)}, bf16[10,192,256]{2,1,0:T(8,128)(2,1)S(1)}, u32[]{:S(2)}, u32[]{:S(2)}) collective-permute-start(bf16[10,192,256]{2,1,0:T(8,128)(2,1)S(1)} %coarse_second.1.coarse), channel_id=1, source_target_pairs={{0,64},{1,65},{2,66},{3,67},{4,68},{5,69},{6,70},{7,71},{8,72},{9,... | collective-permute-start | bytes 2949128 | tf_op jit(solution)/shard_map/ppermute | solution.py:457
  62.4 23.7 %copy-start.5 = (f32[96]{0:T(128)S(1)}, f32[96]{0:T(128)}, u32[]{:S(2)}) copy-start(f32[96]{0:T(128)} %param.18) | copy-start | bytes 1156
  62.4 23.7 %copy-start.6 = (f32[96]{0:T(128)S(1)}, f32[96]{0:T(128)}, u32[]{:S(2)}) copy-start(f32[96]{0:T(128)} %param.19) | copy-start | bytes 1156
  84.6 10.9 %collective-permute-start.7 = (bf16[2,96,512]{2,1,0:T(8,128)(2,1)S(1)}, bf16[2,96,512]{2,1,0:T(8,128)(2,1)S(1)}, u32[]{:S(2)}, u32[]{:S(2)}) collective-permute-start(bf16[2,96,512]{2,1,0:T(8,128)(2,1)S(1)} %get-tuple-element.59.fine_b), channel_id=1, source_target_pairs={{64,0},{65,1},{66,2},{67,3},{68,4},{69,5},{70,6},{71,7},{72,8},{73... | collective-permute-start | bytes 589832 | tf_op jit(solution)/shard_map/ppermute | solution.py:466
  89.5 5.9 %copy-start.7 = (f32[96]{0:T(128)S(1)}, f32[96]{0:T(128)}, u32[]{:S(2)}) copy-start(f32[96]{0:T(128)} %param.21) | copy-start | bytes 1156

commit v4 on v3

--- a/solution.py
+++ b/solution.py
@@ -133,6 +133,17 @@
 CHUNKS = 4
 
 
+def fold(ref, line):
+    channels, width = line.shape
+    ref[:channels] = line[:, : width // 2]
+    ref[channels:] = line[:, width // 2 :]
+
+
+def unfold(ref):
+    channels = ref.shape[0] // 2
+    return jnp.concatenate([ref[:channels], ref[channels:]], axis=1)
+
+
 def fetches(source, target, arrived):
     part = source.shape[0] // CHUNKS
     cuts = [pl.ds(k * part, part) for k in range(CHUNKS)]
@@ -171,7 +182,6 @@
 
 def moments_kernel(lat_t, cache_t, fine, pay, fine_t, up, down):
     rows, _, width = lat_t.shape
-    c2 = fine.shape[0]
     fine_t[...] = jnp.swapaxes(fine[...], 0, 1)
     for ref, cut, line in (
         (up, slice(rows - 2, rows), fine_t[2 * rows - 1]),
@@ -179,20 +189,12 @@
     ):
         ref[0:2] = lat_t[cut]
         ref[2:4] = cache_t[cut]
-        ref[4, :c2] = line[:, :width]
-        ref[4, c2:] = line[:, width:]
+        fold(ref.at[4], line)
     payload(pay, *moments([lat_t[r] for r in range(rows)], rows * width))
 
 
-def coarse_first(cache_t, above, below, fine_t, weights, acc, fine_a, fine_b, stack):
+def coarse_first(cache_t, above, below, weights, acc, stack):
     rows, channels, width = cache_t.shape
-    c2 = fine_t.shape[1]
-    early, late = fine_a.shape[0], fine_b.shape[0]
-    fine_a[1:] = fine_t[: early - 1]
-    fine_b[: late - 1] = fine_t[early - 1 :]
-    for rim, ref in ((fine_a.at[0], above), (fine_b.at[late - 1], below)):
-        rim[:, :width] = ref[4, :c2]
-        rim[:, width:] = ref[4, c2:]
     for r in range(2):
         put(stack, 0, r, above[2 + r])
         put(stack, 0, rows + 2 + r, below[2 + r])
@@ -234,7 +236,7 @@
 
 
 def coarse_second(
-    other, above, below, stats, gain, shift, weights, acc, out, stack
+    other, above, below, stats, gain, shift, weights, acc, out, rims, stack
 ):
     frame = lax.axis_index("tm")
     tile = lax.axis_index("tile")
@@ -258,7 +260,8 @@
             value = value * jnp.where(tile == 0, 0.0, 1.0)
         if r == rows + 1:
             value = value * jnp.where(tile == last, 0.0, 1.0)
-        out[r] = value.astype(bf16)
+        target = rims.at[r // rows] if r in (0, rows + 1) else out.at[r - 1]
+        target[...] = value.astype(bf16)
 
 
 def raise_rows(coarse, weights, raised, stack):
@@ -276,8 +279,19 @@
         raised[2 * m + 1] = both[c2:]
 
 
-def up_kernel(coarse, weights, raised, pay, stack):
-    raise_rows(rows_of(coarse), weights, raised, stack)
+def up_kernel(coarse, rims, above, below, weights, raised, pay, late, stack):
+    frame = lax.axis_index("tm")
+
+    @pl.when(frame == 0)
+    def _():
+        late[...] = rims[...]
+
+    @pl.when(frame != 0)
+    def _():
+        late[0] = above[4]
+        late[1] = below[4]
+
+    raise_rows([rims.at[0], *rows_of(coarse), rims.at[1]], weights, raised, stack)
     count = raised.shape[0] - 2
     payload(pay, *moments([raised[r + 1] for r in range(count)], count * raised.shape[2]))
 
@@ -285,7 +299,7 @@
 def put_active(stack, raised, stats, frame, gain, shift):
     tile = lax.axis_index("tile")
     last = lax.axis_size("tile") - 1
-    rows, channels, width = raised.shape
+    rows, (channels, width) = len(raised), raised[0].shape
     centre, spread = combine(stats, frame, channels, (rows - 2) * width)
     scale, offset = spread * column(gain), column(shift)
     for r in range(rows):
@@ -297,69 +311,65 @@
         put(stack, 0, r, value)
 
 
-def put_cache(stack, start, fine):
-    for r in range(fine.shape[0]):
-        put(stack, 0, start + r, fine[r])
+def put_rims(stack, last, above, below):
+    put(stack, 0, 0, unfold(above))
+    put(stack, 0, last, unfold(below))
+
+
+def put_cache(stack, fine_t):
+    for r in range(fine_t.shape[0]):
+        put(stack, 0, 1 + r, fine_t[r])
 
 
 def fine_window(stack, m, step):
     return stack[0, 2 * m * step : (2 * m + 4) * step]
 
 
-def fine_first(fine_a, fine_b, weights, acc, stack):
-    put_cache(stack, 0, fine_a)
-    put_cache(stack, fine_a.shape[0], fine_b)
+def fine_first(fine_t, above, below, weights, acc, stack):
+    put_rims(stack, fine_t.shape[0] + 1, above.at[4], below.at[4])
+    put_cache(stack, fine_t)
     for m in range(acc.shape[0]):
-        acc[m] = dot(weights[0], fine_window(stack, m, 3 * fine_a.shape[1]))
+        acc[m] = dot(weights[0], fine_window(stack, m, 3 * fine_t.shape[1]))
 
 
 def fine_third(raised, stats, gain, shift, weights, acc, out, stack):
-    put_active(stack, raised, stats, lax.axis_index("tm"), gain, shift)
+    put_active(stack, rows_of(raised), stats, lax.axis_index("tm"), gain, shift)
     for m in range(acc.shape[0]):
         out[m] = acc[m] + dot(weights[2], fine_window(stack, m, 3 * raised.shape[1]))
 
 
-def raise_other(coarse, weights, raised, stack):
-    @pl.when(lax.axis_index("tm") != 0)
-    def _():
-        raise_rows(rows_of(coarse), weights, raised, stack)
-
-
-def fine_stack(fine_a, raised, stats, gain, shift, stack):
+def fine_begin(fine_r, coarse, weights, raised, stack, stack_up):
     frame = lax.axis_index("tm")
 
     @pl.when(frame == 0)
     def _():
-        put_cache(stack, 0, fine_a)
+        put_cache(stack, fine_r)
 
     @pl.when(frame != 0)
     def _():
-        put_active(stack, raised, stats, 0, gain, shift)
-
-
-def fine_second(partial, fine_b, bias, weights, acc, out, stack, turned):
-    late, c2, _ = fine_b.shape
-    start = 2 * acc.shape[0] + 2 - late
-    cut = start * 3 * c2
-
-    @pl.when(lax.axis_index("tm") == 0)
-    def _():
-        put_cache(stack, start, fine_b)
-
-    @pl.when(lax.axis_index("tm") != 0)
-    def _():
-        stack[0, cut:] = partial[0, cut:]
-
+        raise_rows(rows_of(coarse), weights, raised, stack_up)
+
+
+def fine_end(begun, coarse, late, raised, stats, gain, shift, weights, stack, ends, stack_up):
+    frame = lax.axis_index("tm")
+
+    @pl.when(frame == 0)
+    def _():
+        put_rims(stack, 2 * coarse.shape[0] + 1, late.at[0], late.at[1])
+
+    @pl.when(frame != 0)
+    def _():
+        top, bottom = ends.at[0:2], ends.at[2:4]
+        raise_rows([late.at[0], coarse.at[0]], weights, top, stack_up)
+        raise_rows([coarse.at[coarse.shape[0] - 1], late.at[1]], weights, bottom, stack_up)
+        put_active(stack, rows_of(top, raised, bottom), stats, 0, gain, shift)
+
+
+def fine_second(stack, bias, weights, acc, out, turned):
+    c2 = out.shape[0]
     offset = column(bias)
-    whole = cut // (6 * c2) - 1
     for m in range(acc.shape[0]):
-        if m < whole:
-            window = fine_window(partial, m, 3 * c2)
-        else:
-            if m == whole:
-                stack[0, 2 * m * 3 * c2 : cut] = partial[0, 2 * m * 3 * c2 : cut]
-            window = fine_window(stack, m, 3 * c2)
-        both = acc[m] + dot(weights[1], window)
+        both = acc[m] + dot(weights[1], fine_window(stack, m, 3 * c2))
         turned[2 * m] = (both[:c2] + offset).astype(bf16)
         turned[2 * m + 1] = (both[c2:] + offset).astype(bf16)
     out[...] = jnp.swapaxes(turned[...], 0, 1)
@@ -404,7 +414,6 @@
     raised_shape = ((fine_rows + 2, c2, fine_cols), bf16)
 
     rim = ((5, c1, cols), bf16)
-    early = fine_rows + 2 - 2
     fine_raw = ((c2, fine_rows, fine_cols), bf16)
     lat_t, cache_t, send, fine_v = call(
         turn_kernel,
@@ -428,16 +437,9 @@
     )(weight_coarse, weight_up, weight_fine)
     stats = shared(after(pay, w_coarse))
     stats, other, above, below = lax.optimization_barrier((stats, other, above, below))
-    acc, fine_a, fine_b = call(
-        coarse_first,
-        "coarse_first",
-        [
-            coarse_acc,
-            ((early, c2, fine_cols), bf16),
-            ((fine_rows + 2 - early, c2, fine_cols), bf16),
-        ],
-        [coarse_stack],
-    )(cache_t, above, below, fine_t, w_coarse)
+    (acc,) = call(coarse_first, "coarse_first", [coarse_acc], [coarse_stack])(
+        cache_t, above, below, w_coarse
+    )
     other_above = lax.ppermute(other[rows - 2 :], "tile", forward)
     other_below = lax.ppermute(other[:2], "tile", backward)
     (acc,) = call(coarse_third, "coarse_third", [coarse_acc], [coarse_stack])(
@@ -450,33 +452,50 @@
         w_coarse,
         after(acc, other_above, other_below),
     )
-    fine_ra = lax.ppermute(after(fine_a, other_above, other_below), "tm", earlier)
-    (coarse,) = call(
-        coarse_second, "coarse_second", [((rows + 2, c1, cols), bf16)], [coarse_stack]
+    fine_r = lax.ppermute(after(fine_t, other_above, other_below), "tm", earlier)
+    coarse, coarse_rims = call(
+        coarse_second,
+        "coarse_second",
+        [(coarse_shape, bf16), ((2, c1, cols), bf16)],
+        [coarse_stack],
     )(other, other_above, other_below, stats, gain_coarse, shift_coarse, w_coarse, acc)
     coarse_r = lax.ppermute(coarse, "tm", later)
-    raised, pay = call(up_kernel, "up", [raised_shape, ((devices, 1, 4 * GROUPS), f32)], [up_stack])(
-        coarse, w_up
+    raised, pay, late = call(
+        up_kernel,
+        "up",
+        [raised_shape, ((devices, 1, 4 * GROUPS), f32), ((2, c1, cols), bf16)],
+        [up_stack],
+    )(coarse, coarse_rims, above, below, w_up)
+    (acc,) = call(fine_first, "fine_first", [fine_acc], [fine_scratch])(
+        fine_t, above, below, w_fine
     )
-    (acc,) = call(fine_first, "fine_first", [fine_acc], [fine_scratch])(fine_a, fine_b, w_fine)
 
     stats = shared(after(pay, acc))
-    stats, fine_ra, coarse_r = lax.optimization_barrier((stats, fine_ra, coarse_r))
-    (raised_r,) = call(raise_other, "raise_other", [raised_shape], [up_stack])(coarse_r, w_up)
-    fine_rb = lax.ppermute(after(fine_b, raised_r), "tm", earlier)
+    stats, fine_r, coarse_r = lax.optimization_barrier((stats, fine_r, coarse_r))
+    late = lax.ppermute(after(late, stats), "tm", [(0, 1), (1, 0)])
+    raised_r, stack = call(
+        fine_begin,
+        "fine_begin",
+        [((fine_rows - 2, c2, fine_cols), bf16), stack_shape],
+        [up_stack],
+    )(fine_r, coarse_r, w_up)
     (acc,) = call(fine_third, "fine_third", [fine_acc], [fine_scratch])(
         raised, stats, gain_fine, shift_fine, w_fine, acc
     )
-    (partial,) = call(fine_stack, "fine_stack", [stack_shape])(
-        fine_ra, raised_r, stats, gain_fine, shift_fine
-    )
+    (stack,) = call(
+        fine_end,
+        "fine_end",
+        [stack_shape],
+        [pltpu.VMEM((4, c2, fine_cols), bf16), up_stack],
+        aliases={0: 0},
+    )(stack, coarse_r, late, raised_r, stats, gain_fine, shift_fine, w_up)
     (out,) = call(
         fine_second,
         "fine_second",
         [fine_raw],
-        [fine_scratch, pltpu.VMEM((fine_rows, c2, fine_cols), bf16)],
+        [pltpu.VMEM((fine_rows, c2, fine_cols), bf16)],
         local=False,
-    )(partial, fine_rb, bias_fine, w_fine, acc)
+    )(stack, bias_fine, w_fine, acc)
     return out[None]
 
 

time: 99.8 us -> 98.6 us (0.988)
  the two profiles are of different devices: /device:TPU:1 before, /device:TPU:16 now
where the time goes in v4:
time: 98.6 us; the launch traced here: 98.3 us
  blocking collectives  49.1 us (50%)
  Pallas kernels  33.8 us (34%)
  starting transfers between devices  14 us (14%)
  waiting for transfers between devices  1.05 us (1%)
    all_to_all x2, blocking collectives, shared(): return lax.all_to_all(stats, ('tm', 'tile'), 0, 0)  49.1 us
    pallas_call x12, Pallas kernels, with_arrays(): pl.pallas_call(kernel, in_specs=[pl.BlockSpec(memory_space=pltpu.HBM)] *...  33.8 us
    ppermute x1, starting transfers between devices, per_device(): other_above = lax.ppermute(other[rows - 2:], 'tile', forward)  3.04 us
    ppermute x1, starting transfers between devices, per_device(): lax.ppermute(after(fine_t, other_above, other_below), 'tm', earlier)  2.62 us
    ppermute x1, starting transfers between devices, per_device(): late = lax.ppermute(after(late, stats), 'tm', [(0, 1), (1, 0)])  2.57 us
  transfers between devices with their start and end apart: 8, of which 1 were waited for; matrix products, arithmetic and copies ran while one was open for 0% of the time, Pallas kernels for 25%

profile of v4, /device:TPU:16, one launch (start us, length us, event | category | flops | bytes accessed | tf_op | source)
XLA Modules:
  0.0 98.3 jit_solution(13411321320436286204)
XLA Ops:
  0.0 0.0 copy-start.1
  0.0 2.4 %turn.1 = (bf16[8,192,256]{2,1,0:T(8,128)(2,1)S(1)}, bf16[8,192,256]{2,1,0:T(8,128)(2,1)S(1)}, bf16[8,192,256]{2,1,0:T(8,128)(2,1)S(1)}, bf16[96,16,512]{2,1,0:T(8,128)(2,1)S(1)}) custom-call(bf16[192,8,256]{2,1,0:T(8,128)(2,1)} %bitcast.19, bf16[192,8,256]{2,1,0:T(8,128)(2,1)} %bitcast.20, bf16[96,16,512]{2,1,0:T(8,128)(2,1)} %bitcast.18), custom_call_target="tpu_custom_call" | custom-call | tf_op jit(solution)/shard_map/turn/pallas_call | solution.py:18
  2.4 0.0 copy-start
  2.4 0.0 copy-start.2
  2.4 0.3 collective-permute-start
  2.7 1.8 %moments.1 = (f32[128,1,128]{2,1,0:T(1,128)S(1)}, bf16[16,96,512]{2,1,0:T(8,128)(2,1)S(1)}, bf16[5,192,256]{2,1,0:T(8,128)(2,1)S(1)}, bf16[5,192,256]{2,1,0:T(8,128)(2,1)S(1)}) custom-call(bf16[8,192,256]{2,1,0:T(8,128)(2,1)S(1)} %get-tuple-element.35.lat_t, bf16[8,192,256]{2,1,0:T(8,128)(2,1)S(1)} %get-tuple-element.36.cache_t, ...), custom_call_target="tpu_custom_call" | custom-call | tf_op jit(solution)/shard_map/moments/pallas_call | solution.py:18
  4.5 1.5 %collective-permute-start.1 = (bf16[5,192,256]{2,1,0:T(8,128)(2,1)S(1)}, bf16[5,192,256]{2,1,0:T(8,128)(2,1)S(1)}, u32[]{:S(2)}, u32[]{:S(2)}) collective-permute-start(bf16[5,192,256]{2,1,0:T(8,128)(2,1)S(1)} %get-tuple-element.42), channel_id=1, source_target_pairs={{0,1},{1,2},{2,3},{3,4},{4,5},{5,6},{6,7},{7,8},{8,9},{9,10},{10,1... | collective-permute-start | bytes 1474568 | tf_op jit(solution)/shard_map/ppermute | solution.py:431
  6.0 1.3 %collective-permute-start.2 = (bf16[5,192,256]{2,1,0:T(8,128)(2,1)S(1)}, bf16[5,192,256]{2,1,0:T(8,128)(2,1)S(1)}, u32[]{:S(2)}, u32[]{:S(2)}) collective-permute-start(bf16[5,192,256]{2,1,0:T(8,128)(2,1)S(1)} %get-tuple-element.43), channel_id=1, source_target_pairs={{1,0},{2,1},{3,2},{4,3},{5,4},{6,5},{7,6},{8,7},{9,8},{10,9},{11,1... | collective-permute-start | bytes 1474568 | tf_op jit(solution)/shard_map/ppermute | solution.py:432
  7.3 0.0 copy-done.1
  7.3 0.0 copy-done
  7.4 0.0 copy-done.2
  7.4 1.0 %weights.1 = (bf16[3,192,1728]{2,1,0:T(8,128)(2,1)S(1)}, bf16[192,1152]{1,0:T(8,128)(2,1)S(1)}, bf16[3,192,1152]{2,1,0:T(8,128)(2,1)S(1)}) custom-call(bf16[3,3,3,192,192]{4,3,2,1,0:T(8,128)(2,1)S(1)} %copy-done, bf16[3,3,96,192]{3,2,1,0:T(8,128)(2,1)S(1)} %copy-done.2, bf16[3,3,3,96,96]{4,3,2,1,0:T(8,128)(2,1)S(1)} %copy-done.1), custom_call_target="tpu_custom_call" | custom-call | tf_op jit(solution)/shard_map/weights/pallas_call | solution.py:18
  8.4 24.3 %all_to_all.10.stats = f32[128,1,128]{2,1,0:T(1,128)S(1)} all-to-all(f32[128,1,128]{2,1,0:T(1,128)S(1)} %get-tuple-element.40), channel_id=1, replica_groups=mesh['tm'=2,'tile'=64] {'tm','tile'}, dimensions={0} | all-to-all | bytes 131072 | tf_op jit(solution)/shard_map/all_to_all | solution.py:402
  32.7 0.0 collective-permute-done.1.above
  32.7 0.0 collective-permute-done.2.below
  32.7 0.0 collective-permute-done.other
  32.8 1.3 %collective-permute-start.4 = (bf16[2,192,256]{2,1,0:T(8,128)(2,1)S(1)}, bf16[2,192,256]{2,1,0:T(8,128)(2,1)S(1)}, u32[]{:S(2)}, u32[]{:S(2)}) collective-permute-start(bf16[2,192,256]{2,1,0:T(8,128)(2,1)S(1)} %get-tuple-element.65), channel_id=1, source_target_pairs={{1,0},{2,1},{3,2},{4,3},{5,4},{6,5},{7,6},{8,7},{9,8},{10,9},{11,1... | collective-permute-start | bytes 589832 | tf_op jit(solution)/shard_map/ppermute | solution.py:444
  34.1 3.0 %collective-permute-start.3 = (bf16[2,192,256]{2,1,0:T(8,128)(2,1)S(1)}, bf16[2,192,256]{2,1,0:T(8,128)(2,1)S(1)}, u32[]{:S(2)}, u32[]{:S(2)}) collective-permute-start(bf16[2,192,256]{2,1,0:T(8,128)(2,1)S(1)} %get-tuple-element.66), channel_id=1, source_target_pairs={{0,1},{1,2},{2,3},{3,4},{4,5},{5,6},{6,7},{7,8},{8,9},{9,10},{10,1... | collective-permute-start | bytes 589832 | tf_op jit(solution)/shard_map/ppermute | solution.py:443
  37.1 0.0 collective-permute-done.4.below
  37.1 1.0 %collective-permute-done.3.above = bf16[2,192,256]{2,1,0:T(8,128)(2,1)S(1)} collective-permute-done((bf16[2,192,256]{2,1,0:T(8,128)(2,1)S(1)}, bf16[2,192,256]{2,1,0:T(8,128)(2,1)S(1)}, u32[]{:S(2)}, u32[]{:S(2)}) %collective-permute-start.3) | collective-permute-done | bytes 196640 | tf_op jit(solution)/shard_map/ppermute | solution.py:443
  38.1 0.0 copy-start.3
  38.1 0.0 copy-start.4
  38.1 2.6 %collective-permute-start.5 = (bf16[16,96,512]{2,1,0:T(8,128)(2,1)S(1)}, bf16[16,96,512]{2,1,0:T(8,128)(2,1)S(1)}, u32[]{:S(2)}, u32[]{:S(2)}) collective-permute-start(bf16[16,96,512]{2,1,0:T(8,128)(2,1)S(1)} %get-tuple-element.56.fine_t), channel_id=1, source_target_pairs={{64,0},{65,1},{66,2},{67,3},{68,4},{69,5},{70,6},{71,7},{72,8},{73... | collective-permute-start | bytes 4718600 | tf_op jit(solution)/shard_map/ppermute | solution.py:455
  40.8 2.1 %coarse_first.1.acc = f32[10,192,256]{2,1,0:T(8,128)S(1)} custom-call(bf16[8,192,256]{2,1,0:T(8,128)(2,1)S(1)} %get-tuple-element.36.cache_t, bf16[5,192,256]{2,1,0:T(8,128)(2,1)S(1)} %collective-permute-done.1.above, bf16[5,192,256]{2,1,0:T(8,128)(2,1)S(1)} %collective-permute-done.2.below, bf16[3,192,1728]{2,1,0:T(8,128)(2,1)S(1)} %get-tuple-element.39.weights), custom_call_target="tpu_custom_call" | custom-call | tf_op jit(solution)/shard_map/coarse_first/pallas_call | solution.py:18
  42.9 0.0 copy-done.3
  42.9 0.0 copy-done.4
  42.9 3.1 %coarse_third.1.acc = f32[10,192,256]{2,1,0:T(8,128)S(1)} custom-call(bf16[8,192,256]{2,1,0:T(8,128)(2,1)S(1)} %get-tuple-element.35.lat_t, bf16[5,192,256]{2,1,0:T(8,128)(2,1)S(1)} %collective-permute-done.1.above, bf16[5,192,256]{2,1,0:T(8,128)(2,1)S(1)} %collective-permute-done.2.below, f32[128,1,128]{2,1,0:T(1,128)S(1)} %all_to_all.10.stats, ...), custom_call_target="tpu_custom_call" | custom-call | tf_op jit(solution)/shard_map/coarse_third/pallas_call | solution.py:18
  46.0 3.9 %coarse_second.1 = (bf16[8,192,256]{2,1,0:T(8,128)(2,1)S(1)}, bf16[2,192,256]{2,1,0:T(8,128)(2,1)S(1)}) custom-call(bf16[8,192,256]{2,1,0:T(8,128)(2,1)S(1)} %collective-permute-done.other, bf16[2,192,256]{2,1,0:T(8,128)(2,1)S(1)} %collective-permute-done.3.above, bf16[2,192,256]{2,1,0:T(8,128)(2,1)S(1)} %collective-permute-done.4.below, ...), custom_call_target="tpu_custom_call" | custom-call | tf_op jit(solution)/shard_map/coarse_second/pallas_call | solution.py:18
  49.8 1.3 %collective-permute-start.6 = (bf16[8,192,256]{2,1,0:T(8,128)(2,1)S(1)}, bf16[8,192,256]{2,1,0:T(8,128)(2,1)S(1)}, u32[]{:S(2)}, u32[]{:S(2)}) collective-permute-start(bf16[8,192,256]{2,1,0:T(8,128)(2,1)S(1)} %get-tuple-element.49.coarse), channel_id=1, source_target_pairs={{0,64},{1,65},{2,66},{3,67},{4,68},{5,69},{6,70},{7,71},{8,72},{9,... | collective-permute-start | bytes 2359304 | tf_op jit(solution)/shard_map/ppermute | solution.py:462
  51.1 2.3 %fine_first.1.acc = f32[8,192,512]{2,1,0:T(8,128)S(1)} custom-call(bf16[16,96,512]{2,1,0:T(8,128)(2,1)S(1)} %get-tuple-element.56.fine_t, bf16[5,192,256]{2,1,0:T(8,128)(2,1)S(1)} %collective-permute-done.1.above, bf16[5,192,256]{2,1,0:T(8,128)(2,1)S(1)} %collective-permute-done.2.below, bf16[3,192,1152]{2,1,0:T(8,128)(2,1)S(1)} %get-tuple-element.54.weights), custom_call_target="tpu_custom_call" | custom-call | tf_op jit(solution)/shard_map/fine_first/pallas_call | solution.py:18
  53.5 4.4 %up.3 = (bf16[18,96,512]{2,1,0:T(8,128)(2,1)S(1)}, f32[128,1,128]{2,1,0:T(1,128)S(1)}, bf16[2,192,256]{2,1,0:T(8,128)(2,1)S(1)}) custom-call(bf16[8,192,256]{2,1,0:T(8,128)(2,1)S(1)} %get-tuple-element.49.coarse, bf16[2,192,256]{2,1,0:T(8,128)(2,1)S(1)} %get-tuple-element.50.rims, bf16[5,192,256]{2,1,0:T(8,128)(2,1)S(1)} %collective-permute-done.1.above, ...), custom_call_target="tpu_custom_call" | custom-call | tf_op jit(solution)/shard_map/up/pallas_call | solution.py:18
  57.9 0.0 copy-start.5
  57.9 0.0 copy-start.6
  57.9 24.8 %all_to_all.11.stats = f32[128,1,128]{2,1,0:T(1,128)S(1)} all-to-all(f32[128,1,128]{2,1,0:T(1,128)S(1)} %get-tuple-element.55), channel_id=1, replica_groups=mesh['tm'=2,'tile'=64] {'tm','tile'}, dimensions={0} | all-to-all | bytes 131072 | tf_op jit(solution)/shard_map/all_to_all | solution.py:402
  82.7 0.0 collective-permute-done.6.coarse
  82.7 0.0 collective-permute-done.5.fine_r
  82.7 2.6 %collective-permute-start.7 = (bf16[2,192,256]{2,1,0:T(8,128)(2,1)S(1)}, bf16[2,192,256]{2,1,0:T(8,128)(2,1)S(1)}, u32[]{:S(2)}, u32[]{:S(2)}) collective-permute-start(bf16[2,192,256]{2,1,0:T(8,128)(2,1)S(1)} %get-tuple-element.62), channel_id=1, source_target_pairs={{0,64},{64,0},{1,65},{65,1},{2,66},{66,2},{3,67},{67,3},{4,68},{68... | collective-permute-start | bytes 589832 | tf_op jit(solution)/shard_map/ppermute | solution.py:475
  85.3 2.7 %fine_begin.1 = (bf16[14,96,512]{2,1,0:T(8,128)(2,1)S(1)}, bf16[1,5184,512]{2,1,0:T(8,128)(2,1)S(1)}) custom-call(bf16[16,96,512]{2,1,0:T(8,128)(2,1)S(1)} %collective-permute-done.5.fine_r, bf16[8,192,256]{2,1,0:T(8,128)(2,1)S(1)} %collective-permute-done.6.coarse, bf16[192,1152]{1,0:T(8,128)(2,1)S(1)} %get-tuple-element.51.weights), custom_call_target="tpu_custom_call" | custom-call | tf_op jit(solution)/shard_map/fine_begin/pallas_call | solution.py:18
  88.0 0.0 copy-done.5
  88.0 0.0 copy-done.6
  88.0 3.4 %fine_third.1.acc = f32[8,192,512]{2,1,0:T(8,128)S(1)} custom-call(bf16[18,96,512]{2,1,0:T(8,128)(2,1)S(1)} %get-tuple-element.64.raised, f32[128,1,128]{2,1,0:T(1,128)S(1)} %all_to_all.11.stats, f32[1,96]{1,0:T(1,128)S(1)} %bitcast.13, f32[1,96]{1,0:T(1,128)S(1)} %bitcast.15, bf16[3,192,1152]{2,1,0:T(8,128)(2,1)S(1)} %get-tuple-element.54.weights, ...), custom_call_target="tpu_custom_call" | custom-call | tf_op jit(solution)/shard_map/fine_third/pallas_call | solution.py:18
  91.4 0.0 collective-permute-done.7.late
  91.4 0.0 copy-start.7
  91.4 3.0 %fine_end.1.stack = bf16[1,5184,512]{2,1,0:T(8,128)(2,1)S(1)} custom-call(bf16[1,5184,512]{2,1,0:T(8,128)(2,1)S(1)} %get-tuple-element.59.begun, bf16[8,192,256]{2,1,0:T(8,128)(2,1)S(1)} %collective-permute-done.6.coarse, bf16[2,192,256]{2,1,0:T(8,128)(2,1)S(1)} %collective-permute-done.7.late, ...), custom_call_target="tpu_custom_call", output_to_operand_aliasing={{}: (0, {})} | custom-call | tf_op jit(solution)/shard_map/fine_end/pallas_call | solution.py:18
  94.4 0.0 copy-done.7
  94.4 3.8 %fine_second.1 = bf16[96,16,512]{2,1,0:T(8,128)(2,1)} custom-call(bf16[1,5184,512]{2,1,0:T(8,128)(2,1)S(1)} %fine_end.1.stack, f32[1,96]{1,0:T(1,128)S(1)} %bitcast.17, bf16[3,192,1152]{2,1,0:T(8,128)(2,1)S(1)} %get-tuple-element.54.weights, f32[8,192,512]{2,1,0:T(8,128)S(1)} %fine_third.1.acc), custom_call_target="tpu_custom_call" | custom-call | tf_op jit(solution)/shard_map/fine_second/pallas_call | solution.py:18
  (1 shorter events, 0.0 us)
Async XLA Ops:
  0.0 7.3 %copy-start.1 = (bf16[3,3,3,96,96]{4,3,2,1,0:T(8,128)(2,1)S(1)}, bf16[3,3,3,96,96]{4,3,2,1,0:T(8,128)(2,1)}, u32[]{:S(2)}) copy-start(bf16[3,3,3,96,96]{4,3,2,1,0:T(8,128)(2,1)} %fine.1) | copy-start | bytes 1492996
  2.4 5.0 %copy-start = (bf16[3,3,3,192,192]{4,3,2,1,0:T(8,128)(2,1)S(1)}, bf16[3,3,3,192,192]{4,3,2,1,0:T(8,128)(2,1)}, u32[]{:S(2)}) copy-start(bf16[3,3,3,192,192]{4,3,2,1,0:T(8,128)(2,1)} %coarse.1) | copy-start | bytes 5971972
  2.4 5.0 %copy-start.2 = (bf16[3,3,96,192]{3,2,1,0:T(8,128)(2,1)S(1)}, bf16[3,3,96,192]{3,2,1,0:T(8,128)(2,1)}, u32[]{:S(2)}) copy-start(bf16[3,3,96,192]{3,2,1,0:T(8,128)(2,1)} %up.2) | copy-start | bytes 995332
  2.4 30.3 %collective-permute-start = (bf16[8,192,256]{2,1,0:T(8,128)(2,1)S(1)}, bf16[8,192,256]{2,1,0:T(8,128)(2,1)S(1)}, u32[]{:S(2)}, u32[]{:S(2)}) collective-permute-start(bf16[8,192,256]{2,1,0:T(8,128)(2,1)S(1)} %get-tuple-element.41), channel_id=1, source_target_pairs={{0,64},{64,0},{1,65},{65,1},{2,66},{66,2},{3,67},{67,3},{4,68},{68... | collective-permute-start | bytes 2359304 | tf_op jit(solution)/shard_map/ppermute | solution.py:425
  4.5 28.2 %collective-permute-start.1 = (bf16[5,192,256]{2,1,0:T(8,128)(2,1)S(1)}, bf16[5,192,256]{2,1,0:T(8,128)(2,1)S(1)}, u32[]{:S(2)}, u32[]{:S(2)}) collective-permute-start(bf16[5,192,256]{2,1,0:T(8,128)(2,1)S(1)} %get-tuple-element.42), channel_id=1, source_target_pairs={{0,1},{1,2},{2,3},{3,4},{4,5},{5,6},{6,7},{7,8},{8,9},{9,10},{10,1... | collective-permute-start | bytes 1474568 | tf_op jit(solution)/shard_map/ppermute | solution.py:431
  6.0 26.7 %collective-permute-start.2 = (bf16[5,192,256]{2,1,0:T(8,128)(2,1)S(1)}, bf16[5,192,256]{2,1,0:T(8,128)(2,1)S(1)}, u32[]{:S(2)}, u32[]{:S(2)}) collective-permute-start(bf16[5,192,256]{2,1,0:T(8,128)(2,1)S(1)} %get-tuple-element.43), channel_id=1, source_target_pairs={{1,0},{2,1},{3,2},{4,3},{5,4},{6,5},{7,6},{8,7},{9,8},{10,9},{11,1... | collective-permute-start | bytes 1474568 | tf_op jit(solution)/shard_map/ppermute | solution.py:432
  32.8 4.4 %collective-permute-start.4 = (bf16[2,192,256]{2,1,0:T(8,128)(2,1)S(1)}, bf16[2,192,256]{2,1,0:T(8,128)(2,1)S(1)}, u32[]{:S(2)}, u32[]{:S(2)}) collective-permute-start(bf16[2,192,256]{2,1,0:T(8,128)(2,1)S(1)} %get-tuple-element.65), channel_id=1, source_target_pairs={{1,0},{2,1},{3,2},{4,3},{5,4},{6,5},{7,6},{8,7},{9,8},{10,9},{11,1... | collective-permute-start | bytes 589832 | tf_op jit(solution)/shard_map/ppermute | solution.py:444
  34.1 4.1 %collective-permute-start.3 = (bf16[2,192,256]{2,1,0:T(8,128)(2,1)S(1)}, bf16[2,192,256]{2,1,0:T(8,128)(2,1)S(1)}, u32[]{:S(2)}, u32[]{:S(2)}) collective-permute-start(bf16[2,192,256]{2,1,0:T(8,128)(2,1)S(1)} %get-tuple-element.66), channel_id=1, source_target_pairs={{0,1},{1,2},{2,3},{3,4},{4,5},{5,6},{6,7},{7,8},{8,9},{9,10},{10,1... | collective-permute-start | bytes 589832 | tf_op jit(solution)/shard_map/ppermute | solution.py:443
  38.1 4.7 %copy-start.3 = (f32[192]{0:T(256)S(1)}, f32[192]{0:T(256)}, u32[]{:S(2)}) copy-start(f32[192]{0:T(256)} %param.14) | copy-start | bytes 2308
  38.1 4.7 %copy-start.4 = (f32[192]{0:T(256)S(1)}, f32[192]{0:T(256)}, u32[]{:S(2)}) copy-start(f32[192]{0:T(256)} %param.15) | copy-start | bytes 2308
  38.1 44.6 %collective-permute-start.5 = (bf16[16,96,512]{2,1,0:T(8,128)(2,1)S(1)}, bf16[16,96,512]{2,1,0:T(8,128)(2,1)S(1)}, u32[]{:S(2)}, u32[]{:S(2)}) collective-permute-start(bf16[16,96,512]{2,1,0:T(8,128)(2,1)S(1)} %get-tuple-element.56.fine_t), channel_id=1, source_target_pairs={{64,0},{65,1},{66,2},{67,3},{68,4},{69,5},{70,6},{71,7},{72,8},{73... | collective-permute-start | bytes 4718600 | tf_op jit(solution)/shard_map/ppermute | solution.py:455
  49.8 32.9 %collective-permute-start.6 = (bf16[8,192,256]{2,1,0:T(8,128)(2,1)S(1)}, bf16[8,192,256]{2,1,0:T(8,128)(2,1)S(1)}, u32[]{:S(2)}, u32[]{:S(2)}) collective-permute-start(bf16[8,192,256]{2,1,0:T(8,128)(2,1)S(1)} %get-tuple-element.49.coarse), channel_id=1, source_target_pairs={{0,64},{1,65},{2,66},{3,67},{4,68},{5,69},{6,70},{7,71},{8,72},{9,... | collective-permute-start | bytes 2359304 | tf_op jit(solution)/shard_map/ppermute | solution.py:462
  57.9 30.1 %copy-start.5 = (f32[96]{0:T(128)S(1)}, f32[96]{0:T(128)}, u32[]{:S(2)}) copy-start(f32[96]{0:T(128)} %param.18) | copy-start | bytes 1156
  57.9 30.1 %copy-start.6 = (f32[96]{0:T(128)S(1)}, f32[96]{0:T(128)}, u32[]{:S(2)}) copy-start(f32[96]{0:T(128)} %param.19) | copy-start | bytes 1156
  82.7 8.7 %collective-permute-start.7 = (bf16[2,192,256]{2,1,0:T(8,128)(2,1)S(1)}, bf16[2,192,256]{2,1,0:T(8,128)(2,1)S(1)}, u32[]{:S(2)}, u32[]{:S(2)}) collective-permute-start(bf16[2,192,256]{2,1,0:T(8,128)(2,1)S(1)} %get-tuple-element.62), channel_id=1, source_target_pairs={{0,64},{64,0},{1,65},{65,1},{2,66},{66,2},{3,67},{67,3},{4,68},{68... | collective-permute-start | bytes 589832 | tf_op jit(solution)/shard_map/ppermute | solution.py:475
  91.4 3.0 %copy-start.7 = (f32[96]{0:T(128)S(1)}, f32[96]{0:T(128)}, u32[]{:S(2)}) copy-start(f32[96]{0:T(128)} %param.21) | copy-start | bytes 1156

commit v5 on v4

--- a/solution.py
+++ b/solution.py
@@ -338,23 +338,18 @@
         out[m] = acc[m] + dot(weights[2], fine_window(stack, m, 3 * raised.shape[1]))
 
 
-def fine_begin(fine_r, coarse, weights, raised, stack, stack_up):
+def fine_begin(coarse, weights, raised, stack_up):
+    @pl.when(lax.axis_index("tm") != 0)
+    def _():
+        raise_rows(rows_of(coarse), weights, raised, stack_up)
+
+
+def fine_end(fine_r, coarse, late, raised, stats, gain, shift, weights, stack, ends, stack_up):
     frame = lax.axis_index("tm")
 
     @pl.when(frame == 0)
     def _():
         put_cache(stack, fine_r)
-
-    @pl.when(frame != 0)
-    def _():
-        raise_rows(rows_of(coarse), weights, raised, stack_up)
-
-
-def fine_end(begun, coarse, late, raised, stats, gain, shift, weights, stack, ends, stack_up):
-    frame = lax.axis_index("tm")
-
-    @pl.when(frame == 0)
-    def _():
         put_rims(stack, 2 * coarse.shape[0] + 1, late.at[0], late.at[1])
 
     @pl.when(frame != 0)
@@ -437,7 +432,7 @@
     )(weight_coarse, weight_up, weight_fine)
     stats = shared(after(pay, w_coarse))
     stats, other, above, below = lax.optimization_barrier((stats, other, above, below))
-    (acc,) = call(coarse_first, "coarse_first", [coarse_acc], [coarse_stack])(
+    (first,) = call(coarse_first, "coarse_first", [coarse_acc], [coarse_stack])(
         cache_t, above, below, w_coarse
     )
     other_above = lax.ppermute(other[rows - 2 :], "tile", forward)
@@ -450,9 +445,9 @@
         gain_coarse,
         shift_coarse,
         w_coarse,
-        after(acc, other_above, other_below),
-    )
-    fine_r = lax.ppermute(after(fine_t, other_above, other_below), "tm", earlier)
+        after(first, other_above, other_below),
+    )
+    fine_r = lax.ppermute(after(fine_t, first, other_above, other_below), "tm", earlier)
     coarse, coarse_rims = call(
         coarse_second,
         "coarse_second",
@@ -472,23 +467,16 @@
 
     stats = shared(after(pay, acc))
     stats, fine_r, coarse_r = lax.optimization_barrier((stats, fine_r, coarse_r))
-    late = lax.ppermute(after(late, stats), "tm", [(0, 1), (1, 0)])
-    raised_r, stack = call(
-        fine_begin,
-        "fine_begin",
-        [((fine_rows - 2, c2, fine_cols), bf16), stack_shape],
-        [up_stack],
-    )(fine_r, coarse_r, w_up)
+    (raised_r,) = call(
+        fine_begin, "fine_begin", [((fine_rows - 2, c2, fine_cols), bf16)], [up_stack]
+    )(coarse_r, w_up)
+    late = lax.ppermute(after(late, raised_r), "tm", [(0, 1), (1, 0)])
     (acc,) = call(fine_third, "fine_third", [fine_acc], [fine_scratch])(
         raised, stats, gain_fine, shift_fine, w_fine, acc
     )
     (stack,) = call(
-        fine_end,
-        "fine_end",
-        [stack_shape],
-        [pltpu.VMEM((4, c2, fine_cols), bf16), up_stack],
-        aliases={0: 0},
-    )(stack, coarse_r, late, raised_r, stats, gain_fine, shift_fine, w_up)
+        fine_end, "fine_end", [stack_shape], [pltpu.VMEM((4, c2, fine_cols), bf16), up_stack]
+    )(fine_r, coarse_r, late, raised_r, stats, gain_fine, shift_fine, w_up)
     (out,) = call(
         fine_second,
         "fine_second",

time: 98.6 us -> 101 us (1.024)
  waiting for transfers between devices: 1.05 us -> 4.71 us
  starting transfers between devices: 14 us -> 11.6 us
  blocking collectives: 49.1 us -> 50.3 us
    ppermute x2, waiting for transfers between devices: 0.01 us -> 4.69 us  [the longest x1 4.69 us: per_device(): late = lax.ppermute(after(late, raised_r), 'tm', [(0, 1), (1, 0)])]
    ppermute x2, starting transfers between devices: 5.19 us -> 2.8 us  [the longest x1 2.49 us: per_device(): lax.ppermute(after(fine_t, first, other_above, other_below), 'tm', earlier)]
    all_to_all x2, blocking collectives: 49.1 us -> 50.3 us  [shared(): return lax.all_to_all(stats, ('tm', 'tile'), 0, 0)]
    ppermute x1, waiting for transfers between devices: 1.03 us -> 0.01 us  [per_device(): other_above = lax.ppermute(other[rows - 2:], 'tile', forward)]
  transfers between devices with their start and end apart: 8 -> 8, of which waited for: 1 -> 1; matrix products, arithmetic and copies ran while one was open for 0% -> 0% of each run, Pallas kernels for 25% -> 22%
where the time goes in v5:
time: 101 us; the launch traced here: 100 us
  blocking collectives  50.3 us (50%)
  Pallas kernels  33.5 us (33%)
  starting transfers between devices  11.6 us (11%)
  waiting for transfers between devices  4.71 us (5%)
    all_to_all x2, blocking collectives, shared(): return lax.all_to_all(stats, ('tm', 'tile'), 0, 0)  50.3 us
    pallas_call x12, Pallas kernels, with_arrays(): pl.pallas_call(kernel, in_specs=[pl.BlockSpec(memory_space=pltpu.HBM)] *...  33.5 us
    ppermute x1, waiting for transfers between devices, per_device(): late = lax.ppermute(after(late, raised_r), 'tm', [(0, 1), (1, 0)])  4.69 us
    ppermute x1, starting transfers between devices, per_device(): other_above = lax.ppermute(other[rows - 2:], 'tile', forward)  3.04 us
    ppermute x1, starting transfers between devices, per_device(): lax.ppermute(after(fine_t, first, other_above, other_below), 'tm', earlier)  2.49 us
  transfers between devices with their start and end apart: 8, of which 1 were waited for; matrix products, arithmetic and copies ran while one was open for 0% of the time, Pallas kernels for 22%

profile of v5, /device:TPU:16, one launch (start us, length us, event | category | flops | bytes accessed | tf_op | source)
XLA Modules:
  0.0 100.5 jit_solution(1996134903508706654)
XLA Ops:
  0.0 0.0 copy-start.1
  0.0 2.4 %turn.1 = (bf16[8,192,256]{2,1,0:T(8,128)(2,1)S(1)}, bf16[8,192,256]{2,1,0:T(8,128)(2,1)S(1)}, bf16[8,192,256]{2,1,0:T(8,128)(2,1)S(1)}, bf16[96,16,512]{2,1,0:T(8,128)(2,1)S(1)}) custom-call(bf16[192,8,256]{2,1,0:T(8,128)(2,1)} %bitcast.19, bf16[192,8,256]{2,1,0:T(8,128)(2,1)} %bitcast.20, bf16[96,16,512]{2,1,0:T(8,128)(2,1)} %bitcast.18), custom_call_target="tpu_custom_call" | custom-call | tf_op jit(solution)/shard_map/turn/pallas_call | solution.py:18
  2.4 0.0 copy-start
  2.4 0.0 copy-start.2
  2.4 0.3 collective-permute-start
  2.7 1.8 %moments.1 = (f32[128,1,128]{2,1,0:T(1,128)S(1)}, bf16[16,96,512]{2,1,0:T(8,128)(2,1)S(1)}, bf16[5,192,256]{2,1,0:T(8,128)(2,1)S(1)}, bf16[5,192,256]{2,1,0:T(8,128)(2,1)S(1)}) custom-call(bf16[8,192,256]{2,1,0:T(8,128)(2,1)S(1)} %get-tuple-element.33.lat_t, bf16[8,192,256]{2,1,0:T(8,128)(2,1)S(1)} %get-tuple-element.34.cache_t, ...), custom_call_target="tpu_custom_call" | custom-call | tf_op jit(solution)/shard_map/moments/pallas_call | solution.py:18
  4.5 1.5 %collective-permute-start.1 = (bf16[5,192,256]{2,1,0:T(8,128)(2,1)S(1)}, bf16[5,192,256]{2,1,0:T(8,128)(2,1)S(1)}, u32[]{:S(2)}, u32[]{:S(2)}) collective-permute-start(bf16[5,192,256]{2,1,0:T(8,128)(2,1)S(1)} %get-tuple-element.40), channel_id=1, source_target_pairs={{0,1},{1,2},{2,3},{3,4},{4,5},{5,6},{6,7},{7,8},{8,9},{9,10},{10,1... | collective-permute-start | bytes 1474568 | tf_op jit(solution)/shard_map/ppermute | solution.py:426
  6.0 1.3 %collective-permute-start.2 = (bf16[5,192,256]{2,1,0:T(8,128)(2,1)S(1)}, bf16[5,192,256]{2,1,0:T(8,128)(2,1)S(1)}, u32[]{:S(2)}, u32[]{:S(2)}) collective-permute-start(bf16[5,192,256]{2,1,0:T(8,128)(2,1)S(1)} %get-tuple-element.41), channel_id=1, source_target_pairs={{1,0},{2,1},{3,2},{4,3},{5,4},{6,5},{7,6},{8,7},{9,8},{10,9},{11,1... | collective-permute-start | bytes 1474568 | tf_op jit(solution)/shard_map/ppermute | solution.py:427
  7.3 0.0 copy-done.1
  7.3 0.0 copy-done
  7.3 0.0 copy-done.2
  7.4 1.0 %weights.1 = (bf16[3,192,1728]{2,1,0:T(8,128)(2,1)S(1)}, bf16[192,1152]{1,0:T(8,128)(2,1)S(1)}, bf16[3,192,1152]{2,1,0:T(8,128)(2,1)S(1)}) custom-call(bf16[3,3,3,192,192]{4,3,2,1,0:T(8,128)(2,1)S(1)} %copy-done, bf16[3,3,96,192]{3,2,1,0:T(8,128)(2,1)S(1)} %copy-done.2, bf16[3,3,3,96,96]{4,3,2,1,0:T(8,128)(2,1)S(1)} %copy-done.1), custom_call_target="tpu_custom_call" | custom-call | tf_op jit(solution)/shard_map/weights/pallas_call | solution.py:18
  8.4 24.3 %all_to_all.10.stats = f32[128,1,128]{2,1,0:T(1,128)S(1)} all-to-all(f32[128,1,128]{2,1,0:T(1,128)S(1)} %get-tuple-element.38), channel_id=1, replica_groups=mesh['tm'=2,'tile'=64] {'tm','tile'}, dimensions={0} | all-to-all | bytes 131072 | tf_op jit(solution)/shard_map/all_to_all | solution.py:397
  32.7 0.0 collective-permute-done.1.above
  32.7 0.0 collective-permute-done.2.below
  32.7 0.0 collective-permute-done.other
  32.8 1.3 %collective-permute-start.4 = (bf16[2,192,256]{2,1,0:T(8,128)(2,1)S(1)}, bf16[2,192,256]{2,1,0:T(8,128)(2,1)S(1)}, u32[]{:S(2)}, u32[]{:S(2)}) collective-permute-start(bf16[2,192,256]{2,1,0:T(8,128)(2,1)S(1)} %get-tuple-element.61), channel_id=1, source_target_pairs={{1,0},{2,1},{3,2},{4,3},{5,4},{6,5},{7,6},{8,7},{9,8},{10,9},{11,1... | collective-permute-start | bytes 589832 | tf_op jit(solution)/shard_map/ppermute | solution.py:439
  34.1 0.0 copy-start.3
  34.1 0.0 copy-start.4
  34.1 3.0 %collective-permute-start.3 = (bf16[2,192,256]{2,1,0:T(8,128)(2,1)S(1)}, bf16[2,192,256]{2,1,0:T(8,128)(2,1)S(1)}, u32[]{:S(2)}, u32[]{:S(2)}) collective-permute-start(bf16[2,192,256]{2,1,0:T(8,128)(2,1)S(1)} %get-tuple-element.62), channel_id=1, source_target_pairs={{0,1},{1,2},{2,3},{3,4},{4,5},{5,6},{6,7},{7,8},{8,9},{9,10},{10,1... | collective-permute-start | bytes 589832 | tf_op jit(solution)/shard_map/ppermute | solution.py:438
  37.1 2.1 %coarse_first.1.acc = f32[10,192,256]{2,1,0:T(8,128)S(1)} custom-call(bf16[8,192,256]{2,1,0:T(8,128)(2,1)S(1)} %get-tuple-element.34.cache_t, bf16[5,192,256]{2,1,0:T(8,128)(2,1)S(1)} %collective-permute-done.1.above, bf16[5,192,256]{2,1,0:T(8,128)(2,1)S(1)} %collective-permute-done.2.below, bf16[3,192,1728]{2,1,0:T(8,128)(2,1)S(1)} %get-tuple-element.37.weights), custom_call_target="tpu_custom_call" | custom-call | tf_op jit(solution)/shard_map/coarse_first/pallas_call | solution.py:18
  39.2 0.0 collective-permute-done.4.below
  39.2 0.0 collective-permute-done.3.above
  39.3 2.5 %collective-permute-start.5 = (bf16[16,96,512]{2,1,0:T(8,128)(2,1)S(1)}, bf16[16,96,512]{2,1,0:T(8,128)(2,1)S(1)}, u32[]{:S(2)}, u32[]{:S(2)}) collective-permute-start(bf16[16,96,512]{2,1,0:T(8,128)(2,1)S(1)} %get-tuple-element.54.fine_t), channel_id=1, source_target_pairs={{64,0},{65,1},{66,2},{67,3},{68,4},{69,5},{70,6},{71,7},{72,8},{73... | collective-permute-start | bytes 4718600 | tf_op jit(solution)/shard_map/ppermute | solution.py:450
  41.8 0.0 copy-done.3
  41.8 0.0 copy-done.4
  41.8 3.1 %coarse_third.1.acc = f32[10,192,256]{2,1,0:T(8,128)S(1)} custom-call(bf16[8,192,256]{2,1,0:T(8,128)(2,1)S(1)} %get-tuple-element.33.lat_t, bf16[5,192,256]{2,1,0:T(8,128)(2,1)S(1)} %collective-permute-done.1.above, bf16[5,192,256]{2,1,0:T(8,128)(2,1)S(1)} %collective-permute-done.2.below, f32[128,1,128]{2,1,0:T(1,128)S(1)} %all_to_all.10.stats, ...), custom_call_target="tpu_custom_call" | custom-call | tf_op jit(solution)/shard_map/coarse_third/pallas_call | solution.py:18
  44.8 3.9 %coarse_second.1 = (bf16[8,192,256]{2,1,0:T(8,128)(2,1)S(1)}, bf16[2,192,256]{2,1,0:T(8,128)(2,1)S(1)}) custom-call(bf16[8,192,256]{2,1,0:T(8,128)(2,1)S(1)} %collective-permute-done.other, bf16[2,192,256]{2,1,0:T(8,128)(2,1)S(1)} %collective-permute-done.3.above, bf16[2,192,256]{2,1,0:T(8,128)(2,1)S(1)} %collective-permute-done.4.below, ...), custom_call_target="tpu_custom_call" | custom-call | tf_op jit(solution)/shard_map/coarse_second/pallas_call | solution.py:18
  48.7 1.3 %collective-permute-start.6 = (bf16[8,192,256]{2,1,0:T(8,128)(2,1)S(1)}, bf16[8,192,256]{2,1,0:T(8,128)(2,1)S(1)}, u32[]{:S(2)}, u32[]{:S(2)}) collective-permute-start(bf16[8,192,256]{2,1,0:T(8,128)(2,1)S(1)} %get-tuple-element.47.coarse), channel_id=1, source_target_pairs={{0,64},{1,65},{2,66},{3,67},{4,68},{5,69},{6,70},{7,71},{8,72},{9,... | collective-permute-start | bytes 2359304 | tf_op jit(solution)/shard_map/ppermute | solution.py:457
  50.0 2.3 %fine_first.1.acc = f32[8,192,512]{2,1,0:T(8,128)S(1)} custom-call(bf16[16,96,512]{2,1,0:T(8,128)(2,1)S(1)} %get-tuple-element.54.fine_t, bf16[5,192,256]{2,1,0:T(8,128)(2,1)S(1)} %collective-permute-done.1.above, bf16[5,192,256]{2,1,0:T(8,128)(2,1)S(1)} %collective-permute-done.2.below, bf16[3,192,1152]{2,1,0:T(8,128)(2,1)S(1)} %get-tuple-element.52.weights), custom_call_target="tpu_custom_call" | custom-call | tf_op jit(solution)/shard_map/fine_first/pallas_call | solution.py:18
  52.3 4.4 %up.3 = (bf16[18,96,512]{2,1,0:T(8,128)(2,1)S(1)}, f32[128,1,128]{2,1,0:T(1,128)S(1)}, bf16[2,192,256]{2,1,0:T(8,128)(2,1)S(1)}) custom-call(bf16[8,192,256]{2,1,0:T(8,128)(2,1)S(1)} %get-tuple-element.47.coarse, bf16[2,192,256]{2,1,0:T(8,128)(2,1)S(1)} %get-tuple-element.48.rims, bf16[5,192,256]{2,1,0:T(8,128)(2,1)S(1)} %collective-permute-done.1.above, ...), custom_call_target="tpu_custom_call" | custom-call | tf_op jit(solution)/shard_map/up/pallas_call | solution.py:18
  56.7 0.0 copy-start.5
  56.8 0.0 copy-start.6
  56.8 26.0 %all_to_all.11.stats = f32[128,1,128]{2,1,0:T(1,128)S(1)} all-to-all(f32[128,1,128]{2,1,0:T(1,128)S(1)} %get-tuple-element.53), channel_id=1, replica_groups=mesh['tm'=2,'tile'=64] {'tm','tile'}, dimensions={0} | all-to-all | bytes 131072 | tf_op jit(solution)/shard_map/all_to_all | solution.py:397
  82.8 0.0 collective-permute-done.6.coarse
  82.8 0.0 collective-permute-done.5.fine_r
  82.8 2.4 %fine_begin.1.raised = bf16[14,96,512]{2,1,0:T(8,128)(2,1)S(1)} custom-call(bf16[8,192,256]{2,1,0:T(8,128)(2,1)S(1)} %collective-permute-done.6.coarse, bf16[192,1152]{1,0:T(8,128)(2,1)S(1)} %get-tuple-element.49.weights), custom_call_target="tpu_custom_call" | custom-call | tf_op jit(solution)/shard_map/fine_begin/pallas_call | solution.py:18
  85.2 0.3 collective-permute-start.7
  85.5 0.0 copy-done.5
  85.5 0.0 copy-done.6
  85.6 3.4 %fine_third.1.acc = f32[8,192,512]{2,1,0:T(8,128)S(1)} custom-call(bf16[18,96,512]{2,1,0:T(8,128)(2,1)S(1)} %get-tuple-element.60.raised, f32[128,1,128]{2,1,0:T(1,128)S(1)} %all_to_all.11.stats, f32[1,96]{1,0:T(1,128)S(1)} %bitcast.13, f32[1,96]{1,0:T(1,128)S(1)} %bitcast.15, bf16[3,192,1152]{2,1,0:T(8,128)(2,1)S(1)} %get-tuple-element.52.weights, ...), custom_call_target="tpu_custom_call" | custom-call | tf_op jit(solution)/shard_map/fine_third/pallas_call | solution.py:18
  89.0 0.0 copy-start.7
  89.0 4.7 %collective-permute-done.7.late = bf16[2,192,256]{2,1,0:T(8,128)(2,1)S(1)} collective-permute-done((bf16[2,192,256]{2,1,0:T(8,128)(2,1)S(1)}, bf16[2,192,256]{2,1,0:T(8,128)(2,1)S(1)}, u32[]{:S(2)}, u32[]{:S(2)}) %collective-permute-start.7) | collective-permute-done | bytes 196640 | tf_op jit(solution)/shard_map/ppermute | solution.py:473
  93.7 3.0 %fine_end.1.stack = bf16[1,5184,512]{2,1,0:T(8,128)(2,1)S(1)} custom-call(bf16[16,96,512]{2,1,0:T(8,128)(2,1)S(1)} %collective-permute-done.5.fine_r, bf16[8,192,256]{2,1,0:T(8,128)(2,1)S(1)} %collective-permute-done.6.coarse, bf16[2,192,256]{2,1,0:T(8,128)(2,1)S(1)} %collective-permute-done.7.late, bf16[14,96,512]{2,1,0:T(8,128)(2,1)S(1)} %fine_begin.1.raised, ...), custom_call_target="tpu_custom_call" | custom-call | tf_op jit(solution)/shard_map/fine_end/pallas_call | solution.py:18
  96.7 0.0 copy-done.7
  96.7 3.8 %fine_second.1 = bf16[96,16,512]{2,1,0:T(8,128)(2,1)} custom-call(bf16[1,5184,512]{2,1,0:T(8,128)(2,1)S(1)} %fine_end.1.stack, f32[1,96]{1,0:T(1,128)S(1)} %bitcast.17, bf16[3,192,1152]{2,1,0:T(8,128)(2,1)S(1)} %get-tuple-element.52.weights, f32[8,192,512]{2,1,0:T(8,128)S(1)} %fine_third.1.acc), custom_call_target="tpu_custom_call" | custom-call | tf_op jit(solution)/shard_map/fine_second/pallas_call | solution.py:18
  (1 shorter events, 0.0 us)
Async XLA Ops:
  0.0 7.3 %copy-start.1 = (bf16[3,3,3,96,96]{4,3,2,1,0:T(8,128)(2,1)S(1)}, bf16[3,3,3,96,96]{4,3,2,1,0:T(8,128)(2,1)}, u32[]{:S(2)}) copy-start(bf16[3,3,3,96,96]{4,3,2,1,0:T(8,128)(2,1)} %fine.1) | copy-start | bytes 1492996
  2.4 5.0 %copy-start = (bf16[3,3,3,192,192]{4,3,2,1,0:T(8,128)(2,1)S(1)}, bf16[3,3,3,192,192]{4,3,2,1,0:T(8,128)(2,1)}, u32[]{:S(2)}) copy-start(bf16[3,3,3,192,192]{4,3,2,1,0:T(8,128)(2,1)} %coarse.1) | copy-start | bytes 5971972
  2.4 5.0 %copy-start.2 = (bf16[3,3,96,192]{3,2,1,0:T(8,128)(2,1)S(1)}, bf16[3,3,96,192]{3,2,1,0:T(8,128)(2,1)}, u32[]{:S(2)}) copy-start(bf16[3,3,96,192]{3,2,1,0:T(8,128)(2,1)} %up.2) | copy-start | bytes 995332
  2.4 30.3 %collective-permute-start = (bf16[8,192,256]{2,1,0:T(8,128)(2,1)S(1)}, bf16[8,192,256]{2,1,0:T(8,128)(2,1)S(1)}, u32[]{:S(2)}, u32[]{:S(2)}) collective-permute-start(bf16[8,192,256]{2,1,0:T(8,128)(2,1)S(1)} %get-tuple-element.39), channel_id=1, source_target_pairs={{0,64},{64,0},{1,65},{65,1},{2,66},{66,2},{3,67},{67,3},{4,68},{68... | collective-permute-start | bytes 2359304 | tf_op jit(solution)/shard_map/ppermute | solution.py:420
  4.5 28.2 %collective-permute-start.1 = (bf16[5,192,256]{2,1,0:T(8,128)(2,1)S(1)}, bf16[5,192,256]{2,1,0:T(8,128)(2,1)S(1)}, u32[]{:S(2)}, u32[]{:S(2)}) collective-permute-start(bf16[5,192,256]{2,1,0:T(8,128)(2,1)S(1)} %get-tuple-element.40), channel_id=1, source_target_pairs={{0,1},{1,2},{2,3},{3,4},{4,5},{5,6},{6,7},{7,8},{8,9},{9,10},{10,1... | collective-permute-start | bytes 1474568 | tf_op jit(solution)/shard_map/ppermute | solution.py:426
  6.0 26.7 %collective-permute-start.2 = (bf16[5,192,256]{2,1,0:T(8,128)(2,1)S(1)}, bf16[5,192,256]{2,1,0:T(8,128)(2,1)S(1)}, u32[]{:S(2)}, u32[]{:S(2)}) collective-permute-start(bf16[5,192,256]{2,1,0:T(8,128)(2,1)S(1)} %get-tuple-element.41), channel_id=1, source_target_pairs={{1,0},{2,1},{3,2},{4,3},{5,4},{6,5},{7,6},{8,7},{9,8},{10,9},{11,1... | collective-permute-start | bytes 1474568 | tf_op jit(solution)/shard_map/ppermute | solution.py:427
  32.8 6.5 %collective-permute-start.4 = (bf16[2,192,256]{2,1,0:T(8,128)(2,1)S(1)}, bf16[2,192,256]{2,1,0:T(8,128)(2,1)S(1)}, u32[]{:S(2)}, u32[]{:S(2)}) collective-permute-start(bf16[2,192,256]{2,1,0:T(8,128)(2,1)S(1)} %get-tuple-element.61), channel_id=1, source_target_pairs={{1,0},{2,1},{3,2},{4,3},{5,4},{6,5},{7,6},{8,7},{9,8},{10,9},{11,1... | collective-permute-start | bytes 589832 | tf_op jit(solution)/shard_map/ppermute | solution.py:439
  34.1 7.7 %copy-start.3 = (f32[192]{0:T(256)S(1)}, f32[192]{0:T(256)}, u32[]{:S(2)}) copy-start(f32[192]{0:T(256)} %param.14) | copy-start | bytes 2308
  34.1 7.7 %copy-start.4 = (f32[192]{0:T(256)S(1)}, f32[192]{0:T(256)}, u32[]{:S(2)}) copy-start(f32[192]{0:T(256)} %param.15) | copy-start | bytes 2308
  34.1 5.2 %collective-permute-start.3 = (bf16[2,192,256]{2,1,0:T(8,128)(2,1)S(1)}, bf16[2,192,256]{2,1,0:T(8,128)(2,1)S(1)}, u32[]{:S(2)}, u32[]{:S(2)}) collective-permute-start(bf16[2,192,256]{2,1,0:T(8,128)(2,1)S(1)} %get-tuple-element.62), channel_id=1, source_target_pairs={{0,1},{1,2},{2,3},{3,4},{4,5},{5,6},{6,7},{7,8},{8,9},{9,10},{10,1... | collective-permute-start | bytes 589832 | tf_op jit(solution)/shard_map/ppermute | solution.py:438
  39.3 43.5 %collective-permute-start.5 = (bf16[16,96,512]{2,1,0:T(8,128)(2,1)S(1)}, bf16[16,96,512]{2,1,0:T(8,128)(2,1)S(1)}, u32[]{:S(2)}, u32[]{:S(2)}) collective-permute-start(bf16[16,96,512]{2,1,0:T(8,128)(2,1)S(1)} %get-tuple-element.54.fine_t), channel_id=1, source_target_pairs={{64,0},{65,1},{66,2},{67,3},{68,4},{69,5},{70,6},{71,7},{72,8},{73... | collective-permute-start | bytes 4718600 | tf_op jit(solution)/shard_map/ppermute | solution.py:450
  48.7 34.1 %collective-permute-start.6 = (bf16[8,192,256]{2,1,0:T(8,128)(2,1)S(1)}, bf16[8,192,256]{2,1,0:T(8,128)(2,1)S(1)}, u32[]{:S(2)}, u32[]{:S(2)}) collective-permute-start(bf16[8,192,256]{2,1,0:T(8,128)(2,1)S(1)} %get-tuple-element.47.coarse), channel_id=1, source_target_pairs={{0,64},{1,65},{2,66},{3,67},{4,68},{5,69},{6,70},{7,71},{8,72},{9,... | collective-permute-start | bytes 2359304 | tf_op jit(solution)/shard_map/ppermute | solution.py:457
  56.7 28.8 %copy-start.5 = (f32[96]{0:T(128)S(1)}, f32[96]{0:T(128)}, u32[]{:S(2)}) copy-start(f32[96]{0:T(128)} %param.18) | copy-start | bytes 1156
  56.8 28.8 %copy-start.6 = (f32[96]{0:T(128)S(1)}, f32[96]{0:T(128)}, u32[]{:S(2)}) copy-start(f32[96]{0:T(128)} %param.19) | copy-start | bytes 1156
  85.2 8.4 %collective-permute-start.7 = (bf16[2,192,256]{2,1,0:T(8,128)(2,1)S(1)}, bf16[2,192,256]{2,1,0:T(8,128)(2,1)S(1)}, u32[]{:S(2)}, u32[]{:S(2)}) collective-permute-start(bf16[2,192,256]{2,1,0:T(8,128)(2,1)S(1)} %get-tuple-element.58), channel_id=1, source_target_pairs={{0,64},{64,0},{1,65},{65,1},{2,66},{66,2},{3,67},{67,3},{4,68},{68... | collective-permute-start | bytes 589832 | tf_op jit(solution)/shard_map/ppermute | solution.py:473
  89.0 7.7 %copy-start.7 = (f32[96]{0:T(128)S(1)}, f32[96]{0:T(128)}, u32[]{:S(2)}) copy-start(f32[96]{0:T(128)} %param.21) | copy-start | bytes 1156

commit v6 on v4

--- a/solution.py
+++ b/solution.py
@@ -437,7 +437,7 @@
     )(weight_coarse, weight_up, weight_fine)
     stats = shared(after(pay, w_coarse))
     stats, other, above, below = lax.optimization_barrier((stats, other, above, below))
-    (acc,) = call(coarse_first, "coarse_first", [coarse_acc], [coarse_stack])(
+    (acc_first,) = call(coarse_first, "coarse_first", [coarse_acc], [coarse_stack])(
         cache_t, above, below, w_coarse
     )
     other_above = lax.ppermute(other[rows - 2 :], "tile", forward)
@@ -450,9 +450,9 @@
         gain_coarse,
         shift_coarse,
         w_coarse,
-        after(acc, other_above, other_below),
+        after(acc_first, other_above, other_below),
     )
-    fine_r = lax.ppermute(after(fine_t, other_above, other_below), "tm", earlier)
+    fine_r = lax.ppermute(after(fine_t, acc_first, other_above, other_below), "tm", earlier)
     coarse, coarse_rims = call(
         coarse_second,
         "coarse_second",

time: 98.6 us -> 98.4 us (level)
  starting transfers between devices: 14 us -> 12.6 us
  blocking collectives: 49.1 us -> 50.3 us
    ppermute x1, starting transfers between devices: 2.57 us -> 1.33 us  [per_device(): late = lax.ppermute(after(late, stats), 'tm', [(0, 1), (1, 0)])]
    all_to_all x2, blocking collectives: 49.1 us -> 50.3 us  [shared(): return lax.all_to_all(stats, ('tm', 'tile'), 0, 0)]
    ppermute x1, waiting for transfers between devices: 1.03 us -> 0.01 us  [per_device(): other_above = lax.ppermute(other[rows - 2:], 'tile', forward)]
where the time goes in v6:
time: 98.4 us; the launch traced here: 97.8 us
  blocking collectives  50.3 us (51%)
  Pallas kernels  33.8 us (34%)
  starting transfers between devices  12.6 us (13%)
    all_to_all x2, blocking collectives, shared(): return lax.all_to_all(stats, ('tm', 'tile'), 0, 0)  50.3 us
    pallas_call x12, Pallas kernels, with_arrays(): pl.pallas_call(kernel, in_specs=[pl.BlockSpec(memory_space=pltpu.HBM)] *...  33.8 us
    ppermute x1, starting transfers between devices, per_device(): other_above = lax.ppermute(other[rows - 2:], 'tile', forward)  3.04 us
    ppermute x1, starting transfers between devices, per_device(): lax.ppermute(after(fine_t, acc_first, other_above, other_below), 'tm', ea...  2.49 us
  transfers between devices with their start and end apart: 8, of which 1 were waited for; matrix products, arithmetic and copies ran while one was open for 0% of the time, Pallas kernels for 25%

profile of v6, /device:TPU:16, one launch (start us, length us, event | category | flops | bytes accessed | tf_op | source)
XLA Modules:
  0.0 97.8 jit_solution(3039498967997155090)
XLA Ops:
  0.0 0.0 copy-start.1
  0.0 2.4 %turn.1 = (bf16[8,192,256]{2,1,0:T(8,128)(2,1)S(1)}, bf16[8,192,256]{2,1,0:T(8,128)(2,1)S(1)}, bf16[8,192,256]{2,1,0:T(8,128)(2,1)S(1)}, bf16[96,16,512]{2,1,0:T(8,128)(2,1)S(1)}) custom-call(bf16[192,8,256]{2,1,0:T(8,128)(2,1)} %bitcast.19, bf16[192,8,256]{2,1,0:T(8,128)(2,1)} %bitcast.20, bf16[96,16,512]{2,1,0:T(8,128)(2,1)} %bitcast.18), custom_call_target="tpu_custom_call" | custom-call | tf_op jit(solution)/shard_map/turn/pallas_call | solution.py:18
  2.4 0.0 copy-start
  2.4 0.0 copy-start.2
  2.4 0.3 collective-permute-start
  2.7 1.8 %moments.1 = (f32[128,1,128]{2,1,0:T(1,128)S(1)}, bf16[16,96,512]{2,1,0:T(8,128)(2,1)S(1)}, bf16[5,192,256]{2,1,0:T(8,128)(2,1)S(1)}, bf16[5,192,256]{2,1,0:T(8,128)(2,1)S(1)}) custom-call(bf16[8,192,256]{2,1,0:T(8,128)(2,1)S(1)} %get-tuple-element.35.lat_t, bf16[8,192,256]{2,1,0:T(8,128)(2,1)S(1)} %get-tuple-element.36.cache_t, ...), custom_call_target="tpu_custom_call" | custom-call | tf_op jit(solution)/shard_map/moments/pallas_call | solution.py:18
  4.5 1.5 %collective-permute-start.1 = (bf16[5,192,256]{2,1,0:T(8,128)(2,1)S(1)}, bf16[5,192,256]{2,1,0:T(8,128)(2,1)S(1)}, u32[]{:S(2)}, u32[]{:S(2)}) collective-permute-start(bf16[5,192,256]{2,1,0:T(8,128)(2,1)S(1)} %get-tuple-element.42), channel_id=1, source_target_pairs={{0,1},{1,2},{2,3},{3,4},{4,5},{5,6},{6,7},{7,8},{8,9},{9,10},{10,1... | collective-permute-start | bytes 1474568 | tf_op jit(solution)/shard_map/ppermute | solution.py:431
  6.0 1.3 %collective-permute-start.2 = (bf16[5,192,256]{2,1,0:T(8,128)(2,1)S(1)}, bf16[5,192,256]{2,1,0:T(8,128)(2,1)S(1)}, u32[]{:S(2)}, u32[]{:S(2)}) collective-permute-start(bf16[5,192,256]{2,1,0:T(8,128)(2,1)S(1)} %get-tuple-element.43), channel_id=1, source_target_pairs={{1,0},{2,1},{3,2},{4,3},{5,4},{6,5},{7,6},{8,7},{9,8},{10,9},{11,1... | collective-permute-start | bytes 1474568 | tf_op jit(solution)/shard_map/ppermute | solution.py:432
  7.3 0.0 copy-done.1
  7.3 0.0 copy-done
  7.4 0.0 copy-done.2
  7.4 1.0 %weights.1 = (bf16[3,192,1728]{2,1,0:T(8,128)(2,1)S(1)}, bf16[192,1152]{1,0:T(8,128)(2,1)S(1)}, bf16[3,192,1152]{2,1,0:T(8,128)(2,1)S(1)}) custom-call(bf16[3,3,3,192,192]{4,3,2,1,0:T(8,128)(2,1)S(1)} %copy-done, bf16[3,3,96,192]{3,2,1,0:T(8,128)(2,1)S(1)} %copy-done.2, bf16[3,3,3,96,96]{4,3,2,1,0:T(8,128)(2,1)S(1)} %copy-done.1), custom_call_target="tpu_custom_call" | custom-call | tf_op jit(solution)/shard_map/weights/pallas_call | solution.py:18
  8.4 24.3 %all_to_all.10.stats = f32[128,1,128]{2,1,0:T(1,128)S(1)} all-to-all(f32[128,1,128]{2,1,0:T(1,128)S(1)} %get-tuple-element.40), channel_id=1, replica_groups=mesh['tm'=2,'tile'=64] {'tm','tile'}, dimensions={0} | all-to-all | bytes 131072 | tf_op jit(solution)/shard_map/all_to_all | solution.py:402
  32.7 0.0 collective-permute-done.1.above
  32.7 0.0 collective-permute-done.2.below
  32.7 0.0 collective-permute-done.other
  32.8 1.3 %collective-permute-start.4 = (bf16[2,192,256]{2,1,0:T(8,128)(2,1)S(1)}, bf16[2,192,256]{2,1,0:T(8,128)(2,1)S(1)}, u32[]{:S(2)}, u32[]{:S(2)}) collective-permute-start(bf16[2,192,256]{2,1,0:T(8,128)(2,1)S(1)} %get-tuple-element.65), channel_id=1, source_target_pairs={{1,0},{2,1},{3,2},{4,3},{5,4},{6,5},{7,6},{8,7},{9,8},{10,9},{11,1... | collective-permute-start | bytes 589832 | tf_op jit(solution)/shard_map/ppermute | solution.py:444
  34.1 0.0 copy-start.3
  34.1 0.0 copy-start.4
  34.1 3.0 %collective-permute-start.3 = (bf16[2,192,256]{2,1,0:T(8,128)(2,1)S(1)}, bf16[2,192,256]{2,1,0:T(8,128)(2,1)S(1)}, u32[]{:S(2)}, u32[]{:S(2)}) collective-permute-start(bf16[2,192,256]{2,1,0:T(8,128)(2,1)S(1)} %get-tuple-element.66), channel_id=1, source_target_pairs={{0,1},{1,2},{2,3},{3,4},{4,5},{5,6},{6,7},{7,8},{8,9},{9,10},{10,1... | collective-permute-start | bytes 589832 | tf_op jit(solution)/shard_map/ppermute | solution.py:443
  37.1 2.1 %coarse_first.1.acc = f32[10,192,256]{2,1,0:T(8,128)S(1)} custom-call(bf16[8,192,256]{2,1,0:T(8,128)(2,1)S(1)} %get-tuple-element.36.cache_t, bf16[5,192,256]{2,1,0:T(8,128)(2,1)S(1)} %collective-permute-done.1.above, bf16[5,192,256]{2,1,0:T(8,128)(2,1)S(1)} %collective-permute-done.2.below, bf16[3,192,1728]{2,1,0:T(8,128)(2,1)S(1)} %get-tuple-element.39.weights), custom_call_target="tpu_custom_call" | custom-call | tf_op jit(solution)/shard_map/coarse_first/pallas_call | solution.py:18
  39.2 0.0 collective-permute-done.4.below
  39.2 0.0 collective-permute-done.3.above
  39.3 2.5 %collective-permute-start.5 = (bf16[16,96,512]{2,1,0:T(8,128)(2,1)S(1)}, bf16[16,96,512]{2,1,0:T(8,128)(2,1)S(1)}, u32[]{:S(2)}, u32[]{:S(2)}) collective-permute-start(bf16[16,96,512]{2,1,0:T(8,128)(2,1)S(1)} %get-tuple-element.56.fine_t), channel_id=1, source_target_pairs={{64,0},{65,1},{66,2},{67,3},{68,4},{69,5},{70,6},{71,7},{72,8},{73... | collective-permute-start | bytes 4718600 | tf_op jit(solution)/shard_map/ppermute | solution.py:455
  41.8 0.0 copy-done.3
  41.8 0.0 copy-done.4
  41.8 3.1 %coarse_third.1.acc = f32[10,192,256]{2,1,0:T(8,128)S(1)} custom-call(bf16[8,192,256]{2,1,0:T(8,128)(2,1)S(1)} %get-tuple-element.35.lat_t, bf16[5,192,256]{2,1,0:T(8,128)(2,1)S(1)} %collective-permute-done.1.above, bf16[5,192,256]{2,1,0:T(8,128)(2,1)S(1)} %collective-permute-done.2.below, f32[128,1,128]{2,1,0:T(1,128)S(1)} %all_to_all.10.stats, ...), custom_call_target="tpu_custom_call" | custom-call | tf_op jit(solution)/shard_map/coarse_third/pallas_call | solution.py:18
  44.8 3.9 %coarse_second.1 = (bf16[8,192,256]{2,1,0:T(8,128)(2,1)S(1)}, bf16[2,192,256]{2,1,0:T(8,128)(2,1)S(1)}) custom-call(bf16[8,192,256]{2,1,0:T(8,128)(2,1)S(1)} %collective-permute-done.other, bf16[2,192,256]{2,1,0:T(8,128)(2,1)S(1)} %collective-permute-done.3.above, bf16[2,192,256]{2,1,0:T(8,128)(2,1)S(1)} %collective-permute-done.4.below, ...), custom_call_target="tpu_custom_call" | custom-call | tf_op jit(solution)/shard_map/coarse_second/pallas_call | solution.py:18
  48.7 1.3 %collective-permute-start.6 = (bf16[8,192,256]{2,1,0:T(8,128)(2,1)S(1)}, bf16[8,192,256]{2,1,0:T(8,128)(2,1)S(1)}, u32[]{:S(2)}, u32[]{:S(2)}) collective-permute-start(bf16[8,192,256]{2,1,0:T(8,128)(2,1)S(1)} %get-tuple-element.49.coarse), channel_id=1, source_target_pairs={{0,64},{1,65},{2,66},{3,67},{4,68},{5,69},{6,70},{7,71},{8,72},{9,... | collective-permute-start | bytes 2359304 | tf_op jit(solution)/shard_map/ppermute | solution.py:462
  50.0 2.3 %fine_first.1.acc = f32[8,192,512]{2,1,0:T(8,128)S(1)} custom-call(bf16[16,96,512]{2,1,0:T(8,128)(2,1)S(1)} %get-tuple-element.56.fine_t, bf16[5,192,256]{2,1,0:T(8,128)(2,1)S(1)} %collective-permute-done.1.above, bf16[5,192,256]{2,1,0:T(8,128)(2,1)S(1)} %collective-permute-done.2.below, bf16[3,192,1152]{2,1,0:T(8,128)(2,1)S(1)} %get-tuple-element.54.weights), custom_call_target="tpu_custom_call" | custom-call | tf_op jit(solution)/shard_map/fine_first/pallas_call | solution.py:18
  52.3 4.4 %up.3 = (bf16[18,96,512]{2,1,0:T(8,128)(2,1)S(1)}, f32[128,1,128]{2,1,0:T(1,128)S(1)}, bf16[2,192,256]{2,1,0:T(8,128)(2,1)S(1)}) custom-call(bf16[8,192,256]{2,1,0:T(8,128)(2,1)S(1)} %get-tuple-element.49.coarse, bf16[2,192,256]{2,1,0:T(8,128)(2,1)S(1)} %get-tuple-element.50.rims, bf16[5,192,256]{2,1,0:T(8,128)(2,1)S(1)} %collective-permute-done.1.above, ...), custom_call_target="tpu_custom_call" | custom-call | tf_op jit(solution)/shard_map/up/pallas_call | solution.py:18
  56.8 0.0 copy-start.5
  56.8 0.0 copy-start.6
  56.8 26.0 %all_to_all.11.stats = f32[128,1,128]{2,1,0:T(1,128)S(1)} all-to-all(f32[128,1,128]{2,1,0:T(1,128)S(1)} %get-tuple-element.55), channel_id=1, replica_groups=mesh['tm'=2,'tile'=64] {'tm','tile'}, dimensions={0} | all-to-all | bytes 131072 | tf_op jit(solution)/shard_map/all_to_all | solution.py:402
  82.8 0.0 collective-permute-done.6.coarse
  82.8 0.0 collective-permute-done.5.fine_r
  82.8 1.3 %collective-permute-start.7 = (bf16[2,192,256]{2,1,0:T(8,128)(2,1)S(1)}, bf16[2,192,256]{2,1,0:T(8,128)(2,1)S(1)}, u32[]{:S(2)}, u32[]{:S(2)}) collective-permute-start(bf16[2,192,256]{2,1,0:T(8,128)(2,1)S(1)} %get-tuple-element.62), channel_id=1, source_target_pairs={{0,64},{64,0},{1,65},{65,1},{2,66},{66,2},{3,67},{67,3},{4,68},{68... | collective-permute-start | bytes 589832 | tf_op jit(solution)/shard_map/ppermute | solution.py:475
  84.1 2.7 %fine_begin.1 = (bf16[14,96,512]{2,1,0:T(8,128)(2,1)S(1)}, bf16[1,5184,512]{2,1,0:T(8,128)(2,1)S(1)}) custom-call(bf16[16,96,512]{2,1,0:T(8,128)(2,1)S(1)} %collective-permute-done.5.fine_r, bf16[8,192,256]{2,1,0:T(8,128)(2,1)S(1)} %collective-permute-done.6.coarse, bf16[192,1152]{1,0:T(8,128)(2,1)S(1)} %get-tuple-element.51.weights), custom_call_target="tpu_custom_call" | custom-call | tf_op jit(solution)/shard_map/fine_begin/pallas_call | solution.py:18
  86.8 0.0 copy-done.5
  86.8 0.0 copy-done.6
  86.8 3.4 %fine_third.1.acc = f32[8,192,512]{2,1,0:T(8,128)S(1)} custom-call(bf16[18,96,512]{2,1,0:T(8,128)(2,1)S(1)} %get-tuple-element.64.raised, f32[128,1,128]{2,1,0:T(1,128)S(1)} %all_to_all.11.stats, f32[1,96]{1,0:T(1,128)S(1)} %bitcast.13, f32[1,96]{1,0:T(1,128)S(1)} %bitcast.15, bf16[3,192,1152]{2,1,0:T(8,128)(2,1)S(1)} %get-tuple-element.54.weights, ...), custom_call_target="tpu_custom_call" | custom-call | tf_op jit(solution)/shard_map/fine_third/pallas_call | solution.py:18
  90.2 0.7 collective-permute-done.7.late
  90.9 0.0 copy-start.7
  90.9 3.0 %fine_end.1.stack = bf16[1,5184,512]{2,1,0:T(8,128)(2,1)S(1)} custom-call(bf16[1,5184,512]{2,1,0:T(8,128)(2,1)S(1)} %get-tuple-element.59.begun, bf16[8,192,256]{2,1,0:T(8,128)(2,1)S(1)} %collective-permute-done.6.coarse, bf16[2,192,256]{2,1,0:T(8,128)(2,1)S(1)} %collective-permute-done.7.late, ...), custom_call_target="tpu_custom_call", output_to_operand_aliasing={{}: (0, {})} | custom-call | tf_op jit(solution)/shard_map/fine_end/pallas_call | solution.py:18
  93.9 0.0 copy-done.7
  93.9 3.8 %fine_second.1 = bf16[96,16,512]{2,1,0:T(8,128)(2,1)} custom-call(bf16[1,5184,512]{2,1,0:T(8,128)(2,1)S(1)} %fine_end.1.stack, f32[1,96]{1,0:T(1,128)S(1)} %bitcast.17, bf16[3,192,1152]{2,1,0:T(8,128)(2,1)S(1)} %get-tuple-element.54.weights, f32[8,192,512]{2,1,0:T(8,128)S(1)} %fine_third.1.acc), custom_call_target="tpu_custom_call" | custom-call | tf_op jit(solution)/shard_map/fine_second/pallas_call | solution.py:18
  (1 shorter events, 0.0 us)
Async XLA Ops:
  0.0 7.3 %copy-start.1 = (bf16[3,3,3,96,96]{4,3,2,1,0:T(8,128)(2,1)S(1)}, bf16[3,3,3,96,96]{4,3,2,1,0:T(8,128)(2,1)}, u32[]{:S(2)}) copy-start(bf16[3,3,3,96,96]{4,3,2,1,0:T(8,128)(2,1)} %fine.1) | copy-start | bytes 1492996
  2.4 5.0 %copy-start = (bf16[3,3,3,192,192]{4,3,2,1,0:T(8,128)(2,1)S(1)}, bf16[3,3,3,192,192]{4,3,2,1,0:T(8,128)(2,1)}, u32[]{:S(2)}) copy-start(bf16[3,3,3,192,192]{4,3,2,1,0:T(8,128)(2,1)} %coarse.1) | copy-start | bytes 5971972
  2.4 5.0 %copy-start.2 = (bf16[3,3,96,192]{3,2,1,0:T(8,128)(2,1)S(1)}, bf16[3,3,96,192]{3,2,1,0:T(8,128)(2,1)}, u32[]{:S(2)}) copy-start(bf16[3,3,96,192]{3,2,1,0:T(8,128)(2,1)} %up.2) | copy-start | bytes 995332
  2.4 30.3 %collective-permute-start = (bf16[8,192,256]{2,1,0:T(8,128)(2,1)S(1)}, bf16[8,192,256]{2,1,0:T(8,128)(2,1)S(1)}, u32[]{:S(2)}, u32[]{:S(2)}) collective-permute-start(bf16[8,192,256]{2,1,0:T(8,128)(2,1)S(1)} %get-tuple-element.41), channel_id=1, source_target_pairs={{0,64},{64,0},{1,65},{65,1},{2,66},{66,2},{3,67},{67,3},{4,68},{68... | collective-permute-start | bytes 2359304 | tf_op jit(solution)/shard_map/ppermute | solution.py:425
  4.5 28.2 %collective-permute-start.1 = (bf16[5,192,256]{2,1,0:T(8,128)(2,1)S(1)}, bf16[5,192,256]{2,1,0:T(8,128)(2,1)S(1)}, u32[]{:S(2)}, u32[]{:S(2)}) collective-permute-start(bf16[5,192,256]{2,1,0:T(8,128)(2,1)S(1)} %get-tuple-element.42), channel_id=1, source_target_pairs={{0,1},{1,2},{2,3},{3,4},{4,5},{5,6},{6,7},{7,8},{8,9},{9,10},{10,1... | collective-permute-start | bytes 1474568 | tf_op jit(solution)/shard_map/ppermute | solution.py:431
  6.0 26.7 %collective-permute-start.2 = (bf16[5,192,256]{2,1,0:T(8,128)(2,1)S(1)}, bf16[5,192,256]{2,1,0:T(8,128)(2,1)S(1)}, u32[]{:S(2)}, u32[]{:S(2)}) collective-permute-start(bf16[5,192,256]{2,1,0:T(8,128)(2,1)S(1)} %get-tuple-element.43), channel_id=1, source_target_pairs={{1,0},{2,1},{3,2},{4,3},{5,4},{6,5},{7,6},{8,7},{9,8},{10,9},{11,1... | collective-permute-start | bytes 1474568 | tf_op jit(solution)/shard_map/ppermute | solution.py:432
  32.8 6.5 %collective-permute-start.4 = (bf16[2,192,256]{2,1,0:T(8,128)(2,1)S(1)}, bf16[2,192,256]{2,1,0:T(8,128)(2,1)S(1)}, u32[]{:S(2)}, u32[]{:S(2)}) collective-permute-start(bf16[2,192,256]{2,1,0:T(8,128)(2,1)S(1)} %get-tuple-element.65), channel_id=1, source_target_pairs={{1,0},{2,1},{3,2},{4,3},{5,4},{6,5},{7,6},{8,7},{9,8},{10,9},{11,1... | collective-permute-start | bytes 589832 | tf_op jit(solution)/shard_map/ppermute | solution.py:444
  34.1 7.7 %copy-start.3 = (f32[192]{0:T(256)S(1)}, f32[192]{0:T(256)}, u32[]{:S(2)}) copy-start(f32[192]{0:T(256)} %param.14) | copy-start | bytes 2308
  34.1 7.7 %copy-start.4 = (f32[192]{0:T(256)S(1)}, f32[192]{0:T(256)}, u32[]{:S(2)}) copy-start(f32[192]{0:T(256)} %param.15) | copy-start | bytes 2308
  34.1 5.2 %collective-permute-start.3 = (bf16[2,192,256]{2,1,0:T(8,128)(2,1)S(1)}, bf16[2,192,256]{2,1,0:T(8,128)(2,1)S(1)}, u32[]{:S(2)}, u32[]{:S(2)}) collective-permute-start(bf16[2,192,256]{2,1,0:T(8,128)(2,1)S(1)} %get-tuple-element.66), channel_id=1, source_target_pairs={{0,1},{1,2},{2,3},{3,4},{4,5},{5,6},{6,7},{7,8},{8,9},{9,10},{10,1... | collective-permute-start | bytes 589832 | tf_op jit(solution)/shard_map/ppermute | solution.py:443
  39.3 43.5 %collective-permute-start.5 = (bf16[16,96,512]{2,1,0:T(8,128)(2,1)S(1)}, bf16[16,96,512]{2,1,0:T(8,128)(2,1)S(1)}, u32[]{:S(2)}, u32[]{:S(2)}) collective-permute-start(bf16[16,96,512]{2,1,0:T(8,128)(2,1)S(1)} %get-tuple-element.56.fine_t), channel_id=1, source_target_pairs={{64,0},{65,1},{66,2},{67,3},{68,4},{69,5},{70,6},{71,7},{72,8},{73... | collective-permute-start | bytes 4718600 | tf_op jit(solution)/shard_map/ppermute | solution.py:455
  48.7 34.1 %collective-permute-start.6 = (bf16[8,192,256]{2,1,0:T(8,128)(2,1)S(1)}, bf16[8,192,256]{2,1,0:T(8,128)(2,1)S(1)}, u32[]{:S(2)}, u32[]{:S(2)}) collective-permute-start(bf16[8,192,256]{2,1,0:T(8,128)(2,1)S(1)} %get-tuple-element.49.coarse), channel_id=1, source_target_pairs={{0,64},{1,65},{2,66},{3,67},{4,68},{5,69},{6,70},{7,71},{8,72},{9,... | collective-permute-start | bytes 2359304 | tf_op jit(solution)/shard_map/ppermute | solution.py:462
  56.8 30.0 %copy-start.5 = (f32[96]{0:T(128)S(1)}, f32[96]{0:T(128)}, u32[]{:S(2)}) copy-start(f32[96]{0:T(128)} %param.18) | copy-start | bytes 1156
  56.8 30.0 %copy-start.6 = (f32[96]{0:T(128)S(1)}, f32[96]{0:T(128)}, u32[]{:S(2)}) copy-start(f32[96]{0:T(128)} %param.19) | copy-start | bytes 1156
  82.8 8.1 %collective-permute-start.7 = (bf16[2,192,256]{2,1,0:T(8,128)(2,1)S(1)}, bf16[2,192,256]{2,1,0:T(8,128)(2,1)S(1)}, u32[]{:S(2)}, u32[]{:S(2)}) collective-permute-start(bf16[2,192,256]{2,1,0:T(8,128)(2,1)S(1)} %get-tuple-element.62), channel_id=1, source_target_pairs={{0,64},{64,0},{1,65},{65,1},{2,66},{66,2},{3,67},{67,3},{4,68},{68... | collective-permute-start | bytes 589832 | tf_op jit(solution)/shard_map/ppermute | solution.py:475
  90.9 3.0 %copy-start.7 = (f32[96]{0:T(128)S(1)}, f32[96]{0:T(128)}, u32[]{:S(2)}) copy-start(f32[96]{0:T(128)} %param.21) | copy-start | bytes 1156
